TPU v7x, 512 devices: a whole 4x4x16 slice. The times are simulated.
512 devices in a mesh: dp: 8 (over z_hi, y), rows: 64 (over x, z_lo, core).
Axes of the slice: x: 4, y: 4, z: 16 (z_hi: 2, z_lo: 8; z = z_hi * 8 + z_lo), core: 2. Of those that a mesh axis runs over, the one named last changes fastest.
Arguments:
- fake: bfloat16 [8, 3, 256, 256], P('dp', None, 'rows'), may hold values from -1 to 1
- real: bfloat16 [8, 3, 256, 256], P('dp', None, 'rows'), may hold values from -1 to 1
- vgg_first: bfloat16 [64, 3, 3, 3], replicated, may hold values from -1.25 to 1.25
- vgg_second: bfloat16 [64, 64, 3, 3], replicated, may hold values from -0.25 to 0.25
- lpips_weights: float32 [64], replicated, may hold values from 0.5 to 2
- critic_conv: bfloat16 [64, 3, 4, 4], replicated, may hold values from -0.875 to 0.875
- critic_head: float32 [64], replicated, may hold values from -0.75 to 0.75
Outputs:
- grad_fake: float32 [8, 3, 256, 256], P('dp', None, 'rows')
- conv_grad: float32 [64, 3, 4, 4], replicated
- head_grad: float32 [64], replicated
All inputs are finite; a program needn't handle non-finite values.
Results may differ from a plain program's by a relative error of at most 0.0053.
Values may be sent and summed in bfloat16 or wider, within the bound.
No kernel may reach another device: no remote copies, remote signals or barrier semaphores. Data moves between devices by JAX's collectives and lax.ppermute only.
A program may use at most 64 MiB of HBM per device.

v0:
```python
import jax
import jax.numpy as jnp
from jax import lax
from jax.sharding import PartitionSpec as P

LPIPS_SHIFT = (-0.03, -0.088, -0.188)
LPIPS_SCALE = (0.458, 0.448, 0.45)
SOFTNESS = 0.04
LAYOUT = ("NCHW", "OIHW", "NCHW")


def padded(block, sides, width):
    for axis, dim in sides:
        count = lax.axis_size(axis)
        forward = [(i, i + 1) for i in range(count - 1)]
        backward = [(target, source) for source, target in forward]
        low = lax.ppermute(
            lax.slice_in_dim(block, block.shape[dim] - width, None, axis=dim), axis, forward
        )
        high = lax.ppermute(lax.slice_in_dim(block, 0, width, axis=dim), axis, backward)
        block = jnp.concatenate([low, block, high], axis=dim)
    return block


def smooth_relu(value):
    return 0.5 * (value + jnp.sqrt(value * value + SOFTNESS))


def smooth_grad(value):
    return 0.5 * (1.0 + value / jnp.sqrt(value * value + SOFTNESS))


def leaky_value(value):
    return 0.6 * value + 0.4 * jnp.sqrt(value * value + SOFTNESS)


def leaky_slope(value):
    return 0.6 + 0.4 * value / jnp.sqrt(value * value + SOFTNESS)


def padded_cols(tensor):
    return jnp.pad(tensor, ((0, 0), (0, 0), (0, 0), (1, 1)))


def valid_rows(first_row, number, height):
    global_rows = first_row + jnp.arange(number, dtype=jnp.int32)
    return ((global_rows >= 0) & (global_rows < height)).astype(jnp.float32)[:, None]


def scaled_image(tensor, mask):
    shift = jnp.array(LPIPS_SHIFT, jnp.float32)[:, None, None]
    scale = jnp.array(LPIPS_SCALE, jnp.float32)[:, None, None]
    return ((tensor.astype(jnp.float32) - shift) / scale * mask).astype(jnp.bfloat16)


def forward_taps(inputs, weight):
    return lax.conv_general_dilated(
        inputs,
        weight,
        (1, 1),
        ((0, 0), (0, 0)),
        dimension_numbers=LAYOUT,
        preferred_element_type=jnp.float32,
    )


def backward_taps(inputs, weight):
    flipped = jnp.transpose(jnp.flip(weight, (2, 3)), (1, 0, 2, 3))
    return lax.conv_general_dilated(
        inputs,
        flipped,
        (1, 1),
        ((0, 0), (0, 0)),
        dimension_numbers=LAYOUT,
        preferred_element_type=jnp.float32,
    )


def critic_forward(inputs, weight):
    return lax.conv_general_dilated(
        inputs,
        weight,
        (2, 2),
        ((0, 0), (0, 0)),
        dimension_numbers=LAYOUT,
        preferred_element_type=jnp.float32,
    )


def critic_backward(grads, weight):
    flipped = jnp.transpose(jnp.flip(weight, (2, 3)), (1, 0, 2, 3))
    return lax.conv_general_dilated(
        grads,
        flipped,
        (1, 1),
        ((3, 3), (3, 3)),
        lhs_dilation=(2, 2),
        dimension_numbers=LAYOUT,
        preferred_element_type=jnp.float32,
    )


def critic_weights(signal, inputs):
    outputs = signal.shape[2]
    half = signal.shape[3]
    rows_list = []
    for row_tap in range(4):
        cols_list = []
        for col_tap in range(4):
            window = inputs[
                :, :, row_tap : row_tap + 2 * outputs - 1 : 2, col_tap : col_tap + 2 * half - 1 : 2
            ].astype(jnp.float32)
            cols_list.append(
                jnp.einsum("borj,bcrj->oc", signal, window, precision=lax.Precision.HIGHEST)
            )
        rows_list.append(jnp.stack(cols_list, axis=-1))
    return jnp.stack(rows_list, axis=-2)


def lpips_gradient(features, weights):
    norm = jnp.sqrt(jnp.sum(features * features, axis=1) + 1e-06)
    unit = features / norm[:, None]
    direction = 2.0 * weights[:, None, None] * (unit[0] - unit[1])
    inner = jnp.sum(direction * unit[0], axis=0)
    return ((direction - unit[0] * inner[None]) / norm[0][None])[None]


def feature_rims(tensor):
    return padded(tensor, (("rows", 2),), 1)


def shards(fake, real, vgg_first, vgg_second, lpips_weights, critic_conv, critic_head):
    slab_rows = fake.shape[2]
    width = fake.shape[3]
    height = slab_rows * lax.axis_size("rows")
    first_row = lax.axis_index("rows") * slab_rows
    scale = jnp.array(LPIPS_SCALE, jnp.float32)[:, None, None]
    images = jnp.concatenate([fake, real], axis=0)
    rim_depth = 3
    extended = padded(images, (("rows", 2),), rim_depth)
    scaled = scaled_image(
        extended[:, :, 2 : slab_rows + 4], valid_rows(first_row - 1, slab_rows + 2, height)
    )
    pre_first = forward_taps(padded_cols(scaled), vgg_first)
    act_first = smooth_relu(pre_first).astype(jnp.bfloat16)
    pre_second = forward_taps(padded_cols(feature_rims(act_first)), vgg_second)
    grad_feature = lpips_gradient(smooth_relu(pre_second), lpips_weights)
    grad_second = (grad_feature * smooth_grad(pre_second[0:1])).astype(jnp.bfloat16)
    grad_act = backward_taps(padded_cols(feature_rims(grad_second)), vgg_second)
    grad_first = (grad_act * smooth_grad(pre_first[0:1])).astype(jnp.bfloat16)
    grad_scaled = backward_taps(padded_cols(feature_rims(grad_first)), vgg_first)
    critic_input = padded_cols(extended)
    pre_critic = critic_forward(critic_input, critic_conv)
    slope = leaky_slope(pre_critic)
    hidden = leaky_value(pre_critic)
    out_valid = valid_rows(first_row // 2 - 1, slab_rows // 2 + 2, height // 2)
    gen_signal = (-critic_head[None, :, None, None] * slope[0:1] * out_valid).astype(jnp.bfloat16)
    grad_gan = critic_backward(gen_signal, critic_conv)[:, :, 3 : slab_rows + 3, 1 : width + 1]
    grad_image = grad_scaled / scale + grad_gan
    total_patches = lax.axis_size("dp") * fake.shape[0] * (height // 2) * (width // 2)
    hidden_own = hidden[:, :, 1 : slab_rows // 2 + 1]
    slope_own = slope[:, :, 1 : slab_rows // 2 + 1]
    logits = jnp.einsum("o,borj->brj", critic_head, hidden_own, precision=lax.Precision.HIGHEST)
    logit_grad = (
        jnp.stack([jnp.where(logits[0] > -1.0, 1.0, 0.0), jnp.where(logits[1] < 1.0, -1.0, 0.0)])
        / total_patches
    )
    head_part = jnp.einsum("brj,borj->o", logit_grad, hidden_own, precision=lax.Precision.HIGHEST)
    critic_signal = critic_head[None, :, None, None] * logit_grad[:, None] * slope_own
    conv_part = critic_weights(critic_signal, critic_input[:, :, 2 : slab_rows + 4])
    conv_grad, head_grad = lax.psum((conv_part, head_part), ("dp", "rows"))
    return (grad_image, conv_grad, head_grad)


def solution(mesh):
    return jax.shard_map(
        shards,
        mesh=mesh,
        in_specs=(
            P("dp", None, "rows", None),
            P("dp", None, "rows", None),
            P(),
            P(),
            P(),
            P(),
            P(),
        ),
        out_specs=(P("dp", None, "rows", None), P(), P()),
        check_vma=False,
    )
```

profile of v0, /device:TPU:1, one launch (start us, length us, event | category | flops | bytes accessed | tf_op | source)
XLA Modules:
  0.0 217.2 jit_solution(1451398319895819803)
XLA Ops:
  2.1 4.9 %collective-permute-start = (bf16[2,3,3,256]{3,1,2,0:T(4,128)(2,1)S(1)}, bf16[2,3,3,256]{3,1,2,0:T(4,128)(2,1)S(1)}, u32[]{:S(2)}, u32[]{:S(2)}) collective-permute-start(bf16[2,3,3,256]{3,1,2,0:T(4,128)(2,1)S(1)} %get-tuple-element.27), channel_id=1, source_target_pairs={{0,1},{1,2},{2,3},{3,4},{4,5},{5,6},{6,7},{7,8},{8,9},{9,10},{10,1... | collective-permute-start | bytes 27656 | tf_op jit(solution)/shard_map/ppermute | solution.py:17
  7.1 5.1 %collective-permute-start.1 = (bf16[2,3,3,256]{3,1,2,0:T(4,128)(2,1)S(1)}, bf16[2,3,3,256]{3,1,2,0:T(4,128)(2,1)S(1)}, u32[]{:S(2)}, u32[]{:S(2)}) collective-permute-start(bf16[2,3,3,256]{3,1,2,0:T(4,128)(2,1)S(1)} %get-tuple-element.28), channel_id=1, source_target_pairs={{1,0},{2,1},{3,2},{4,3},{5,4},{6,5},{7,6},{8,7},{9,8},{10,9},{11,1... | collective-permute-start | bytes 27656 | tf_op jit(solution)/shard_map/ppermute | solution.py:20
  13.7 1.0 slice.149
  14.7 1.0 slice.148
  15.7 1.0 slice.147
  16.7 1.0 slice.146
  17.6 0.9 slice.145
  18.6 0.9 slice.144
  21.4 0.9 slice.141
  29.8 1.8 add_sqrt_fusion
  33.0 1.0 multiply_convert_fusion
  41.6 1.9 collective-permute-start.2
  43.7 2.6 %collective-permute-start.3 = (bf16[2,64,1,256]{1,3,0,2:T(8,128)(2,1)S(1)}, bf16[2,64,1,256]{1,3,0,2:T(8,128)(2,1)S(1)}, u32[]{:S(2)}, u32[]{:S(2)}) collective-permute-start(bf16[2,64,1,256]{1,3,0,2:T(8,128)(2,1)S(1)} %slice_bitcast_fusion.3), channel_id=1, source_target_pairs={{1,0},{2,1},{3,2},{4,3},{5,4},{6,5},{7,6},{8,7},{9,8},{10,9},{11,1... | collective-permute-start | bytes 196616 | tf_op jit(solution)/shard_map/ppermute | solution.py:20
  46.3 2.0 convolution_select_fusion.4
  48.4 1.6 collective-permute-done.3
  52.5 3.0 %multiply_reduce_fusion = (f32[4,16,33]{1,2,0:T(8,128)S(1)}, f32[4,16,33,64]{3,1,2,0:T(8,128)S(1)}, f32[4,16,33,64]{3,1,2,0:T(8,128)}) fusion(bf16[64,64,3,3]{1,0,3,2:T(8,128)(2,1)S(1)} %copy-done, bf16[64,6,2,8,35]{0,2,4,3,1:T(2,128)(2,1)S(1)} %fusion, pred[16,33]{0,1:T(8,128)(4,1)S(1)} %copy-done.11), kind=kOutput, calls=%fused_computation.23 | convolution fusion | flops 156657600 | bytes 1594128 | tf_op jit(solution)/shard_map/conv_general_dilated | solution.py:57
  56.6 1.7 copy.157
  59.1 1.9 collective-permute-start.4
  61.0 2.4 %collective-permute-start.5 = (bf16[1,64,1,256]{3,1,2,0:T(8,128)(2,1)S(1)}, bf16[1,64,1,256]{3,1,2,0:T(8,128)(2,1)S(1)}, u32[]{:S(2)}, u32[]{:S(2)}) collective-permute-start(bf16[1,64,1,256]{3,1,2,0:T(8,128)(2,1)S(1)} %get-tuple-element.26), channel_id=1, source_target_pairs={{1,0},{2,1},{3,2},{4,3},{5,4},{6,5},{7,6},{8,7},{9,8},{10,9},{11,1... | collective-permute-start | bytes 98312 | tf_op jit(solution)/shard_map/ppermute | solution.py:20
  64.3 1.9 collective-permute-done.5
  68.8 1.9 collective-permute-start.6
  70.7 2.4 %collective-permute-start.7 = (bf16[1,64,1,256]{3,1,2,0:T(8,128)(2,1)S(1)}, bf16[1,64,1,256]{3,1,2,0:T(8,128)(2,1)S(1)}, u32[]{:S(2)}, u32[]{:S(2)}) collective-permute-start(bf16[1,64,1,256]{3,1,2,0:T(8,128)(2,1)S(1)} %get-tuple-element.24), channel_id=1, source_target_pairs={{1,0},{2,1},{3,2},{4,3},{5,4},{6,5},{7,6},{8,7},{9,8},{10,9},{11,1... | collective-permute-start | bytes 98312 | tf_op jit(solution)/shard_map/ppermute | solution.py:20
  73.2 134.6 %all-reduce.1 = (f32[64,3,4,4]{0,1,3,2:T(4,128)S(1)}, f32[64]{0:T(128)}) all-reduce(f32[64,3,4,4]{0,1,3,2:T(4,128)S(1)} %pad_maximum_fusion.1, f32[64]{0:T(128)S(1)} %convolution_bitcast_fusion.16), channel_id=1, replica_groups=mesh['dp'=8,'rows'=64] {'dp','rows'}, use_global_device_ids=true, to_apply=%region_2.3 | all-reduce | flops 3136 | bytes 25088 | tf_op jit(solution)/shard_map/psum | solution.py:171
  210.2 6.0 %fusion.10 = f32[4,8,33,3]{1,3,2,0:T(4,128)S(1)} fusion(bf16[64,6,1,7,2]{0,3,4,1,2:T(8,128)(2,1)S(1)} %slice.198, bf16[64,6,1,8,33]{0,3,4,1,2:T(8,128)(2,1)S(1)} %copy.168, bf16[64,3,3,3]{0,3,2,1:T(4,128)(2,1)S(1)} %copy-done.9), kind=kOutput, calls=%fused_computation.41 | convolution fusion | flops 4294656 | bytes 229632 | tf_op jit(solution)/shard_map/conv_general_dilated | solution.py:69
  (163 shorter events, 32.1 us)
Async XLA Ops:
  0.6 51.9 %copy-start = (bf16[64,64,3,3]{1,0,3,2:T(8,128)(2,1)S(1)}, bf16[64,64,3,3]{1,0,3,2:T(8,128)(2,1)}, u32[]{:S(2)}) copy-start(bf16[64,64,3,3]{1,0,3,2:T(8,128)(2,1)} %param.13) | copy-start | bytes 221188
  0.6 29.1 %copy-start.13 = (pred[16,17]{0,1:T(8,128)(4,1)S(1)}, pred[16,17]{0,1:T(8,128)(4,1)}, u32[]{:S(2)}) copy-start(pred[16,17]{0,1:T(8,128)(4,1)} %constant.101) | copy-start | bytes 820
  0.7 29.1 %copy-start.8 = (bf16[64,3,4,4]{0,3,2,1:T(4,128)(2,1)S(1)}, bf16[64,3,4,4]{0,3,2,1:T(4,128)(2,1)}, u32[]{:S(2)}) copy-start(bf16[64,3,4,4]{0,3,2,1:T(4,128)(2,1)} %param.15) | copy-start | bytes 18436
  2.1 11.4 %collective-permute-start = (bf16[2,3,3,256]{3,1,2,0:T(4,128)(2,1)S(1)}, bf16[2,3,3,256]{3,1,2,0:T(4,128)(2,1)S(1)}, u32[]{:S(2)}, u32[]{:S(2)}) collective-permute-start(bf16[2,3,3,256]{3,1,2,0:T(4,128)(2,1)S(1)} %get-tuple-element.27), channel_id=1, source_target_pairs={{0,1},{1,2},{2,3},{3,4},{4,5},{5,6},{6,7},{7,8},{8,9},{9,10},{10,1... | collective-permute-start | bytes 27656 | tf_op jit(solution)/shard_map/ppermute | solution.py:17
  7.1 6.5 %collective-permute-start.1 = (bf16[2,3,3,256]{3,1,2,0:T(4,128)(2,1)S(1)}, bf16[2,3,3,256]{3,1,2,0:T(4,128)(2,1)S(1)}, u32[]{:S(2)}, u32[]{:S(2)}) collective-permute-start(bf16[2,3,3,256]{3,1,2,0:T(4,128)(2,1)S(1)} %get-tuple-element.28), channel_id=1, source_target_pairs={{1,0},{2,1},{3,2},{4,3},{5,4},{6,5},{7,6},{8,7},{9,8},{10,9},{11,1... | collective-permute-start | bytes 27656 | tf_op jit(solution)/shard_map/ppermute | solution.py:20
  31.6 0.7 copy-start.5
  31.6 0.7 copy-start.7
  31.6 1.4 copy-start.9
  31.6 1.4 copy-start.11
  34.0 1.1 copy-start.3
  34.0 1.2 copy-start.4
  35.2 0.7 copy-start.2
  41.2 5.1 %copy-start.12 = (pred[8,34]{0,1:T(8,128)(4,1)S(1)}, pred[8,34]{0,1:T(8,128)(4,1)}, u32[]{:S(2)}) copy-start(pred[8,34]{0,1:T(8,128)(4,1)} %constant.100) | copy-start | bytes 820
  41.6 6.6 %collective-permute-start.2 = (bf16[2,64,1,256]{1,3,0,2:T(8,128)(2,1)S(1)}, bf16[2,64,1,256]{1,3,0,2:T(8,128)(2,1)S(1)}, u32[]{:S(2)}, u32[]{:S(2)}) collective-permute-start(bf16[2,64,1,256]{1,3,0,2:T(8,128)(2,1)S(1)} %slice_bitcast_fusion.4), channel_id=1, source_target_pairs={{0,1},{1,2},{2,3},{3,4},{4,5},{5,6},{6,7},{7,8},{8,9},{9,10},{10,1... | collective-permute-start | bytes 196616 | tf_op jit(solution)/shard_map/ppermute | solution.py:17
  43.7 6.3 %collective-permute-start.3 = (bf16[2,64,1,256]{1,3,0,2:T(8,128)(2,1)S(1)}, bf16[2,64,1,256]{1,3,0,2:T(8,128)(2,1)S(1)}, u32[]{:S(2)}, u32[]{:S(2)}) collective-permute-start(bf16[2,64,1,256]{1,3,0,2:T(8,128)(2,1)S(1)} %slice_bitcast_fusion.3), channel_id=1, source_target_pairs={{1,0},{2,1},{3,2},{4,3},{5,4},{6,5},{7,6},{8,7},{9,8},{10,9},{11,1... | collective-permute-start | bytes 196616 | tf_op jit(solution)/shard_map/ppermute | solution.py:20
  59.1 5.2 %collective-permute-start.4 = (bf16[1,64,1,256]{3,1,2,0:T(8,128)(2,1)S(1)}, bf16[1,64,1,256]{3,1,2,0:T(8,128)(2,1)S(1)}, u32[]{:S(2)}, u32[]{:S(2)}) collective-permute-start(bf16[1,64,1,256]{3,1,2,0:T(8,128)(2,1)S(1)} %get-tuple-element.25), channel_id=1, source_target_pairs={{0,1},{1,2},{2,3},{3,4},{4,5},{5,6},{6,7},{7,8},{8,9},{9,10},{10,1... | collective-permute-start | bytes 98312 | tf_op jit(solution)/shard_map/ppermute | solution.py:17
  61.0 5.2 %collective-permute-start.5 = (bf16[1,64,1,256]{3,1,2,0:T(8,128)(2,1)S(1)}, bf16[1,64,1,256]{3,1,2,0:T(8,128)(2,1)S(1)}, u32[]{:S(2)}, u32[]{:S(2)}) collective-permute-start(bf16[1,64,1,256]{3,1,2,0:T(8,128)(2,1)S(1)} %get-tuple-element.26), channel_id=1, source_target_pairs={{1,0},{2,1},{3,2},{4,3},{5,4},{6,5},{7,6},{8,7},{9,8},{10,9},{11,1... | collective-permute-start | bytes 98312 | tf_op jit(solution)/shard_map/ppermute | solution.py:20
  66.4 1.3 copy-start.10
  68.5 139.9 %copy-start.1 = (f32[4,8,34,3]{1,3,2,0:T(4,128)S(1)}, f32[4,8,34,3]{1,3,2,0:T(4,128)}, u32[]{:S(2)}) copy-start(f32[4,8,34,3]{1,3,2,0:T(4,128)} %convolution_select_fusion.4) | copy-start | bytes 39172
  68.8 139.9 %collective-permute-start.6 = (bf16[1,64,1,256]{3,1,2,0:T(8,128)(2,1)S(1)}, bf16[1,64,1,256]{3,1,2,0:T(8,128)(2,1)S(1)}, u32[]{:S(2)}, u32[]{:S(2)}) collective-permute-start(bf16[1,64,1,256]{3,1,2,0:T(8,128)(2,1)S(1)} %get-tuple-element.23), channel_id=1, source_target_pairs={{0,1},{1,2},{2,3},{3,4},{4,5},{5,6},{6,7},{7,8},{8,9},{9,10},{10,1... | collective-permute-start | bytes 98312 | tf_op jit(solution)/shard_map/ppermute | solution.py:17
  70.7 137.9 %collective-permute-start.7 = (bf16[1,64,1,256]{3,1,2,0:T(8,128)(2,1)S(1)}, bf16[1,64,1,256]{3,1,2,0:T(8,128)(2,1)S(1)}, u32[]{:S(2)}, u32[]{:S(2)}) collective-permute-start(bf16[1,64,1,256]{3,1,2,0:T(8,128)(2,1)S(1)} %get-tuple-element.24), channel_id=1, source_target_pairs={{1,0},{2,1},{3,2},{4,3},{5,4},{6,5},{7,6},{8,7},{9,8},{10,9},{11,1... | collective-permute-start | bytes 98312 | tf_op jit(solution)/shard_map/ppermute | solution.py:20
  210.2 6.2 %copy-start.6 = (pred[8,33]{1,0:T(8,128)(4,1)S(1)}, pred[8,33]{1,0:T(8,128)(4,1)}, u32[]{:S(2)}) copy-start(pred[8,33]{1,0:T(8,128)(4,1)} %constant.95) | copy-start | bytes 796
where the time goes:
time: 218 us; the launch traced here: 217 us
  blocking collectives  135 us (62%)
  local copies, waits for them, and re-layouts  31.3 us (14%)
  starting transfers between devices  23.2 us (11%)
  matrix products  18.7 us (9%)
  other arithmetic  4.08 us (2%)
  waiting for transfers between devices  3.57 us (2%)
    psum x1, blocking collectives, shards(): conv_grad, head_grad = lax.psum((conv_part, head_part), ('dp', 'rows'))  135 us
    slice x16, local copies, waits for them, and re-layouts, critic_weights(): inputs[:, :, row_tap:row_tap + 2 * outputs - 1:2, col_tap:col_tap + 2 * h...  15.1 us
    ppermute x4, starting transfers between devices, padded(): lax.ppermute(lax.slice_in_dim(block, 0, width, axis=dim), axis, backward)  12.5 us
    ppermute x4, starting transfers between devices, padded(): lax.ppermute(lax.slice_in_dim(block, block.shape[dim] - width, None, axis...  10.7 us
    conv_general_dilated x2, matrix products, backward_taps(): lax.conv_general_dilated(inputs, flipped, (1, 1), ((0, 0), (0, 0)), dimen...  6.57 us
    unnamed x40, local copies, waits for them, and re-layouts  5.12 us
  transfers between devices with their start and end apart: 8, of which 2 were waited for; matrix products, arithmetic and copies ran while one was open for 2% of the time, Pallas kernels for 0%

commit v1 on v0

v1 whole, which is shorter than its diff:
```python
import functools

import jax
import jax.numpy as jnp
from jax import lax
from jax.experimental import pallas as pl
from jax.experimental.pallas import tpu as pltpu
from jax.sharding import Mesh, PartitionSpec as P

LPIPS_SHIFT = (-0.03, -0.088, -0.188)
LPIPS_SCALE = (0.458, 0.448, 0.45)
SOFTNESS = 0.04
ROWS = ("x", "zl", "c")
DP = ("zh", "y")
PLANE = ("y", "x", "c")
COLUMN = ("zh", "zl")
F32 = jnp.float32
BF16 = jnp.bfloat16
VMEM = pl.BlockSpec(memory_space=pltpu.VMEM)
SMEM = pl.BlockSpec(memory_space=pltpu.SMEM)
TN = (((0,), (0,)), ((), ()))
NT = (((1,), (1,)), ((), ()))


def iota(shape, dim):
    return lax.broadcasted_iota(jnp.int32, shape, dim)


def dot(lhs, rhs):
    return jnp.dot(lhs, rhs, preferred_element_type=F32)


def split(value):
    high = value.astype(BF16)
    return high, (value - high.astype(F32)).astype(BF16)


def tap_index(m):
    return m >> 4, (m >> 2) & 3, m & 3


def block_index(k):
    tap = (k >= 48).astype(jnp.int32) + (k >= 96).astype(jnp.int32) + (k >= 144).astype(jnp.int32)
    rest = k - 48 * tap
    return tap, rest >> 4, rest & 15


def prepare_kernel(first_ref, second_ref, critic_ref, spread_ref, critic_fwd_ref, critic_bwd_ref,
                   first_fwd_ref, first_bwd_ref, second_fwd_ref, second_bwd_ref):
    column = iota((256, 512), 0)
    place = iota((256, 512), 1)
    spread_ref[...] = (column == 2 * (place & 127) + (place >> 7) - 1).astype(F32).astype(BF16)

    def expand(weight, width, first_row):
        channel, row_tap, col_tap = tap_index(iota((48, width), 0))
        block_tap, block_channel, block_row = block_index(iota((48, width), 1))
        chosen = (channel == block_channel) & (col_tap == block_tap) & (block_row == first_row + row_tap)
        return lax.dot_general(
            weight, chosen.astype(F32).astype(BF16), TN, preferred_element_type=F32
        ).astype(BF16)

    critic = critic_ref[...]
    first = first_ref[...]
    for patch in range(4):
        critic_fwd_ref[64 * patch : 64 * patch + 64, :] = expand(critic, 192, 1 + 2 * patch)
    for row in range(10):
        first_fwd_ref[64 * row : 64 * row + 64, :] = expand(first, 144, row)

    def gather(weight, shift):
        row = iota((64, 48), 0)
        channel, row_tap, col_tap = tap_index(iota((64, 48), 1))
        inner = row & 15
        chosen = (row >> 4 == col_tap) & (inner >> 2 == channel) & ((inner & 3) + shift == row_tap)
        return dot(chosen.astype(F32).astype(BF16), weight).astype(BF16)

    critic_bwd_ref[...] = jnp.concatenate([gather(critic, 3 - 2 * patch) for patch in range(4)], axis=1)
    first_bwd_ref[...] = jnp.concatenate([gather(first, 2 - row)[:48] for row in range(6)], axis=1)
    for row_tap in range(3):
        second_fwd_ref[64 * row_tap : 64 * row_tap + 64, :] = jnp.concatenate(
            [second_ref[row_tap, col_tap] for col_tap in range(3)], axis=1
        )
        second_bwd_ref[64 * row_tap : 64 * row_tap + 64, :] = jnp.concatenate(
            [second_ref[row_tap, col_tap].astype(F32).T.astype(BF16) for col_tap in range(3)], axis=1
        )


def prepare(first, second, critic):
    shapes = [(256, 512), (256, 192), (64, 256), (640, 144), (48, 384), (192, 192), (192, 192)]
    return pl.pallas_call(
        prepare_kernel,
        out_shape=[jax.ShapeDtypeStruct(shape, BF16) for shape in shapes],
        in_specs=[VMEM] * 3,
        out_specs=[VMEM] * len(shapes),
        name="prepare",
    )(first, second, critic)


def critic_kernel(row_ref, image_ref, spread_ref, weight_ref, head_ref, sums_ref, signal_ref):
    first_patch = row_ref[0] // 2 - 1
    taps = dot(image_ref[...], spread_ref[...]).astype(BF16)
    windows = jnp.concatenate(
        [
            jnp.concatenate([taps[48 * image : 48 * image + 48, 128 * tap : 128 * tap + 128] for tap in range(4)], axis=0)
            for image in range(2)
        ],
        axis=1,
    )
    pre = dot(weight_ref[...], windows)
    head = head_ref[...]
    square = pre * pre + SOFTNESS
    inverse = lax.rsqrt(square)
    hidden = 0.6 * pre + 0.4 * (square * inverse)
    slope = 0.6 + 0.4 * (pre * inverse)
    for patch in range(4):
        valid = ((first_patch + patch >= 0) & (first_patch + patch < 128)).astype(F32)
        signal_ref[64 * patch : 64 * patch + 64, :] = (
            slope[64 * patch : 64 * patch + 64, :128] * (head * -valid)
        ).astype(BF16)
    lane = iota((1, 256), 1)
    signals = []
    hiddens = []
    for patch in (1, 2):
        part = hidden[64 * patch : 64 * patch + 64]
        logit = jnp.sum(head * part, axis=0, keepdims=True)
        sign = jnp.where(
            lane < 128, jnp.where(logit > -1.0, 1.0, 0.0), jnp.where(logit < 1.0, -1.0, 0.0)
        )
        signals.append(slope[64 * patch : 64 * patch + 64] * head * sign)
        hiddens.append(part * sign)
    signal = jnp.concatenate(signals, axis=0)
    high, low = split(signal)
    grads = lax.dot_general(windows, high, NT, preferred_element_type=F32) + lax.dot_general(
        windows, low, NT, preferred_element_type=F32
    )
    rows = []
    for block in range(12):
        here = grads[16 * block : 16 * block + 16]
        rows.append(here[3:7, :64] + here[5:9, 64:])
    sums_ref[0:24, :] = 128.0 * jnp.concatenate(
        [jnp.concatenate(rows[:6], axis=0), jnp.concatenate(rows[6:], axis=0)], axis=1
    )
    total = hiddens[0] + hiddens[1]
    ones = jnp.ones((8, 256), BF16)
    high, low = split(total)
    low, rest = split(total - high.astype(F32))
    head_sum = (
        lax.dot_general(ones, high, NT, preferred_element_type=F32)
        + lax.dot_general(ones, low, NT, preferred_element_type=F32)
        + lax.dot_general(ones, rest, NT, preferred_element_type=F32)
    )
    sums_ref[24:32, :] = jnp.concatenate([head_sum, jnp.zeros((8, 64), F32)], axis=1)


def critic(first_row, image, spread, weight, head):
    return pl.pallas_call(
        critic_kernel,
        out_shape=[jax.ShapeDtypeStruct((32, 128), F32), jax.ShapeDtypeStruct((256, 128), BF16)],
        in_specs=[SMEM] + [VMEM] * 4,
        out_specs=[VMEM] * 2,
        name="critic",
    )(first_row, image, spread, weight, head)


def shifted(value, step):
    if step == 0:
        return value
    zero = jnp.zeros(value.shape[:1] + (1,), value.dtype)
    parts = []
    for start in range(0, value.shape[1], 256):
        here = value[:, start : start + 256]
        if step > 0:
            parts.append(jnp.concatenate([here[:, 1:], zero], axis=1))
        else:
            parts.append(jnp.concatenate([zero, here[:, :-1]], axis=1))
    return parts[0] if len(parts) == 1 else jnp.concatenate(parts, axis=1)


def feature_kernel(row_ref, image_ref, signal_ref, lpips_ref, spread_ref, critic_bwd_ref, first_fwd_ref,
                   first_bwd_ref, second_fwd_ref, second_bwd_ref, out_ref, slope_ref, pre_ref, act_ref):
    first_row = row_ref[0]

    def valid(row):
        return ((first_row + row >= 0) & (first_row + row < 256)).astype(F32)

    line = iota((16, 256), 0) + (first_row - 4)
    inside = ((line >= 0) & (line < 256)).astype(F32)
    images = []
    for image in range(2):
        parts = []
        for channel in range(3):
            start = 48 * image + 16 * channel
            here = image_ref[start : start + 16, :].astype(F32)
            parts.append((here - LPIPS_SHIFT[channel]) / LPIPS_SCALE[channel] * inside)
        images.append(jnp.concatenate(parts, axis=0))
    scaled = jnp.concatenate(images, axis=1)
    windows = jnp.concatenate([shifted(scaled, step).astype(BF16) for step in (-1, 0, 1)], axis=0)
    pre_ref[...] = dot(first_fwd_ref[...], windows)
    for row in range(10):
        value = pre_ref[64 * row : 64 * row + 64, :]
        square = value * value + SOFTNESS
        inverse = lax.rsqrt(square)
        if 2 <= row < 8:
            slope_ref[64 * row - 128 : 64 * row - 64, :] = 0.5 + 0.5 * (value * inverse)[:, :256]
        act = (value + square * inverse) * (0.5 * valid(row - 3))
        stack = jnp.concatenate([shifted(act, step).astype(BF16) for step in (-1, 0, 1)], axis=0)
        product = dot(second_fwd_ref[...], stack)
        for row_tap in range(3):
            target = row - row_tap
            if 0 <= target < 8:
                part = product[64 * row_tap : 64 * row_tap + 64]
                if row_tap == 0:
                    act_ref[64 * target : 64 * target + 64, :] = part
                else:
                    act_ref[64 * target : 64 * target + 64, :] += part
    weights = lpips_ref[...]
    acts = [None] * 6
    for row in range(8):
        value = act_ref[64 * row : 64 * row + 64, :]
        square = value * value + SOFTNESS
        inverse = lax.rsqrt(square)
        feature = 0.5 * (value + square * inverse)
        power = jnp.sum(feature * feature, axis=0, keepdims=True) + 1e-6
        norm = lax.rsqrt(power)
        unit = feature * norm
        unit_fake = unit[:, :256]
        direction = weights * (unit_fake - unit[:, 256:])
        inner = jnp.sum(direction * unit_fake, axis=0, keepdims=True)
        slope = 0.5 + 0.5 * (value[:, :256] * inverse[:, :256])
        grad = (direction - unit_fake * inner) * slope * (norm[:, :256] * (2.0 * valid(row - 2)))
        stack = jnp.concatenate([shifted(grad, step).astype(BF16) for step in (1, 0, -1)], axis=0)
        product = dot(second_bwd_ref[...], stack)
        for row_tap in range(3):
            target = row - 2 + row_tap
            if 0 <= target < 6:
                part = product[64 * row_tap : 64 * row_tap + 64]
                acts[target] = part if acts[target] is None else acts[target] + part
    grads = jnp.concatenate(
        [
            (acts[row] * slope_ref[64 * row : 64 * row + 64, :] * valid(row - 1)).astype(BF16)
            for row in range(6)
        ],
        axis=0,
    )
    product = dot(first_bwd_ref[...], grads)
    image_grad = shifted(product[0:16], 1) + product[16:32] + shifted(product[32:48], -1)
    product = dot(critic_bwd_ref[...], signal_ref[...])
    taps = jnp.concatenate([product[16 * tap : 16 * tap + 16] for tap in range(4)], axis=1)
    high, low = split(taps)
    critic_grad = lax.dot_general(high, spread_ref[...], NT, preferred_element_type=F32) + lax.dot_general(
        low, spread_ref[...], NT, preferred_element_type=F32
    )
    for channel in range(3):
        out_ref[channel] = (
            image_grad[4 * channel : 4 * channel + 4] / LPIPS_SCALE[channel]
            + critic_grad[4 * channel : 4 * channel + 4]
        )


def features(first_row, image, signal, lpips, spread, critic_bwd, first_fwd, first_bwd, second_fwd, second_bwd):
    return pl.pallas_call(
        feature_kernel,
        out_shape=jax.ShapeDtypeStruct((3, 4, 256), F32),
        in_specs=[SMEM] + [VMEM] * 9,
        out_specs=VMEM,
        scratch_shapes=[
            pltpu.VMEM((384, 256), F32),
            pltpu.VMEM((640, 512), F32),
            pltpu.VMEM((512, 512), F32),
        ],
        compiler_params=pltpu.CompilerParams(vmem_limit_bytes=32 * 1024 * 1024),
        cost_estimate=pl.CostEstimate(flops=1_000_000_000, bytes_accessed=1_000_000, transcendentals=1_000_000),
        name="features",
    )(first_row, image, signal, lpips, spread, critic_bwd, first_fwd, first_bwd, second_fwd, second_bwd)


def weight_rows(weight):
    moved = jnp.transpose(weight, (1, 2, 3, 0))
    taps = moved.shape[1]
    return jnp.pad(moved, ((0, 0), (0, 4 - taps), (0, 4 - taps), (0, 0))).reshape(48, 64)


def exchange_sum(value, axes):
    peers = lax.axis_size(axes)
    copies = jnp.broadcast_to(value[None], (peers,) + value.shape)
    return jnp.sum(lax.all_to_all(copies, axes, 0, 0).astype(F32), axis=0)


def shards(fake, real, vgg_first, vgg_second, lpips_weights, critic_conv, critic_head):
    count = lax.axis_size(ROWS)
    first_row = (lax.axis_index(ROWS) * 4).astype(jnp.int32)[None]
    images = jnp.concatenate([fake, real], axis=0)
    far_pairs = [(2 * k + 1, 2 * k + 2) for k in range(count // 2 - 1)]
    far = lax.ppermute(images, ROWS, far_pairs + [(b, a) for a, b in far_pairs])
    near = lax.ppermute(images, "c", [(0, 1), (1, 0)])
    spread, critic_fwd, critic_bwd, first_fwd, first_bwd, second_fwd, second_bwd = prepare(
        weight_rows(vgg_first), jnp.transpose(vgg_second, (2, 3, 0, 1)), weight_rows(critic_conv)
    )
    lower = lax.axis_index("c") == 0
    image = jnp.concatenate(
        [jnp.where(lower, far, near), images, jnp.where(lower, near, far), jnp.zeros_like(images)], axis=2
    ).reshape(96, 256)
    sums, signal = critic(first_row, image, spread, critic_fwd, critic_head[:, None])
    plane = exchange_sum(sums.astype(jnp.float16), PLANE)
    total = exchange_sum((plane * (1.0 / 32.0)).astype(jnp.float16), COLUMN)
    grad_image = features(
        first_row, image, signal, lpips_weights[:, None], spread, critic_bwd, first_fwd, first_bwd, second_fwd,
        second_bwd,
    )
    patches = 8 * 128 * 128
    conv = jnp.concatenate([total[:24, :64], total[:24, 64:]], axis=0) * (32.0 / 128.0 / patches)
    conv_grad = jnp.transpose(conv.reshape(4, 3, 4, 64), (3, 1, 2, 0))
    head_grad = (total[24, :64] + total[24, 64:]) * (32.0 / patches)
    return grad_image[None], conv_grad, head_grad


def solution(mesh):
    wide = Mesh(mesh.devices.reshape(2, 4, 4, 8, 2), ("zh", "y", "x", "zl", "c"))
    return jax.shard_map(
        shards,
        mesh=wide,
        in_specs=(P(DP, None, ROWS, None), P(DP, None, ROWS, None), P(), P(), P(), P(), P()),
        out_specs=(P(DP, None, ROWS, None), P(), P()),
        check_vma=False,
    )
```

time: 218 us -> 65.9 us (0.30)
  blocking collectives: 135 us -> 22.6 us
  local copies, waits for them, and re-layouts: 31.3 us -> 4.3 us
  matrix products: 18.7 us -> 0 us
  Pallas kernels: 0 us -> 7.47 us
  waiting for transfers between devices: 3.57 us -> 9.1 us
  starting transfers between devices: 23.2 us -> 18.1 us
    psum x1 -> x0, blocking collectives: 135 us -> none  [shards(): conv_grad, head_grad = lax.psum((conv_part, head_part), ('dp', 'rows'))]
    all_to_all x0 -> x1, blocking collectives: none -> 22.6 us  [exchange_sum(): return jnp.sum(lax.all_to_all(copies, axes, 0, 0).astype(F32), axis=0)]
    slice x29 -> x1, local copies, waits for them, and re-layouts: 15.6 us -> 0.07 us  [shards(): total[:24, :64]]
    ppermute x8 -> x2, starting transfers between devices: 23.2 us -> 9.45 us  [the longest x1 4.93 us: shards(): far = lax.ppermute(images, ROWS, far_pairs + [(b, a) for a, b in far_pairs])]
    conv_general_dilated x5 -> x0, matrix products: 12.3 us -> none  [the longest x2 6.57 us: backward_taps(): lax.conv_general_dilated(inputs, flipped, (1, 1), ((0, 0), (0, 0)), dimen...]
    all_to_all x0 -> x1, waiting for transfers between devices: none -> 9.09 us  [exchange_sum(): return jnp.sum(lax.all_to_all(copies, axes, 0, 0).astype(F32), axis=0)]
    all_to_all x0 -> x1, starting transfers between devices: none -> 8.7 us  [exchange_sum(): return jnp.sum(lax.all_to_all(copies, axes, 0, 0).astype(F32), axis=0)]
    pallas_call x0 -> x3, Pallas kernels: none -> 7.47 us  [the longest x1 2.9 us: features(): pl.pallas_call(feature_kernel, out_shape=jax.ShapeDtypeStruct((3, 4, 256)...]
  transfers between devices with their start and end apart: 8 -> 3, of which waited for: 2 -> 1; matrix products, arithmetic and copies ran while one was open for 2% -> 2% of each run, Pallas kernels for 0% -> 8%
where the time goes in v1:
time: 65.9 us; the launch traced here: 64.5 us
  blocking collectives  22.6 us (34%)
  starting transfers between devices  18.1 us (27%)
  waiting for transfers between devices  9.1 us (14%)
  Pallas kernels  7.47 us (11%)
  local copies, waits for them, and re-layouts  4.3 us (7%)
  other arithmetic  2.1 us (3%)
  between operations  0.83 us (1%)
    all_to_all x1, blocking collectives, exchange_sum(): return jnp.sum(lax.all_to_all(copies, axes, 0, 0).astype(F32), axis=0)  22.6 us
    all_to_all x1, waiting for transfers between devices, exchange_sum(): return jnp.sum(lax.all_to_all(copies, axes, 0, 0).astype(F32), axis=0)  9.09 us
    all_to_all x1, starting transfers between devices, exchange_sum(): return jnp.sum(lax.all_to_all(copies, axes, 0, 0).astype(F32), axis=0)  8.7 us
    ppermute x1, starting transfers between devices, shards(): far = lax.ppermute(images, ROWS, far_pairs + [(b, a) for a, b in far_pairs])  4.93 us
    ppermute x1, starting transfers between devices, shards(): near = lax.ppermute(images, 'c', [(0, 1), (1, 0)])  4.51 us
    pallas_call x1, Pallas kernels, features(): pl.pallas_call(feature_kernel, out_shape=jax.ShapeDtypeStruct((3, 4, 256)...  2.9 us
    pallas_call x1, Pallas kernels, critic(): pl.pallas_call(critic_kernel, out_shape=[jax.ShapeDtypeStruct((32, 128),...  2.42 us
    pallas_call x1, Pallas kernels, prepare(): pl.pallas_call(prepare_kernel, out_shape=[jax.ShapeDtypeStruct(shape, BF1...  2.15 us
  transfers between devices with their start and end apart: 3, of which 1 were waited for; matrix products, arithmetic and copies ran while one was open for 2% of the time, Pallas kernels for 8%

profile of v1, /device:TPU:1, one launch (start us, length us, event | category | flops | bytes accessed | tf_op | source)
XLA Modules:
  0.0 64.5 jit_solution(15499042049329483951)
XLA Ops:
  0.6 0.7 %constant_dynamic-update-slice_fusion.1 = bf16[2,3,4,256]{3,2,1,0:T(4,128)(2,1)S(1)} fusion(bf16[1,3,4,256]{3,2,1,0:T(4,128)(2,1)} %param.7), kind=kLoop, calls=%fused_computation.8 | loop fusion | bytes 12288
  1.4 4.9 %collective-permute-start = (bf16[2,3,4,256]{3,2,1,0:T(4,128)(2,1)S(1)}, bf16[2,3,4,256]{3,2,1,0:T(4,128)(2,1)S(1)}, u32[]{:S(2)}, u32[]{:S(2)}) collective-permute-start(bf16[2,3,4,256]{3,2,1,0:T(4,128)(2,1)S(1)} %constant_dynamic-update-slice_fusion), channel_id=1, source_target_pairs={{1,2},{3,4},{5,6},{7,8},{9,10},{11,12},{13,14},{15,16},{17,18},{19... | collective-permute-start | bytes 36872 | tf_op jit(solution)/shard_map/ppermute | solution.py:293
  6.3 4.5 %collective-permute-start.1 = (bf16[2,3,4,256]{3,2,1,0:T(4,128)(2,1)S(1)}, bf16[2,3,4,256]{3,2,1,0:T(4,128)(2,1)S(1)}, u32[]{:S(2)}, u32[]{:S(2)}) collective-permute-start(bf16[2,3,4,256]{3,2,1,0:T(4,128)(2,1)S(1)} %constant_dynamic-update-slice_fusion), channel_id=1, source_target_pairs={{0,1},{1,0},{2,3},{3,2},{4,5},{5,4},{6,7},{7,6},{8,9},{9,8},{10,11... | collective-permute-start | bytes 36872 | tf_op jit(solution)/shard_map/ppermute | solution.py:294
  10.8 0.0 copy-start.10
  10.8 0.6 %copy-done.10 = f32[64]{0:T(128)S(1)} copy-done((f32[64]{0:T(128)S(1)}, f32[64]{0:T(128)}, u32[]{:S(2)}) %copy-start.10) | copy-done | bytes 280
  11.5 0.7 %copy.15.head_ref = f32[64,1]{1,0:T(8,128)} copy(f32[64,1]{0,1:T(1,128)S(1)} %bitcast.23) | data formatting | bytes 512 | tf_op jit(solution)/shard_map/broadcast_in_dim | solution.py:302
  12.2 0.6 pad.4
  12.8 0.1 pad.10.clone
  12.9 2.1 %prepare.1 = (bf16[256,512]{1,0:T(8,128)(2,1)}, bf16[256,192]{1,0:T(8,128)(2,1)}, bf16[64,256]{1,0:T(8,128)(2,1)}, bf16[640,144]{1,0:T(8,128)(2,1)}, bf16[48,384...) custom-call(bf16[48,64]{1,0:T(8,128)(2,1)} %bitcast.20, bf16[3,3,64,64]{3,2,1,0:T(8,128)(2,1)} %bitcast.18, ...), custom_call_target="tpu_custom_call" | custom-call | tf_op jit(solution)/shard_map/prepare/pallas_call | solution.py:89
  15.0 0.0 collective-permute-done
  15.0 0.0 collective-permute-done.1
  15.1 0.7 %maximum_maximum_fusion = bf16[2,3,16,256]{3,2,1,0:T(8,128)(2,1)} fusion(bf16[2,3,4,256]{3,2,1,0:T(4,128)(2,1)S(1)} %get-tuple-element.28, bf16[2,3,4,256]{3,2,1,0:T(4,128)(2,1)S(1)} %constant_dynamic-update-slice_fusion, bf16[2,3,4,256]{3,2,1,0:T(4,128)(2,1)S(1)} %get-tuple-element.27, bf16[16]{0:T(256)(128)(2,1)S(1)} %pad.10.clone), kind=kLoop, calls=%fused_computation.2 | loop fusion | flops 196608 | bytes 86048 | tf_op jit(solution)/shard_map/concatenate | solution.py:299
  15.8 2.4 %critic.1 = (f32[32,128]{1,0:T(8,128)}, bf16[256,128]{1,0:T(8,128)(2,1)}) custom-call(s32[1]{0:T(128)} %bitcast.row_ref, bf16[96,256]{1,0:T(8,128)(2,1)} %bitcast.16, bf16[256,512]{1,0:T(8,128)(2,1)} %get-tuple-element.12.spread_ref, bf16[256,192]{1,0:T(8,128)(2,1)} %get-tuple-element.13.weight_ref, f32[64,1]{1,0:T(8,128)} %copy.15.head_ref), custom_call_target="tpu_custom_call" | custom-call | tf_op jit(solution)/shard_map/critic/pallas_call | solution.py:155
  18.2 0.7 %convert_element_type.18 = f16[32,128]{1,0:T(8,128)(2,1)S(1)} convert(f32[32,128]{1,0:T(8,128)} %get-tuple-element.20) | non-fusion elementwise | flops 4096 | bytes 24576 | tf_op jit(solution)/shard_map/convert_element_type | solution.py:303
  19.0 22.6 %all_to_all.10 = f16[32,32,128]{2,1,0:T(8,128)(2,1)S(1)} all-to-all(f16[32,32,128]{2,1,0:T(8,128)(2,1)S(1)} %broadcast_in_dim.32), channel_id=1, replica_groups=mesh['zh'=2,'y'=4,'x'=4,'zl'=8,'c'=2] {'y','x','c'}, dimensions={0} | all-to-all | bytes 524288 | tf_op jit(solution)/shard_map/all_to_all | solution.py:285
  41.7 0.0 copy-start.11
  41.7 0.7 %broadcast_in_dim.33 = f16[16,32,128]{2,1,0:T(8,128)(2,1)} broadcast(f16[32,128]{1,0:T(8,128)(2,1)S(1)} %multiply_convert_fusion), dimensions={1,2} | broadcast | bytes 139264 | tf_op jit(solution)/shard_map/broadcast_in_dim | solution.py:284
  42.3 8.7 %all-to-all-start.1 = ((f16[16,32,128]{2,1,0:T(8,128)(2,1)}), f16[16,32,128]{2,1,0:T(8,128)(2,1)S(1)}, u32[]{:S(2)}, u32[]{:S(2)}) async-start(f16[16,32,128]{2,1,0:T(8,128)(2,1)} %broadcast_in_dim.33), calls=%async_computation.1 | async-start | bytes 262144 | tf_op jit(solution)/shard_map/all_to_all | solution.py:285
  51.1 0.1 copy.16.lpips_ref
  51.2 2.9 %features.1 = f32[3,4,256]{2,1,0:T(4,128)} custom-call(s32[1]{0:T(128)} %bitcast.row_ref, bf16[96,256]{1,0:T(8,128)(2,1)S(1)} %bitcast.17, bf16[256,128]{1,0:T(8,128)(2,1)S(1)} %copy-done.5, f32[64,1]{1,0:T(8,128)S(1)} %copy.16.lpips_ref, bf16[256,512]{1,0:T(8,128)(2,1)S(1)} %copy-done, bf16[64,256]{1,0:T(8,128)(2,1)S(1)} %copy-done.7, ...), custom_call_target="tpu_custom_call" | custom-call | flops 1000000000 | bytes 1000000 | tf_op jit(solution)/shard_map/features/pallas_call | solution.py:260
  54.1 9.1 %all-to-all-done.1 = f16[16,32,128]{2,1,0:T(8,128)(2,1)S(1)} async-done(((f16[16,32,128]{2,1,0:T(8,128)(2,1)}), f16[16,32,128]{2,1,0:T(8,128)(2,1)S(1)}, u32[]{:S(2)}, u32[]{:S(2)}) %all-to-all-start.1) | async-done | bytes 131104 | tf_op jit(solution)/shard_map/all_to_all | solution.py:285
  63.3 0.1 fusion.2
  63.3 0.6 fusion.1
  63.9 0.6 copy.17
  (29 shorter events, 0.2 us)
Async XLA Ops:
  0.6 0.7 %copy-start.9 = (bf16[1,3,4,256]{3,2,1,0:T(4,128)(2,1)S(1)}, bf16[1,3,4,256]{3,2,1,0:T(4,128)(2,1)}, u32[]{:S(2)}) copy-start(bf16[1,3,4,256]{3,2,1,0:T(4,128)(2,1)} %param.8) | copy-start | bytes 18436
  1.4 13.7 %collective-permute-start = (bf16[2,3,4,256]{3,2,1,0:T(4,128)(2,1)S(1)}, bf16[2,3,4,256]{3,2,1,0:T(4,128)(2,1)S(1)}, u32[]{:S(2)}, u32[]{:S(2)}) collective-permute-start(bf16[2,3,4,256]{3,2,1,0:T(4,128)(2,1)S(1)} %constant_dynamic-update-slice_fusion), channel_id=1, source_target_pairs={{1,2},{3,4},{5,6},{7,8},{9,10},{11,12},{13,14},{15,16},{17,18},{19... | collective-permute-start | bytes 36872 | tf_op jit(solution)/shard_map/ppermute | solution.py:293
  6.3 8.7 %collective-permute-start.1 = (bf16[2,3,4,256]{3,2,1,0:T(4,128)(2,1)S(1)}, bf16[2,3,4,256]{3,2,1,0:T(4,128)(2,1)S(1)}, u32[]{:S(2)}, u32[]{:S(2)}) collective-permute-start(bf16[2,3,4,256]{3,2,1,0:T(4,128)(2,1)S(1)} %constant_dynamic-update-slice_fusion), channel_id=1, source_target_pairs={{0,1},{1,0},{2,3},{3,2},{4,5},{5,4},{6,7},{7,6},{8,9},{9,8},{10,11... | collective-permute-start | bytes 36872 | tf_op jit(solution)/shard_map/ppermute | solution.py:294
  10.8 0.7 %copy-start.10 = (f32[64]{0:T(128)S(1)}, f32[64]{0:T(128)}, u32[]{:S(2)}) copy-start(f32[64]{0:T(128)} %param.13) | copy-start | bytes 772
  11.5 0.7 %copy-start.8 = (bf16[64,3,3,3]{0,3,2,1:T(4,128)(2,1)S(1)}, bf16[64,3,3,3]{0,3,2,1:T(4,128)(2,1)}, u32[]{:S(2)}) copy-start(bf16[64,3,3,3]{0,3,2,1:T(4,128)(2,1)} %param.9) | copy-start | bytes 10372
  19.0 32.2 %copy-start.4 = (bf16[192,192]{1,0:T(8,128)(2,1)S(1)}, bf16[192,192]{1,0:T(8,128)(2,1)}, u32[]{:S(2)}) copy-start(bf16[192,192]{1,0:T(8,128)(2,1)} %get-tuple-element.19.second_bwd_ref) | copy-start | bytes 221188
  19.0 32.2 %copy-start.5 = (bf16[256,128]{1,0:T(8,128)(2,1)S(1)}, bf16[256,128]{1,0:T(8,128)(2,1)}, u32[]{:S(2)}) copy-start(bf16[256,128]{1,0:T(8,128)(2,1)} %get-tuple-element.14.signal_ref) | copy-start | bytes 196612
  19.0 32.2 %copy-start.6 = (bf16[48,384]{1,0:T(8,128)(2,1)S(1)}, bf16[48,384]{1,0:T(8,128)(2,1)}, u32[]{:S(2)}) copy-start(bf16[48,384]{1,0:T(8,128)(2,1)} %get-tuple-element.17.first_bwd_ref) | copy-start | bytes 110596
  19.0 32.2 %copy-start.7 = (bf16[64,256]{1,0:T(8,128)(2,1)S(1)}, bf16[64,256]{1,0:T(8,128)(2,1)}, u32[]{:S(2)}) copy-start(bf16[64,256]{1,0:T(8,128)(2,1)} %get-tuple-element.15.critic_bwd_ref) | copy-start | bytes 98308
  41.6 9.6 %copy-start.2 = (bf16[640,144]{1,0:T(8,128)(2,1)S(1)}, bf16[640,144]{1,0:T(8,128)(2,1)}, u32[]{:S(2)}) copy-start(bf16[640,144]{1,0:T(8,128)(2,1)} %get-tuple-element.16.first_fwd_ref) | copy-start | bytes 552964
  41.6 9.6 %copy-start = (bf16[256,512]{1,0:T(8,128)(2,1)S(1)}, bf16[256,512]{1,0:T(8,128)(2,1)}, u32[]{:S(2)}) copy-start(bf16[256,512]{1,0:T(8,128)(2,1)} %get-tuple-element.12.spread_ref) | copy-start | bytes 786436
  41.7 9.4 %copy-start.11 = (f32[64]{0:T(128)S(1)}, f32[64]{0:T(128)}, u32[]{:S(2)}) copy-start(f32[64]{0:T(128)} %param.11) | copy-start | bytes 772
  42.3 8.9 %copy-start.1 = (bf16[2,3,16,256]{3,2,1,0:T(8,128)(2,1)S(1)}, bf16[2,3,16,256]{3,2,1,0:T(8,128)(2,1)}, u32[]{:S(2)}) copy-start(bf16[2,3,16,256]{3,2,1,0:T(8,128)(2,1)} %maximum_maximum_fusion) | copy-start | bytes 147460
  42.3 8.9 %copy-start.3 = (bf16[192,192]{1,0:T(8,128)(2,1)S(1)}, bf16[192,192]{1,0:T(8,128)(2,1)}, u32[]{:S(2)}) copy-start(bf16[192,192]{1,0:T(8,128)(2,1)} %get-tuple-element.18.second_fwd_ref) | copy-start | bytes 221188
  42.3 20.9 %all-to-all-start.1 = ((f16[16,32,128]{2,1,0:T(8,128)(2,1)}), f16[16,32,128]{2,1,0:T(8,128)(2,1)S(1)}, u32[]{:S(2)}, u32[]{:S(2)}) async-start(f16[16,32,128]{2,1,0:T(8,128)(2,1)} %broadcast_in_dim.33), calls=%async_computation.1 | async-start | bytes 262144 | tf_op jit(solution)/shard_map/all_to_all | solution.py:285

commit v2 on v1

--- a/solution.py
+++ b/solution.py
@@ -20,6 +20,7 @@
 SMEM = pl.BlockSpec(memory_space=pltpu.SMEM)
 TN = (((0,), (0,)), ((), ()))
 NT = (((1,), (1,)), ((), ()))
+SMALL = pltpu.CompilerParams(vmem_limit_bytes=8 * 1024 * 1024)
 
 
 def iota(shape, dim):
@@ -45,24 +46,50 @@
     return tap, rest >> 4, rest & 15
 
 
-def prepare_kernel(first_ref, second_ref, critic_ref, spread_ref, critic_fwd_ref, critic_bwd_ref,
-                   first_fwd_ref, first_bwd_ref, second_fwd_ref, second_bwd_ref):
+def place_rows(previous_ref, image_ref, next_ref, image, channel):
+    parts = [ref[image, channel].astype(F32) for ref in (previous_ref, image_ref, next_ref)]
+    return jnp.concatenate(parts + [jnp.zeros_like(parts[0])], axis=0)
+
+
+def expand(weight, width, first_row):
+    channel, row_tap, col_tap = tap_index(iota((48, width), 0))
+    block_tap, block_channel, block_row = block_index(iota((48, width), 1))
+    chosen = (channel == block_channel) & (col_tap == block_tap) & (block_row == first_row + row_tap)
+    return lax.dot_general(
+        weight, chosen.astype(F32).astype(BF16), TN, preferred_element_type=F32
+    ).astype(BF16)
+
+
+def critic_weights_kernel(critic_ref, head_ref, spread_ref, fwd_ref, column_ref):
     column = iota((256, 512), 0)
     place = iota((256, 512), 1)
     spread_ref[...] = (column == 2 * (place & 127) + (place >> 7) - 1).astype(F32).astype(BF16)
-
-    def expand(weight, width, first_row):
-        channel, row_tap, col_tap = tap_index(iota((48, width), 0))
-        block_tap, block_channel, block_row = block_index(iota((48, width), 1))
-        chosen = (channel == block_channel) & (col_tap == block_tap) & (block_row == first_row + row_tap)
-        return lax.dot_general(
-            weight, chosen.astype(F32).astype(BF16), TN, preferred_element_type=F32
-        ).astype(BF16)
-
+    critic = critic_ref[...]
+    for patch in range(4):
+        fwd_ref[64 * patch : 64 * patch + 64, :] = expand(critic, 192, 1 + 2 * patch)
+    diagonal = iota((64, 64), 0) == iota((64, 64), 1)
+    column_ref[...] = jnp.sum(jnp.where(diagonal, head_ref[...], 0.0), axis=1, keepdims=True)
+
+
+def critic_weights(critic, head):
+    return pl.pallas_call(
+        critic_weights_kernel,
+        out_shape=[
+            jax.ShapeDtypeStruct((256, 512), BF16),
+            jax.ShapeDtypeStruct((256, 192), BF16),
+            jax.ShapeDtypeStruct((64, 1), F32),
+        ],
+        in_specs=[VMEM] * 2,
+        out_specs=[VMEM] * 3,
+        compiler_params=SMALL,
+        name="critic_weights",
+    )(critic, head)
+
+
+def feature_weights_kernel(first_ref, second_ref, critic_ref, critic_bwd_ref, first_fwd_ref, first_bwd_ref,
+                           second_fwd_ref, second_bwd_ref):
     critic = critic_ref[...]
     first = first_ref[...]
-    for patch in range(4):
-        critic_fwd_ref[64 * patch : 64 * patch + 64, :] = expand(critic, 192, 1 + 2 * patch)
     for row in range(10):
         first_fwd_ref[64 * row : 64 * row + 64, :] = expand(first, 144, row)
 
@@ -84,81 +111,80 @@
         )
 
 
-def prepare(first, second, critic):
-    shapes = [(256, 512), (256, 192), (64, 256), (640, 144), (48, 384), (192, 192), (192, 192)]
+def feature_weights(first, second, critic):
+    shapes = [(64, 256), (640, 144), (48, 384), (192, 192), (192, 192)]
     return pl.pallas_call(
-        prepare_kernel,
+        feature_weights_kernel,
         out_shape=[jax.ShapeDtypeStruct(shape, BF16) for shape in shapes],
         in_specs=[VMEM] * 3,
         out_specs=[VMEM] * len(shapes),
-        name="prepare",
+        compiler_params=SMALL,
+        cost_estimate=pl.CostEstimate(flops=100_000_000, bytes_accessed=1_000_000, transcendentals=0),
+        name="feature_weights",
     )(first, second, critic)
 
 
-def critic_kernel(row_ref, image_ref, spread_ref, weight_ref, head_ref, sums_ref, signal_ref):
-    first_patch = row_ref[0] // 2 - 1
-    taps = dot(image_ref[...], spread_ref[...]).astype(BF16)
-    windows = jnp.concatenate(
+def stack_taps(taps, image):
+    return jnp.concatenate(
+        [taps[48 * image : 48 * image + 48, 128 * tap : 128 * tap + 128] for tap in range(4)], axis=0
+    )
+
+
+def critic_kernel(row_ref, previous_ref, image_ref, next_ref, spread_ref, weight_ref, head_ref, sums_ref):
+    index = row_ref[0] // 4
+    takes = (((index & 15) == 0) & (index > 0)).astype(F32)
+    keeps = 1.0 - (((index & 15) == 15) & (index < 63)).astype(F32)
+    image = jnp.concatenate(
         [
-            jnp.concatenate([taps[48 * image : 48 * image + 48, 128 * tap : 128 * tap + 128] for tap in range(4)], axis=0)
+            place_rows(previous_ref, image_ref, next_ref, image, channel)
             for image in range(2)
+            for channel in range(3)
         ],
-        axis=1,
-    )
-    pre = dot(weight_ref[...], windows)
+        axis=0,
+    ).astype(BF16)
+    taps = dot(image, spread_ref[...]).astype(BF16)
+    windows = jnp.concatenate([stack_taps(taps, 0), stack_taps(taps, 1)], axis=1)
+    pre = dot(weight_ref[0:192, :], windows)
     head = head_ref[...]
     square = pre * pre + SOFTNESS
     inverse = lax.rsqrt(square)
     hidden = 0.6 * pre + 0.4 * (square * inverse)
     slope = 0.6 + 0.4 * (pre * inverse)
-    for patch in range(4):
-        valid = ((first_patch + patch >= 0) & (first_patch + patch < 128)).astype(F32)
-        signal_ref[64 * patch : 64 * patch + 64, :] = (
-            slope[64 * patch : 64 * patch + 64, :128] * (head * -valid)
-        ).astype(BF16)
     lane = iota((1, 256), 1)
     signals = []
-    hiddens = []
-    for patch in (1, 2):
+    total = None
+    for patch, share in enumerate((takes, 1.0, keeps)):
         part = hidden[64 * patch : 64 * patch + 64]
         logit = jnp.sum(head * part, axis=0, keepdims=True)
         sign = jnp.where(
             lane < 128, jnp.where(logit > -1.0, 1.0, 0.0), jnp.where(logit < 1.0, -1.0, 0.0)
-        )
+        ) * share
         signals.append(slope[64 * patch : 64 * patch + 64] * head * sign)
-        hiddens.append(part * sign)
-    signal = jnp.concatenate(signals, axis=0)
-    high, low = split(signal)
+        total = part * sign if total is None else total + part * sign
+    high, low = split(jnp.concatenate(signals + [total], axis=0))
+    windows = jnp.concatenate([windows, jnp.ones((16, 256), BF16)], axis=0)
     grads = lax.dot_general(windows, high, NT, preferred_element_type=F32) + lax.dot_general(
         windows, low, NT, preferred_element_type=F32
     )
     rows = []
     for block in range(12):
         here = grads[16 * block : 16 * block + 16]
-        rows.append(here[3:7, :64] + here[5:9, 64:])
+        rows.append(here[1:5, :64] + here[3:7, 64:128] + here[5:9, 128:192])
     sums_ref[0:24, :] = 128.0 * jnp.concatenate(
         [jnp.concatenate(rows[:6], axis=0), jnp.concatenate(rows[6:], axis=0)], axis=1
     )
-    total = hiddens[0] + hiddens[1]
-    ones = jnp.ones((8, 256), BF16)
-    high, low = split(total)
-    low, rest = split(total - high.astype(F32))
-    head_sum = (
-        lax.dot_general(ones, high, NT, preferred_element_type=F32)
-        + lax.dot_general(ones, low, NT, preferred_element_type=F32)
-        + lax.dot_general(ones, rest, NT, preferred_element_type=F32)
-    )
-    sums_ref[24:32, :] = jnp.concatenate([head_sum, jnp.zeros((8, 64), F32)], axis=1)
-
-
-def critic(first_row, image, spread, weight, head):
+    sums_ref[24:32, :] = jnp.concatenate([grads[192:200, 192:256], jnp.zeros((8, 64), F32)], axis=1)
+
+
+def critic(*operands):
     return pl.pallas_call(
         critic_kernel,
-        out_shape=[jax.ShapeDtypeStruct((32, 128), F32), jax.ShapeDtypeStruct((256, 128), BF16)],
-        in_specs=[SMEM] + [VMEM] * 4,
-        out_specs=[VMEM] * 2,
+        out_shape=jax.ShapeDtypeStruct((32, 128), F32),
+        in_specs=[SMEM] + [VMEM] * 6,
+        out_specs=VMEM,
+        compiler_params=SMALL,
         name="critic",
-    )(first_row, image, spread, weight, head)
+    )(*operands)
 
 
 def shifted(value, step):
@@ -175,21 +201,27 @@
     return parts[0] if len(parts) == 1 else jnp.concatenate(parts, axis=1)
 
 
-def feature_kernel(row_ref, image_ref, signal_ref, lpips_ref, spread_ref, critic_bwd_ref, first_fwd_ref,
-                   first_bwd_ref, second_fwd_ref, second_bwd_ref, out_ref, slope_ref, pre_ref, act_ref):
+def feature_kernel(row_ref, previous_ref, image_ref, next_ref, far_ref, lpips_ref, spread_ref, critic_fwd_ref,
+                   head_ref, critic_bwd_ref, first_fwd_ref, first_bwd_ref, second_fwd_ref, second_bwd_ref, out_ref,
+                   below_ref, slope_ref, pre_ref, act_ref):
     first_row = row_ref[0]
+    index = first_row // 4
+    distant = (index & 15) == 15
 
     def valid(row):
         return ((first_row + row >= 0) & (first_row + row < 256)).astype(F32)
 
     line = iota((16, 256), 0) + (first_row - 4)
     inside = ((line >= 0) & (line < 256)).astype(F32)
+    below_ref[...] = jnp.where(distant, far_ref[...].astype(F32), next_ref[...].astype(F32))
     images = []
+    fake = []
     for image in range(2):
         parts = []
         for channel in range(3):
-            start = 48 * image + 16 * channel
-            here = image_ref[start : start + 16, :].astype(F32)
+            here = place_rows(previous_ref, image_ref, below_ref, image, channel)
+            if image == 0:
+                fake.append(here)
             parts.append((here - LPIPS_SHIFT[channel]) / LPIPS_SCALE[channel] * inside)
         images.append(jnp.concatenate(parts, axis=0))
     scaled = jnp.concatenate(images, axis=1)
@@ -243,7 +275,15 @@
     )
     product = dot(first_bwd_ref[...], grads)
     image_grad = shifted(product[0:16], 1) + product[16:32] + shifted(product[32:48], -1)
-    product = dot(critic_bwd_ref[...], signal_ref[...])
+    taps = dot(jnp.concatenate(fake, axis=0).astype(BF16), spread_ref[...]).astype(BF16)
+    pre = dot(critic_fwd_ref[...], stack_taps(taps, 0))
+    slope = 0.6 + 0.4 * (pre * lax.rsqrt(pre * pre + SOFTNESS))
+    head = head_ref[...]
+    signals = []
+    for patch in range(4):
+        inside = (first_row + 2 * patch - 2 >= 0) & (first_row + 2 * patch - 2 < 256)
+        signals.append((slope[64 * patch : 64 * patch + 64] * (head * -inside.astype(F32))).astype(BF16))
+    product = dot(critic_bwd_ref[...], jnp.concatenate(signals, axis=0))
     taps = jnp.concatenate([product[16 * tap : 16 * tap + 16] for tap in range(4)], axis=1)
     high, low = split(taps)
     critic_grad = lax.dot_general(high, spread_ref[...], NT, preferred_element_type=F32) + lax.dot_general(
@@ -256,21 +296,22 @@
         )
 
 
-def features(first_row, image, signal, lpips, spread, critic_bwd, first_fwd, first_bwd, second_fwd, second_bwd):
+def features(*operands):
     return pl.pallas_call(
         feature_kernel,
         out_shape=jax.ShapeDtypeStruct((3, 4, 256), F32),
-        in_specs=[SMEM] + [VMEM] * 9,
+        in_specs=[SMEM] + [VMEM] * 13,
         out_specs=VMEM,
         scratch_shapes=[
+            pltpu.VMEM((2, 3, 4, 256), F32),
             pltpu.VMEM((384, 256), F32),
             pltpu.VMEM((640, 512), F32),
             pltpu.VMEM((512, 512), F32),
         ],
-        compiler_params=pltpu.CompilerParams(vmem_limit_bytes=32 * 1024 * 1024),
+        compiler_params=pltpu.CompilerParams(vmem_limit_bytes=16 * 1024 * 1024),
         cost_estimate=pl.CostEstimate(flops=1_000_000_000, bytes_accessed=1_000_000, transcendentals=1_000_000),
         name="features",
-    )(first_row, image, signal, lpips, spread, critic_bwd, first_fwd, first_bwd, second_fwd, second_bwd)
+    )(*operands)
 
 
 def weight_rows(weight):
@@ -289,22 +330,20 @@
     count = lax.axis_size(ROWS)
     first_row = (lax.axis_index(ROWS) * 4).astype(jnp.int32)[None]
     images = jnp.concatenate([fake, real], axis=0)
-    far_pairs = [(2 * k + 1, 2 * k + 2) for k in range(count // 2 - 1)]
-    far = lax.ppermute(images, ROWS, far_pairs + [(b, a) for a, b in far_pairs])
-    near = lax.ppermute(images, "c", [(0, 1), (1, 0)])
-    spread, critic_fwd, critic_bwd, first_fwd, first_bwd, second_fwd, second_bwd = prepare(
-        weight_rows(vgg_first), jnp.transpose(vgg_second, (2, 3, 0, 1)), weight_rows(critic_conv)
-    )
-    lower = lax.axis_index("c") == 0
-    image = jnp.concatenate(
-        [jnp.where(lower, far, near), images, jnp.where(lower, near, far), jnp.zeros_like(images)], axis=2
-    ).reshape(96, 256)
-    sums, signal = critic(first_row, image, spread, critic_fwd, critic_head[:, None])
+    previous = lax.ppermute(images, ROWS, [(k, k + 1) for k in range(count - 1)])
+    following = lax.ppermute(images, ROWS, [(k + 1, k) for k in range(count - 1) if k % 16 < 15])
+    critic_rows = weight_rows(critic_conv)
+    spread, critic_fwd, head = critic_weights(critic_rows, critic_head[None])
+    sums = critic(first_row, previous, images, following, spread, critic_fwd, head)
+    sums, later, first, second, again = lax.optimization_barrier(
+        (sums, images, weight_rows(vgg_first), jnp.transpose(vgg_second, (2, 3, 0, 1)), critic_rows)
+    )
+    weights = feature_weights(first, second, again)
     plane = exchange_sum(sums.astype(jnp.float16), PLANE)
+    far = lax.ppermute(later, ROWS, [(k + 1, k) for k in range(count - 1) if k % 16 == 15])
     total = exchange_sum((plane * (1.0 / 32.0)).astype(jnp.float16), COLUMN)
     grad_image = features(
-        first_row, image, signal, lpips_weights[:, None], spread, critic_bwd, first_fwd, first_bwd, second_fwd,
-        second_bwd,
+        first_row, previous, images, following, far, lpips_weights[:, None], spread, critic_fwd, head, *weights
     )
     patches = 8 * 128 * 128
     conv = jnp.concatenate([total[:24, :64], total[:24, 64:]], axis=0) * (32.0 / 128.0 / patches)

time: 65.9 us -> 63 us (0.956)
  the two profiles are of different devices: /device:TPU:1 before, /device:TPU:2 now
where the time goes in v2:
time: 63 us; the launch traced here: 62.6 us
  starting transfers between devices  27.7 us (44%)
  blocking collectives  15.1 us (24%)
  waiting for transfers between devices  10.5 us (17%)
  Pallas kernels  4.78 us (8%)
  local copies, waits for them, and re-layouts  2.92 us (5%)
  between operations  0.78 us (1%)
  other arithmetic  0.68 us (1%)
    all_to_all x1, blocking collectives, exchange_sum(): return jnp.sum(lax.all_to_all(copies, axes, 0, 0).astype(F32), axis=0)  15.1 us
    all_to_all x1, starting transfers between devices, exchange_sum(): return jnp.sum(lax.all_to_all(copies, axes, 0, 0).astype(F32), axis=0)  13.9 us
    ppermute x1, starting transfers between devices, shards(): lax.ppermute(later, ROWS, [(k + 1, k) for k in range(count - 1) if k % 16...  10.6 us
    ppermute x1, waiting for transfers between devices, shards(): lax.ppermute(images, ROWS, [(k, k + 1) for k in range(count - 1)])  9.69 us
    pallas_call x1, Pallas kernels, features(): pl.pallas_call(feature_kernel, out_shape=jax.ShapeDtypeStruct((3, 4, 256)...  3.29 us
    unnamed x14, local copies, waits for them, and re-layouts  2.02 us
    ppermute x1, starting transfers between devices, shards(): lax.ppermute(images, ROWS, [(k, k + 1) for k in range(count - 1)])  1.92 us
    ppermute x1, starting transfers between devices, shards(): lax.ppermute(images, ROWS, [(k + 1, k) for k in range(count - 1) if k % 1...  1.29 us
  transfers between devices with their start and end apart: 4, of which 2 were waited for; matrix products, arithmetic and copies ran while one was open for 0% of the time, Pallas kernels for 6%

profile of v2, /device:TPU:2, one launch (start us, length us, event | category | flops | bytes accessed | tf_op | source)
XLA Modules:
  0.0 62.6 jit_solution(8292169706295936218)
XLA Ops:
  0.6 0.7 %constant_dynamic-update-slice_fusion.1 = bf16[2,3,4,256]{3,2,1,0:T(4,128)(2,1)S(1)} fusion(bf16[1,3,4,256]{3,2,1,0:T(4,128)(2,1)} %param.7), kind=kLoop, calls=%fused_computation.5 | loop fusion | bytes 12288
  1.4 1.9 %collective-permute-start = (bf16[2,3,4,256]{3,2,1,0:T(4,128)(2,1)S(1)}, bf16[2,3,4,256]{3,2,1,0:T(4,128)(2,1)S(1)}, u32[]{:S(2)}, u32[]{:S(2)}) collective-permute-start(bf16[2,3,4,256]{3,2,1,0:T(4,128)(2,1)S(1)} %constant_dynamic-update-slice_fusion.image_ref), channel_id=1, source_target_pairs={{0,1},{1,2},{2,3},{3,4},{4,5},{5,6},{6,7},{7,8},{8,9},{9,10},{10,1... | collective-permute-start | bytes 36872 | tf_op jit(solution)/shard_map/ppermute | solution.py:333
  3.3 1.3 %collective-permute-start.1 = (bf16[2,3,4,256]{3,2,1,0:T(4,128)(2,1)S(1)}, bf16[2,3,4,256]{3,2,1,0:T(4,128)(2,1)S(1)}, u32[]{:S(2)}, u32[]{:S(2)}) collective-permute-start(bf16[2,3,4,256]{3,2,1,0:T(4,128)(2,1)S(1)} %constant_dynamic-update-slice_fusion.image_ref), channel_id=1, source_target_pairs={{1,0},{2,1},{3,2},{4,3},{5,4},{6,5},{7,6},{8,7},{9,8},{10,9},{11,1... | collective-permute-start | bytes 36872 | tf_op jit(solution)/shard_map/ppermute | solution.py:334
  4.6 0.0 copy-start
  4.6 0.0 copy-start.1
  4.6 0.0 copy-start.3
  4.6 0.7 %copy-done = bf16[64,3,4,4]{0,3,2,1:T(4,128)(2,1)S(1)} copy-done((bf16[64,3,4,4]{0,3,2,1:T(4,128)(2,1)S(1)}, bf16[64,3,4,4]{0,3,2,1:T(4,128)(2,1)}, u32[]{:S(2)}) %copy-start) | copy-done | bytes 6168
  5.3 0.3 critic_weights.1
  5.6 9.7 %collective-permute-done.previous_ref = bf16[2,3,4,256]{3,2,1,0:T(4,128)(2,1)S(1)} collective-permute-done((bf16[2,3,4,256]{3,2,1,0:T(4,128)(2,1)S(1)}, bf16[2,3,4,256]{3,2,1,0:T(4,128)(2,1)S(1)}, u32[]{:S(2)}, u32[]{:S(2)}) %collective-permute-start) | collective-permute-done | bytes 12320 | tf_op jit(solution)/shard_map/ppermute | solution.py:333
  15.3 0.0 collective-permute-done.1.next_ref
  15.3 0.8 %critic.1 = f32[32,128]{1,0:T(8,128)S(1)} custom-call(s32[1]{0:T(128)} %bitcast.row_ref, bf16[2,3,4,256]{3,2,1,0:T(4,128)(2,1)S(1)} %collective-permute-done.previous_ref, bf16[2,3,4,256]{3,2,1,0:T(4,128)(2,1)S(1)} %constant_dynamic-update-slice_fusion.image_ref, bf16[2,3,4,256]{3,2,1,0:T(4,128)(2,1)S(1)} %collective-permute-done.1.next_ref, ...), custom_call_target="tpu_custom_call" | custom-call | tf_op jit(solution)/shard_map/critic/pallas_call | solution.py:180
  16.2 15.1 %all_to_all.10 = f16[32,32,128]{2,1,0:T(8,128)(2,1)S(1)} all-to-all(f16[32,32,128]{2,1,0:T(8,128)(2,1)S(1)} %broadcast_in_dim.28), channel_id=1, replica_groups=mesh['zh'=2,'y'=4,'x'=4,'zl'=8,'c'=2] {'y','x','c'}, dimensions={0} | all-to-all | bytes 524288 | tf_op jit(solution)/shard_map/all_to_all | solution.py:326
  31.4 0.7 %broadcast_in_dim.29 = f16[16,32,128]{2,1,0:T(8,128)(2,1)} broadcast(f16[32,128]{1,0:T(8,128)(2,1)S(1)} %multiply_convert_fusion), dimensions={1,2} | broadcast | bytes 139264 | tf_op jit(solution)/shard_map/broadcast_in_dim | solution.py:325
  32.0 13.9 %all-to-all-start.1 = ((f16[16,32,128]{2,1,0:T(8,128)(2,1)}), f16[16,32,128]{2,1,0:T(8,128)(2,1)S(1)}, u32[]{:S(2)}, u32[]{:S(2)}) async-start(f16[16,32,128]{2,1,0:T(8,128)(2,1)} %broadcast_in_dim.29), calls=%async_computation.1 | async-start | bytes 262144 | tf_op jit(solution)/shard_map/all_to_all | solution.py:326
  45.9 0.0 copy-start.5
  45.9 10.6 %collective-permute-start.2 = (bf16[2,3,4,256]{3,2,1,0:T(4,128)(2,1)S(1)}, bf16[2,3,4,256]{3,2,1,0:T(4,128)(2,1)S(1)}, u32[]{:S(2)}, u32[]{:S(2)}) collective-permute-start(bf16[2,3,4,256]{3,2,1,0:T(4,128)(2,1)S(1)} %constant_dynamic-update-slice_fusion.image_ref), channel_id=1, source_target_pairs={{16,15},{32,31},{48,47},{80,79},{96,95},{112,111},{144,143},{160,1... | collective-permute-start | bytes 36872 | tf_op jit(solution)/shard_map/ppermute | solution.py:343
  56.6 0.1 copy.13.lpips_ref
  56.7 0.4 feature_weights.1
  57.1 0.8 %collective-permute-done.2.far_ref = bf16[2,3,4,256]{3,2,1,0:T(4,128)(2,1)S(1)} collective-permute-done((bf16[2,3,4,256]{3,2,1,0:T(4,128)(2,1)S(1)}, bf16[2,3,4,256]{3,2,1,0:T(4,128)(2,1)S(1)}, u32[]{:S(2)}, u32[]{:S(2)}) %collective-permute-start.2) | collective-permute-done | bytes 12320 | tf_op jit(solution)/shard_map/ppermute | solution.py:343
  58.0 3.3 %features.1 = f32[3,4,256]{2,1,0:T(4,128)} custom-call(s32[1]{0:T(128)} %bitcast.row_ref, bf16[2,3,4,256]{3,2,1,0:T(4,128)(2,1)S(1)} %collective-permute-done.previous_ref, bf16[2,3,4,256]{3,2,1,0:T(4,128)(2,1)S(1)} %constant_dynamic-update-slice_fusion.image_ref, bf16[2,3,4,256]{3,2,1,0:T(4,128)(2,1)S(1)} %collective-permute-done.1.next_ref, ...), custom_call_target="tpu_custom_call" | custom-call | flops 1000000000 | bytes 1000000 | tf_op jit(solution)/shard_map/features/pallas_call | solution.py:300
  61.2 0.0 all-to-all-done.1
  61.3 0.1 fusion.2
  61.3 0.6 fusion.1
  61.9 0.6 copy.14
  (15 shorter events, 0.2 us)
Async XLA Ops:
  0.6 0.7 %copy-start.4 = (bf16[1,3,4,256]{3,2,1,0:T(4,128)(2,1)S(1)}, bf16[1,3,4,256]{3,2,1,0:T(4,128)(2,1)}, u32[]{:S(2)}) copy-start(bf16[1,3,4,256]{3,2,1,0:T(4,128)(2,1)} %param.8) | copy-start | bytes 18436
  1.4 13.9 %collective-permute-start = (bf16[2,3,4,256]{3,2,1,0:T(4,128)(2,1)S(1)}, bf16[2,3,4,256]{3,2,1,0:T(4,128)(2,1)S(1)}, u32[]{:S(2)}, u32[]{:S(2)}) collective-permute-start(bf16[2,3,4,256]{3,2,1,0:T(4,128)(2,1)S(1)} %constant_dynamic-update-slice_fusion.image_ref), channel_id=1, source_target_pairs={{0,1},{1,2},{2,3},{3,4},{4,5},{5,6},{6,7},{7,8},{8,9},{9,10},{10,1... | collective-permute-start | bytes 36872 | tf_op jit(solution)/shard_map/ppermute | solution.py:333
  3.3 12.0 %collective-permute-start.1 = (bf16[2,3,4,256]{3,2,1,0:T(4,128)(2,1)S(1)}, bf16[2,3,4,256]{3,2,1,0:T(4,128)(2,1)S(1)}, u32[]{:S(2)}, u32[]{:S(2)}) collective-permute-start(bf16[2,3,4,256]{3,2,1,0:T(4,128)(2,1)S(1)} %constant_dynamic-update-slice_fusion.image_ref), channel_id=1, source_target_pairs={{1,0},{2,1},{3,2},{4,3},{5,4},{6,5},{7,6},{8,7},{9,8},{10,9},{11,1... | collective-permute-start | bytes 36872 | tf_op jit(solution)/shard_map/ppermute | solution.py:334
  4.6 0.7 %copy-start = (bf16[64,3,4,4]{0,3,2,1:T(4,128)(2,1)S(1)}, bf16[64,3,4,4]{0,3,2,1:T(4,128)(2,1)}, u32[]{:S(2)}) copy-start(bf16[64,3,4,4]{0,3,2,1:T(4,128)(2,1)} %param.12) | copy-start | bytes 18436
  4.6 0.7 %copy-start.1 = (f32[64]{0:T(128)S(1)}, f32[64]{0:T(128)}, u32[]{:S(2)}) copy-start(f32[64]{0:T(128)} %param.13) | copy-start | bytes 772
  4.6 1.0 %copy-start.3 = (bf16[64,3,3,3]{0,3,2,1:T(4,128)(2,1)S(1)}, bf16[64,3,3,3]{0,3,2,1:T(4,128)(2,1)}, u32[]{:S(2)}) copy-start(bf16[64,3,3,3]{0,3,2,1:T(4,128)(2,1)} %param.9) | copy-start | bytes 10372
  32.0 24.6 %copy-start.2 = (bf16[64,64,3,3]{1,0,3,2:T(8,128)(2,1)S(1)}, bf16[64,64,3,3]{1,0,3,2:T(8,128)(2,1)}, u32[]{:S(2)}) copy-start(bf16[64,64,3,3]{1,0,3,2:T(8,128)(2,1)} %param.10) | copy-start | bytes 221188
  32.0 29.2 %all-to-all-start.1 = ((f16[16,32,128]{2,1,0:T(8,128)(2,1)}), f16[16,32,128]{2,1,0:T(8,128)(2,1)S(1)}, u32[]{:S(2)}, u32[]{:S(2)}) async-start(f16[16,32,128]{2,1,0:T(8,128)(2,1)} %broadcast_in_dim.29), calls=%async_computation.1 | async-start | bytes 262144 | tf_op jit(solution)/shard_map/all_to_all | solution.py:326
  45.9 10.7 %copy-start.5 = (f32[64]{0:T(128)S(1)}, f32[64]{0:T(128)}, u32[]{:S(2)}) copy-start(f32[64]{0:T(128)} %param.11) | copy-start | bytes 772
  45.9 12.0 %collective-permute-start.2 = (bf16[2,3,4,256]{3,2,1,0:T(4,128)(2,1)S(1)}, bf16[2,3,4,256]{3,2,1,0:T(4,128)(2,1)S(1)}, u32[]{:S(2)}, u32[]{:S(2)}) collective-permute-start(bf16[2,3,4,256]{3,2,1,0:T(4,128)(2,1)S(1)} %constant_dynamic-update-slice_fusion.image_ref), channel_id=1, source_target_pairs={{16,15},{32,31},{48,47},{80,79},{96,95},{112,111},{144,143},{160,1... | collective-permute-start | bytes 36872 | tf_op jit(solution)/shard_map/ppermute | solution.py:343

commit v3 on v2

--- a/solution.py
+++ b/solution.py
@@ -14,6 +14,8 @@
 DP = ("zh", "y")
 PLANE = ("y", "x", "c")
 COLUMN = ("zh", "zl")
+PLANE_ORDER = [4] + [peer for peer in range(32) if peer != 4]
+COLUMN_ORDER = list(range(8, 16)) + list(range(8))
 F32 = jnp.float32
 BF16 = jnp.bfloat16
 VMEM = pl.BlockSpec(memory_space=pltpu.VMEM)
@@ -47,8 +49,9 @@
 
 
 def place_rows(previous_ref, image_ref, next_ref, image, channel):
-    parts = [ref[image, channel].astype(F32) for ref in (previous_ref, image_ref, next_ref)]
-    return jnp.concatenate(parts + [jnp.zeros_like(parts[0])], axis=0)
+    refs = (previous_ref, image_ref) if next_ref is None else (previous_ref, image_ref, next_ref)
+    parts = [ref[image, channel].astype(F32) for ref in refs]
+    return jnp.concatenate(parts + [jnp.zeros((16 - 4 * len(parts), 256), F32)], axis=0)
 
 
 def expand(weight, width, first_row):
@@ -130,13 +133,12 @@
     )
 
 
-def critic_kernel(row_ref, previous_ref, image_ref, next_ref, spread_ref, weight_ref, head_ref, sums_ref):
+def critic_kernel(row_ref, previous_ref, image_ref, spread_ref, weight_ref, head_ref, sums_ref):
     index = row_ref[0] // 4
-    takes = (((index & 15) == 0) & (index > 0)).astype(F32)
-    keeps = 1.0 - (((index & 15) == 15) & (index < 63)).astype(F32)
+    shares = ((index > 0).astype(F32), 1.0, (index == 63).astype(F32))
     image = jnp.concatenate(
         [
-            place_rows(previous_ref, image_ref, next_ref, image, channel)
+            place_rows(previous_ref, image_ref, None, image, channel)
             for image in range(2)
             for channel in range(3)
         ],
@@ -153,7 +155,7 @@
     lane = iota((1, 256), 1)
     signals = []
     total = None
-    for patch, share in enumerate((takes, 1.0, keeps)):
+    for patch, share in enumerate(shares):
         part = hidden[64 * patch : 64 * patch + 64]
         logit = jnp.sum(head * part, axis=0, keepdims=True)
         sign = jnp.where(
@@ -180,7 +182,7 @@
     return pl.pallas_call(
         critic_kernel,
         out_shape=jax.ShapeDtypeStruct((32, 128), F32),
-        in_specs=[SMEM] + [VMEM] * 6,
+        in_specs=[SMEM] + [VMEM] * 5,
         out_specs=VMEM,
         compiler_params=SMALL,
         name="critic",
@@ -201,25 +203,22 @@
     return parts[0] if len(parts) == 1 else jnp.concatenate(parts, axis=1)
 
 
-def feature_kernel(row_ref, previous_ref, image_ref, next_ref, far_ref, lpips_ref, spread_ref, critic_fwd_ref,
+def feature_kernel(row_ref, previous_ref, image_ref, next_ref, lpips_ref, spread_ref, critic_fwd_ref,
                    head_ref, critic_bwd_ref, first_fwd_ref, first_bwd_ref, second_fwd_ref, second_bwd_ref, out_ref,
-                   below_ref, slope_ref, pre_ref, act_ref):
+                   slope_ref, pre_ref, act_ref):
     first_row = row_ref[0]
-    index = first_row // 4
-    distant = (index & 15) == 15
 
     def valid(row):
         return ((first_row + row >= 0) & (first_row + row < 256)).astype(F32)
 
     line = iota((16, 256), 0) + (first_row - 4)
     inside = ((line >= 0) & (line < 256)).astype(F32)
-    below_ref[...] = jnp.where(distant, far_ref[...].astype(F32), next_ref[...].astype(F32))
     images = []
     fake = []
     for image in range(2):
         parts = []
         for channel in range(3):
-            here = place_rows(previous_ref, image_ref, below_ref, image, channel)
+            here = place_rows(previous_ref, image_ref, next_ref, image, channel)
             if image == 0:
                 fake.append(here)
             parts.append((here - LPIPS_SHIFT[channel]) / LPIPS_SCALE[channel] * inside)
@@ -300,18 +299,42 @@
     return pl.pallas_call(
         feature_kernel,
         out_shape=jax.ShapeDtypeStruct((3, 4, 256), F32),
-        in_specs=[SMEM] + [VMEM] * 13,
+        in_specs=[SMEM] + [VMEM] * 12,
         out_specs=VMEM,
         scratch_shapes=[
-            pltpu.VMEM((2, 3, 4, 256), F32),
             pltpu.VMEM((384, 256), F32),
             pltpu.VMEM((640, 512), F32),
             pltpu.VMEM((512, 512), F32),
         ],
         compiler_params=pltpu.CompilerParams(vmem_limit_bytes=16 * 1024 * 1024),
-        cost_estimate=pl.CostEstimate(flops=1_000_000_000, bytes_accessed=1_000_000, transcendentals=1_000_000),
+        cost_estimate=pl.CostEstimate(flops=20_000_000_000, bytes_accessed=1_000_000, transcendentals=1_000_000),
         name="features",
     )(*operands)
+
+
+def finish_kernel(total_ref, conv_ref, head_ref):
+    patches = 8 * 128 * 128
+    total = total_ref[...]
+    scaled = total[:24] * (32.0 / 128.0 / patches)
+    halves = (scaled, pltpu.roll(scaled, 64, 1))
+    for col_tap in range(4):
+        for channel in range(3):
+            start = 12 * (col_tap % 2) + 4 * channel
+            rows = halves[col_tap // 2][start : start + 4, :64]
+            for row_tap in range(4):
+                conv_ref[channel, row_tap, col_tap : col_tap + 1, :] = rows[row_tap : row_tap + 1]
+    head_ref[...] = total[24:25, :64] * (32.0 / patches)
+
+
+def finish(total):
+    return pl.pallas_call(
+        finish_kernel,
+        out_shape=[jax.ShapeDtypeStruct((3, 4, 4, 64), F32), jax.ShapeDtypeStruct((1, 64), F32)],
+        in_specs=[VMEM],
+        out_specs=[VMEM] * 2,
+        compiler_params=SMALL,
+        name="finish",
+    )(total)
 
 
 def weight_rows(weight):
@@ -320,10 +343,11 @@
     return jnp.pad(moved, ((0, 0), (0, 4 - taps), (0, 4 - taps), (0, 0))).reshape(48, 64)
 
 
-def exchange_sum(value, axes):
+def exchange_sum(value, axes, order=None):
     peers = lax.axis_size(axes)
     copies = jnp.broadcast_to(value[None], (peers,) + value.shape)
-    return jnp.sum(lax.all_to_all(copies, axes, 0, 0).astype(F32), axis=0)
+    groups = None if order is None else [order]
+    return jnp.sum(lax.all_to_all(copies, axes, 0, 0, axis_index_groups=groups).astype(F32), axis=0)
 
 
 def shards(fake, real, vgg_first, vgg_second, lpips_weights, critic_conv, critic_head):
@@ -331,25 +355,21 @@
     first_row = (lax.axis_index(ROWS) * 4).astype(jnp.int32)[None]
     images = jnp.concatenate([fake, real], axis=0)
     previous = lax.ppermute(images, ROWS, [(k, k + 1) for k in range(count - 1)])
-    following = lax.ppermute(images, ROWS, [(k + 1, k) for k in range(count - 1) if k % 16 < 15])
+    following = lax.ppermute(images, ROWS, [(k + 1, k) for k in range(count - 1)])
     critic_rows = weight_rows(critic_conv)
     spread, critic_fwd, head = critic_weights(critic_rows, critic_head[None])
-    sums = critic(first_row, previous, images, following, spread, critic_fwd, head)
-    sums, later, first, second, again = lax.optimization_barrier(
-        (sums, images, weight_rows(vgg_first), jnp.transpose(vgg_second, (2, 3, 0, 1)), critic_rows)
+    sums = critic(first_row, previous, images, spread, critic_fwd, head)
+    sums, first, second, again = lax.optimization_barrier(
+        (sums, weight_rows(vgg_first), jnp.transpose(vgg_second, (2, 3, 0, 1)), critic_rows)
     )
     weights = feature_weights(first, second, again)
-    plane = exchange_sum(sums.astype(jnp.float16), PLANE)
-    far = lax.ppermute(later, ROWS, [(k + 1, k) for k in range(count - 1) if k % 16 == 15])
-    total = exchange_sum((plane * (1.0 / 32.0)).astype(jnp.float16), COLUMN)
+    plane = exchange_sum(sums.astype(jnp.float16), PLANE, PLANE_ORDER)
+    total = exchange_sum((plane * (1.0 / 32.0)).astype(jnp.float16), COLUMN, COLUMN_ORDER)
     grad_image = features(
-        first_row, previous, images, following, far, lpips_weights[:, None], spread, critic_fwd, head, *weights
-    )
-    patches = 8 * 128 * 128
-    conv = jnp.concatenate([total[:24, :64], total[:24, 64:]], axis=0) * (32.0 / 128.0 / patches)
-    conv_grad = jnp.transpose(conv.reshape(4, 3, 4, 64), (3, 1, 2, 0))
-    head_grad = (total[24, :64] + total[24, 64:]) * (32.0 / patches)
-    return grad_image[None], conv_grad, head_grad
+        first_row, previous, images, following, lpips_weights[:, None], spread, critic_fwd, head, *weights
+    )
+    conv_grad, head_grad = finish(total)
+    return grad_image[None], jnp.transpose(conv_grad, (3, 0, 1, 2)), head_grad[0]
 
 
 def solution(mesh):

time: 63 us -> 56.8 us (0.902)
  the two profiles are of different devices: /device:TPU:2 before, /device:TPU:1 now
where the time goes in v3:
time: 56.8 us; the launch traced here: 56.3 us
  starting transfers between devices  37.3 us (66%)
  waiting for transfers between devices  9.72 us (17%)
  Pallas kernels  5.45 us (10%)
  local copies, waits for them, and re-layouts  2.93 us (5%)
  between operations  0.76 us (1%)
    all_to_all x2, starting transfers between devices, exchange_sum(): lax.all_to_all(copies, axes, 0, 0, axis_index_groups=groups).astype(F32)  30.1 us
    all_to_all x2, waiting for transfers between devices, exchange_sum(): lax.all_to_all(copies, axes, 0, 0, axis_index_groups=groups).astype(F32)  6.86 us
    ppermute x1, starting transfers between devices, shards(): lax.ppermute(images, ROWS, [(k, k + 1) for k in range(count - 1)])  4.93 us
    pallas_call x1, Pallas kernels, features(): pl.pallas_call(feature_kernel, out_shape=jax.ShapeDtypeStruct((3, 4, 256)...  3.28 us
    ppermute x1, waiting for transfers between devices, shards(): lax.ppermute(images, ROWS, [(k, k + 1) for k in range(count - 1)])  2.86 us
    ppermute x1, starting transfers between devices, shards(): lax.ppermute(images, ROWS, [(k + 1, k) for k in range(count - 1)])  2.27 us
    broadcast_in_dim x2, local copies, waits for them, and re-layouts, exchange_sum(): copies = jnp.broadcast_to(value[None], (peers,) + value.shape)  1.41 us
    unnamed x13, local copies, waits for them, and re-layouts  1.4 us
  transfers between devices with their start and end apart: 4, of which 3 were waited for; matrix products, arithmetic and copies ran while one was open for 1% of the time, Pallas kernels for 7%

profile of v3, /device:TPU:1, one launch (start us, length us, event | category | flops | bytes accessed | tf_op | source)
XLA Modules:
  0.0 56.3 jit_solution(18253016677220081511)
XLA Ops:
  0.6 0.0 copy-start.4
  0.6 0.7 %constant_dynamic-update-slice_fusion.1 = bf16[2,3,4,256]{3,2,1,0:T(4,128)(2,1)S(1)} fusion(bf16[1,3,4,256]{3,2,1,0:T(4,128)(2,1)} %param.7), kind=kLoop, calls=%fused_computation.4 | loop fusion | bytes 12288
  1.4 4.9 %collective-permute-start = (bf16[2,3,4,256]{3,2,1,0:T(4,128)(2,1)S(1)}, bf16[2,3,4,256]{3,2,1,0:T(4,128)(2,1)S(1)}, u32[]{:S(2)}, u32[]{:S(2)}) collective-permute-start(bf16[2,3,4,256]{3,2,1,0:T(4,128)(2,1)S(1)} %constant_dynamic-update-slice_fusion.image_ref), channel_id=1, source_target_pairs={{0,1},{1,2},{2,3},{3,4},{4,5},{5,6},{6,7},{7,8},{8,9},{9,10},{10,1... | collective-permute-start | bytes 36872 | tf_op jit(solution)/shard_map/ppermute | solution.py:357
  6.3 0.0 copy-start
  6.3 0.0 copy-start.1
  6.3 0.0 copy-start.3
  6.3 0.7 %copy-done = bf16[64,3,4,4]{0,3,2,1:T(4,128)(2,1)S(1)} copy-done((bf16[64,3,4,4]{0,3,2,1:T(4,128)(2,1)S(1)}, bf16[64,3,4,4]{0,3,2,1:T(4,128)(2,1)}, u32[]{:S(2)}) %copy-start) | copy-done | bytes 6168
  7.0 0.0 copy-done.1
  7.0 0.3 critic_weights.1
  7.3 2.9 %collective-permute-done.previous_ref = bf16[2,3,4,256]{3,2,1,0:T(4,128)(2,1)S(1)} collective-permute-done((bf16[2,3,4,256]{3,2,1,0:T(4,128)(2,1)S(1)}, bf16[2,3,4,256]{3,2,1,0:T(4,128)(2,1)S(1)}, u32[]{:S(2)}, u32[]{:S(2)}) %collective-permute-start) | collective-permute-done | bytes 12320 | tf_op jit(solution)/shard_map/ppermute | solution.py:357
  10.2 0.8 %critic.1 = f32[32,128]{1,0:T(8,128)S(1)} custom-call(s32[1]{0:T(128)} %bitcast.row_ref, bf16[2,3,4,256]{3,2,1,0:T(4,128)(2,1)S(1)} %collective-permute-done.previous_ref, bf16[2,3,4,256]{3,2,1,0:T(4,128)(2,1)S(1)} %constant_dynamic-update-slice_fusion.image_ref, bf16[256,512]{1,0:T(8,128)(2,1)S(1)} %get-tuple-element.17.spread_ref, ...), custom_call_target="tpu_custom_call" | custom-call | tf_op jit(solution)/shard_map/critic/pallas_call | solution.py:182
  11.0 0.7 %broadcast_in_dim.28 = f16[32,32,128]{2,1,0:T(8,128)(2,1)} broadcast(f16[32,128]{1,0:T(8,128)(2,1)S(1)} %convert_element_type.18), dimensions={1,2} | broadcast | bytes 270336 | tf_op jit(solution)/shard_map/broadcast_in_dim | solution.py:348
  11.7 15.0 %all-to-all-start = ((f16[32,32,128]{2,1,0:T(8,128)(2,1)}), f16[32,32,128]{2,1,0:T(8,128)(2,1)S(1)}, u32[]{:S(2)}, u32[]{:S(2)}) async-start(f16[32,32,128]{2,1,0:T(8,128)(2,1)} %broadcast_in_dim.28), calls=%async_computation | async-start | bytes 524288 | tf_op jit(solution)/shard_map/all_to_all | solution.py:350
  26.7 0.0 copy-start.5
  26.7 2.3 %collective-permute-start.1 = (bf16[2,3,4,256]{3,2,1,0:T(4,128)(2,1)S(1)}, bf16[2,3,4,256]{3,2,1,0:T(4,128)(2,1)S(1)}, u32[]{:S(2)}, u32[]{:S(2)}) collective-permute-start(bf16[2,3,4,256]{3,2,1,0:T(4,128)(2,1)S(1)} %constant_dynamic-update-slice_fusion.image_ref), channel_id=1, source_target_pairs={{1,0},{2,1},{3,2},{4,3},{5,4},{6,5},{7,6},{8,7},{9,8},{10,9},{11,1... | collective-permute-start | bytes 36872 | tf_op jit(solution)/shard_map/ppermute | solution.py:358
  29.0 0.1 copy.11.lpips_ref
  29.1 0.4 feature_weights.1
  29.5 3.4 %all-to-all-done = f16[32,32,128]{2,1,0:T(8,128)(2,1)S(1)} async-done(((f16[32,32,128]{2,1,0:T(8,128)(2,1)}), f16[32,32,128]{2,1,0:T(8,128)(2,1)S(1)}, u32[]{:S(2)}, u32[]{:S(2)}) %all-to-all-start) | async-done | bytes 262176 | tf_op jit(solution)/shard_map/all_to_all | solution.py:350
  33.0 0.7 %broadcast_in_dim.29 = f16[16,32,128]{2,1,0:T(8,128)(2,1)} broadcast(f16[32,128]{1,0:T(8,128)(2,1)S(1)} %multiply_convert_fusion), dimensions={1,2} | broadcast | bytes 139264 | tf_op jit(solution)/shard_map/broadcast_in_dim | solution.py:348
  33.7 15.2 %all-to-all-start.1 = ((f16[16,32,128]{2,1,0:T(8,128)(2,1)}), f16[16,32,128]{2,1,0:T(8,128)(2,1)S(1)}, u32[]{:S(2)}, u32[]{:S(2)}) async-start(f16[16,32,128]{2,1,0:T(8,128)(2,1)} %broadcast_in_dim.29), calls=%async_computation.1 | async-start | bytes 262144 | tf_op jit(solution)/shard_map/all_to_all | solution.py:350
  48.8 0.0 collective-permute-done.1.next_ref
  48.9 3.3 %features.1 = f32[3,4,256]{2,1,0:T(4,128)} custom-call(s32[1]{0:T(128)} %bitcast.row_ref, bf16[2,3,4,256]{3,2,1,0:T(4,128)(2,1)S(1)} %collective-permute-done.previous_ref, bf16[2,3,4,256]{3,2,1,0:T(4,128)(2,1)S(1)} %constant_dynamic-update-slice_fusion.image_ref, bf16[2,3,4,256]{3,2,1,0:T(4,128)(2,1)S(1)} %collective-permute-done.1.next_ref, ...), custom_call_target="tpu_custom_call" | custom-call | flops 20000000000 | bytes 1000000 | tf_op jit(solution)/shard_map/features/pallas_call | solution.py:299
  52.1 3.4 %all-to-all-done.1 = f16[16,32,128]{2,1,0:T(8,128)(2,1)S(1)} async-done(((f16[16,32,128]{2,1,0:T(8,128)(2,1)}), f16[16,32,128]{2,1,0:T(8,128)(2,1)S(1)}, u32[]{:S(2)}, u32[]{:S(2)}) %all-to-all-start.1) | async-done | bytes 131104 | tf_op jit(solution)/shard_map/all_to_all | solution.py:350
  55.6 0.7 %finish.1 = (f32[3,4,4,64]{3,2,1,0:T(4,128)}, f32[1,64]{1,0:T(1,128)}) custom-call(f32[32,128]{1,0:T(8,128)S(1)} %convert_reduce_fusion.1.total_ref), custom_call_target="tpu_custom_call" | custom-call | tf_op jit(solution)/shard_map/finish/pallas_call | solution.py:330
  (11 shorter events, 0.1 us)
Async XLA Ops:
  0.6 0.7 %copy-start.4 = (bf16[1,3,4,256]{3,2,1,0:T(4,128)(2,1)S(1)}, bf16[1,3,4,256]{3,2,1,0:T(4,128)(2,1)}, u32[]{:S(2)}) copy-start(bf16[1,3,4,256]{3,2,1,0:T(4,128)(2,1)} %param.8) | copy-start | bytes 18436
  1.4 8.8 %collective-permute-start = (bf16[2,3,4,256]{3,2,1,0:T(4,128)(2,1)S(1)}, bf16[2,3,4,256]{3,2,1,0:T(4,128)(2,1)S(1)}, u32[]{:S(2)}, u32[]{:S(2)}) collective-permute-start(bf16[2,3,4,256]{3,2,1,0:T(4,128)(2,1)S(1)} %constant_dynamic-update-slice_fusion.image_ref), channel_id=1, source_target_pairs={{0,1},{1,2},{2,3},{3,4},{4,5},{5,6},{6,7},{7,8},{8,9},{9,10},{10,1... | collective-permute-start | bytes 36872 | tf_op jit(solution)/shard_map/ppermute | solution.py:357
  6.3 0.7 %copy-start = (bf16[64,3,4,4]{0,3,2,1:T(4,128)(2,1)S(1)}, bf16[64,3,4,4]{0,3,2,1:T(4,128)(2,1)}, u32[]{:S(2)}) copy-start(bf16[64,3,4,4]{0,3,2,1:T(4,128)(2,1)} %param.12) | copy-start | bytes 18436
  6.3 0.7 %copy-start.1 = (f32[64]{0:T(128)S(1)}, f32[64]{0:T(128)}, u32[]{:S(2)}) copy-start(f32[64]{0:T(128)} %param.13) | copy-start | bytes 772
  6.3 1.0 %copy-start.3 = (bf16[64,3,3,3]{0,3,2,1:T(4,128)(2,1)S(1)}, bf16[64,3,3,3]{0,3,2,1:T(4,128)(2,1)}, u32[]{:S(2)}) copy-start(bf16[64,3,3,3]{0,3,2,1:T(4,128)(2,1)} %param.9) | copy-start | bytes 10372
  11.7 17.4 %copy-start.2 = (bf16[64,64,3,3]{1,0,3,2:T(8,128)(2,1)S(1)}, bf16[64,64,3,3]{1,0,3,2:T(8,128)(2,1)}, u32[]{:S(2)}) copy-start(bf16[64,64,3,3]{1,0,3,2:T(8,128)(2,1)} %param.10) | copy-start | bytes 221188
  11.7 21.2 %all-to-all-start = ((f16[32,32,128]{2,1,0:T(8,128)(2,1)}), f16[32,32,128]{2,1,0:T(8,128)(2,1)S(1)}, u32[]{:S(2)}, u32[]{:S(2)}) async-start(f16[32,32,128]{2,1,0:T(8,128)(2,1)} %broadcast_in_dim.28), calls=%async_computation | async-start | bytes 524288 | tf_op jit(solution)/shard_map/all_to_all | solution.py:350
  26.7 2.3 %copy-start.5 = (f32[64]{0:T(128)S(1)}, f32[64]{0:T(128)}, u32[]{:S(2)}) copy-start(f32[64]{0:T(128)} %param.11) | copy-start | bytes 772
  26.7 22.1 %collective-permute-start.1 = (bf16[2,3,4,256]{3,2,1,0:T(4,128)(2,1)S(1)}, bf16[2,3,4,256]{3,2,1,0:T(4,128)(2,1)S(1)}, u32[]{:S(2)}, u32[]{:S(2)}) collective-permute-start(bf16[2,3,4,256]{3,2,1,0:T(4,128)(2,1)S(1)} %constant_dynamic-update-slice_fusion.image_ref), channel_id=1, source_target_pairs={{1,0},{2,1},{3,2},{4,3},{5,4},{6,5},{7,6},{8,7},{9,8},{10,9},{11,1... | collective-permute-start | bytes 36872 | tf_op jit(solution)/shard_map/ppermute | solution.py:358
  33.7 21.9 %all-to-all-start.1 = ((f16[16,32,128]{2,1,0:T(8,128)(2,1)}), f16[16,32,128]{2,1,0:T(8,128)(2,1)S(1)}, u32[]{:S(2)}, u32[]{:S(2)}) async-start(f16[16,32,128]{2,1,0:T(8,128)(2,1)} %broadcast_in_dim.29), calls=%async_computation.1 | async-start | bytes 262144 | tf_op jit(solution)/shard_map/all_to_all | solution.py:350

commit v4 on v3

--- a/solution.py
+++ b/solution.py
@@ -14,7 +14,8 @@
 DP = ("zh", "y")
 PLANE = ("y", "x", "c")
 COLUMN = ("zh", "zl")
-PLANE_ORDER = [4] + [peer for peer in range(32) if peer != 4]
+MIDDLE = 9
+PLANE_ORDER = [5] + [peer for peer in range(32) if peer != 5]
 COLUMN_ORDER = list(range(8, 16)) + list(range(8))
 F32 = jnp.float32
 BF16 = jnp.bfloat16
@@ -46,12 +47,6 @@
     tap = (k >= 48).astype(jnp.int32) + (k >= 96).astype(jnp.int32) + (k >= 144).astype(jnp.int32)
     rest = k - 48 * tap
     return tap, rest >> 4, rest & 15
-
-
-def place_rows(previous_ref, image_ref, next_ref, image, channel):
-    refs = (previous_ref, image_ref) if next_ref is None else (previous_ref, image_ref, next_ref)
-    parts = [ref[image, channel].astype(F32) for ref in refs]
-    return jnp.concatenate(parts + [jnp.zeros((16 - 4 * len(parts), 256), F32)], axis=0)
 
 
 def expand(weight, width, first_row):
@@ -133,56 +128,66 @@
     )
 
 
-def critic_kernel(row_ref, previous_ref, image_ref, spread_ref, weight_ref, head_ref, sums_ref):
+def critic_kernel(row_ref, under_ref, upper_ref, previous_ref, image_ref, spread_ref, weight_ref, head_ref, sums_ref):
     index = row_ref[0] // 4
-    shares = ((index > 0).astype(F32), 1.0, (index == 63).astype(F32))
-    image = jnp.concatenate(
-        [
-            place_rows(previous_ref, image_ref, None, image, channel)
-            for image in range(2)
-            for channel in range(3)
-        ],
-        axis=0,
-    ).astype(BF16)
-    taps = dot(image, spread_ref[...]).astype(BF16)
-    windows = jnp.concatenate([stack_taps(taps, 0), stack_taps(taps, 1)], axis=1)
-    pre = dot(weight_ref[0:192, :], windows)
+    last = index == 63
+    between = ((index & 15) == MIDDLE) & (index > 15)
+    near = (index & 15) != 0
+    shares = (
+        (near.astype(F32), (between | last).astype(F32)),
+        ((near | (index == 0)).astype(F32), between.astype(F32)),
+    )
+    blank = jnp.zeros((8, 256), F32)
+    rows = []
+    for image in range(2):
+        for channel in range(3):
+            rows += [previous_ref[image, channel].astype(F32), image_ref[image, channel].astype(F32), blank]
+    for image in range(2):
+        for channel in range(3):
+            upper = jnp.where(last, image_ref[image, channel].astype(F32), upper_ref[image, channel])
+            rows += [upper, under_ref[image, channel], blank]
+    taps = dot(jnp.concatenate(rows, axis=0).astype(BF16), spread_ref[...]).astype(BF16)
+    windows = jnp.concatenate([stack_taps(taps, place) for place in range(4)], axis=1)
+    pre = dot(weight_ref[0:128, :], windows)
     head = head_ref[...]
     square = pre * pre + SOFTNESS
     inverse = lax.rsqrt(square)
     hidden = 0.6 * pre + 0.4 * (square * inverse)
     slope = 0.6 + 0.4 * (pre * inverse)
-    lane = iota((1, 256), 1)
+    lane = iota((1, 512), 1)
     signals = []
     total = None
-    for patch, share in enumerate(shares):
+    for patch in range(2):
         part = hidden[64 * patch : 64 * patch + 64]
         logit = jnp.sum(head * part, axis=0, keepdims=True)
         sign = jnp.where(
-            lane < 128, jnp.where(logit > -1.0, 1.0, 0.0), jnp.where(logit < 1.0, -1.0, 0.0)
-        ) * share
-        signals.append(slope[64 * patch : 64 * patch + 64] * head * sign)
+            (lane & 128) == 0, jnp.where(logit > -1.0, 1.0, 0.0), jnp.where(logit < 1.0, -1.0, 0.0)
+        ) * jnp.where(lane < 256, shares[patch][0], shares[patch][1])
+        signals.append(slope[64 * patch : 64 * patch + 64] * (head * sign))
         total = part * sign if total is None else total + part * sign
     high, low = split(jnp.concatenate(signals + [total], axis=0))
-    windows = jnp.concatenate([windows, jnp.ones((16, 256), BF16)], axis=0)
+    windows = jnp.concatenate([windows, jnp.ones((16, 512), BF16)], axis=0)
     grads = lax.dot_general(windows, high, NT, preferred_element_type=F32) + lax.dot_general(
         windows, low, NT, preferred_element_type=F32
     )
     rows = []
     for block in range(12):
         here = grads[16 * block : 16 * block + 16]
-        rows.append(here[1:5, :64] + here[3:7, 64:128] + here[5:9, 128:192])
-    sums_ref[0:24, :] = 128.0 * jnp.concatenate(
+        rows.append(here[1:5, :64] + here[3:7, 64:128])
+    packed = 128.0 * jnp.concatenate(
         [jnp.concatenate(rows[:6], axis=0), jnp.concatenate(rows[6:], axis=0)], axis=1
     )
-    sums_ref[24:32, :] = jnp.concatenate([grads[192:200, 192:256], jnp.zeros((8, 64), F32)], axis=1)
+    for row in range(24):
+        sums_ref[row // 12 : row // 12 + 1, 128 * (row % 12) : 128 * (row % 12) + 128] = packed[row : row + 1]
+    head_sum = jnp.concatenate([grads[192:194, 128:192], jnp.zeros((2, 64), F32)], axis=1)
+    sums_ref[:, 1536:1664] = head_sum
 
 
 def critic(*operands):
     return pl.pallas_call(
         critic_kernel,
-        out_shape=jax.ShapeDtypeStruct((32, 128), F32),
-        in_specs=[SMEM] + [VMEM] * 5,
+        out_shape=jax.ShapeDtypeStruct((2, 1664), F32),
+        in_specs=[SMEM] + [VMEM] * 7,
         out_specs=VMEM,
         compiler_params=SMALL,
         name="critic",
@@ -203,10 +208,11 @@
     return parts[0] if len(parts) == 1 else jnp.concatenate(parts, axis=1)
 
 
-def feature_kernel(row_ref, previous_ref, image_ref, next_ref, lpips_ref, spread_ref, critic_fwd_ref,
-                   head_ref, critic_bwd_ref, first_fwd_ref, first_bwd_ref, second_fwd_ref, second_bwd_ref, out_ref,
-                   slope_ref, pre_ref, act_ref):
+def feature_kernel(row_ref, critic_bwd_ref, first_fwd_ref, first_bwd_ref, second_fwd_ref, second_bwd_ref,
+                   previous_ref, image_ref, next_ref, far_ref, lpips_ref, spread_ref, critic_fwd_ref, head_ref,
+                   out_ref, slope_ref, pre_ref, act_ref):
     first_row = row_ref[0]
+    place = first_row // 4 & 15
 
     def valid(row):
         return ((first_row + row >= 0) & (first_row + row < 256)).astype(F32)
@@ -218,7 +224,12 @@
     for image in range(2):
         parts = []
         for channel in range(3):
-            here = place_rows(previous_ref, image_ref, next_ref, image, channel)
+            far = far_ref[image, channel]
+            above = jnp.where(place == 0, far, previous_ref[image, channel].astype(F32))
+            below = jnp.where(place == 15, far, next_ref[image, channel].astype(F32))
+            here = jnp.concatenate(
+                [above, image_ref[image, channel].astype(F32), below, jnp.zeros_like(far)], axis=0
+            )
             if image == 0:
                 fake.append(here)
             parts.append((here - LPIPS_SHIFT[channel]) / LPIPS_SCALE[channel] * inside)
@@ -299,7 +310,7 @@
     return pl.pallas_call(
         feature_kernel,
         out_shape=jax.ShapeDtypeStruct((3, 4, 256), F32),
-        in_specs=[SMEM] + [VMEM] * 12,
+        in_specs=[SMEM] + [VMEM] * 13,
         out_specs=VMEM,
         scratch_shapes=[
             pltpu.VMEM((384, 256), F32),
@@ -314,16 +325,14 @@
 
 def finish_kernel(total_ref, conv_ref, head_ref):
     patches = 8 * 128 * 128
-    total = total_ref[...]
-    scaled = total[:24] * (32.0 / 128.0 / patches)
-    halves = (scaled, pltpu.roll(scaled, 64, 1))
-    for col_tap in range(4):
-        for channel in range(3):
-            start = 12 * (col_tap % 2) + 4 * channel
-            rows = halves[col_tap // 2][start : start + 4, :64]
-            for row_tap in range(4):
-                conv_ref[channel, row_tap, col_tap : col_tap + 1, :] = rows[row_tap : row_tap + 1]
-    head_ref[...] = total[24:25, :64] * (32.0 / patches)
+    for row in range(24):
+        here = total_ref[row // 12 : row // 12 + 1, 128 * (row % 12) : 128 * (row % 12) + 128]
+        here = here * (32.0 / 128.0 / patches)
+        channel, row_tap = row % 12 // 4, row % 4
+        for half in range(2):
+            col_tap = 2 * half + row // 12
+            conv_ref[channel, row_tap, col_tap : col_tap + 1, :] = here[:, 64 * half : 64 * half + 64]
+    head_ref[...] = total_ref[0:1, 1536:1600] * (32.0 / patches)
 
 
 def finish(total):
@@ -354,11 +363,16 @@
     count = lax.axis_size(ROWS)
     first_row = (lax.axis_index(ROWS) * 4).astype(jnp.int32)[None]
     images = jnp.concatenate([fake, real], axis=0)
-    previous = lax.ppermute(images, ROWS, [(k, k + 1) for k in range(count - 1)])
-    following = lax.ppermute(images, ROWS, [(k + 1, k) for k in range(count - 1)])
+    far_pairs = [(k, k + 1) for k in range(15, count - 1, 16)]
+    whole = images.astype(F32)
+    under = lax.ppermute(whole, ROWS, [(b, b + MIDDLE) for a, b in far_pairs])
+    upper = lax.ppermute(whole, ROWS, [(a, b + MIDDLE) for a, b in far_pairs])
     critic_rows = weight_rows(critic_conv)
     spread, critic_fwd, head = critic_weights(critic_rows, critic_head[None])
-    sums = critic(first_row, previous, images, spread, critic_fwd, head)
+    previous = lax.ppermute(images, ROWS, [(k, k + 1) for k in range(count - 1) if k % 16 < 15])
+    following = lax.ppermute(images, ROWS, [(k + 1, k) for k in range(count - 1) if k % 16 < 15])
+    far = lax.ppermute(whole, ROWS, far_pairs + [(b, a) for a, b in far_pairs])
+    sums = critic(first_row, under, upper, previous, images, spread, critic_fwd, head)
     sums, first, second, again = lax.optimization_barrier(
         (sums, weight_rows(vgg_first), jnp.transpose(vgg_second, (2, 3, 0, 1)), critic_rows)
     )
@@ -366,7 +380,7 @@
     plane = exchange_sum(sums.astype(jnp.float16), PLANE, PLANE_ORDER)
     total = exchange_sum((plane * (1.0 / 32.0)).astype(jnp.float16), COLUMN, COLUMN_ORDER)
     grad_image = features(
-        first_row, previous, images, following, lpips_weights[:, None], spread, critic_fwd, head, *weights
+        first_row, *weights, previous, images, following, far, lpips_weights[:, None], spread, critic_fwd, head
     )
     conv_grad, head_grad = finish(total)
     return grad_image[None], jnp.transpose(conv_grad, (3, 0, 1, 2)), head_grad[0]

time: 56.8 us -> 53.8 us (0.947)
  starting transfers between devices: 37.3 us -> 35.6 us
  waiting for transfers between devices: 9.72 us -> 8.03 us
    all_to_all x2, starting transfers between devices: 30.1 us -> 26.4 us  [exchange_sum(): lax.all_to_all(copies, axes, 0, 0, axis_index_groups=groups).astype(F32)]
    ppermute x2 -> x5, starting transfers between devices: 7.2 us -> 9.19 us  [the longest x1 4.94 us: shards(): lax.ppermute(images, ROWS, [(k, k + 1) for k in range(count - 1) if k % 1...]
    all_to_all x2, waiting for transfers between devices: 6.86 us -> 5.16 us  [exchange_sum(): lax.all_to_all(copies, axes, 0, 0, axis_index_groups=groups).astype(F32)]
    ppermute x2 -> x5, waiting for transfers between devices: 2.86 us -> 2.87 us  [the longest x1 2.86 us: shards(): lax.ppermute(images, ROWS, [(k, k + 1) for k in range(count - 1) if k % 1...]
  transfers between devices with their start and end apart: 4 -> 7, of which waited for: 3 -> 3; matrix products, arithmetic and copies ran while one was open for 1% -> 2% of each run, Pallas kernels for 7% -> 8%
where the time goes in v4:
time: 53.8 us; the launch traced here: 53.3 us
  starting transfers between devices  35.6 us (66%)
  waiting for transfers between devices  8.03 us (15%)
  Pallas kernels  5.7 us (11%)
  local copies, waits for them, and re-layouts  3.01 us (6%)
  between operations  0.8 us (1%)
    all_to_all x2, starting transfers between devices, exchange_sum(): lax.all_to_all(copies, axes, 0, 0, axis_index_groups=groups).astype(F32)  26.4 us
    all_to_all x2, waiting for transfers between devices, exchange_sum(): lax.all_to_all(copies, axes, 0, 0, axis_index_groups=groups).astype(F32)  5.16 us
    ppermute x1, starting transfers between devices, shards(): lax.ppermute(images, ROWS, [(k, k + 1) for k in range(count - 1) if k % 1...  4.94 us
    pallas_call x1, Pallas kernels, features(): pl.pallas_call(feature_kernel, out_shape=jax.ShapeDtypeStruct((3, 4, 256)...  3.32 us
    ppermute x1, waiting for transfers between devices, shards(): lax.ppermute(images, ROWS, [(k, k + 1) for k in range(count - 1) if k % 1...  2.86 us
    ppermute x1, starting transfers between devices, shards(): lax.ppermute(images, ROWS, [(k + 1, k) for k in range(count - 1) if k % 1...  2.27 us
    broadcast_in_dim x2, local copies, waits for them, and re-layouts, exchange_sum(): copies = jnp.broadcast_to(value[None], (peers,) + value.shape)  1.49 us
    unnamed x13, local copies, waits for them, and re-layouts  1.4 us
  transfers between devices with their start and end apart: 7, of which 3 were waited for; matrix products, arithmetic and copies ran while one was open for 2% of the time, Pallas kernels for 8%

profile of v4, /device:TPU:1, one launch (start us, length us, event | category | flops | bytes accessed | tf_op | source)
XLA Modules:
  0.0 53.3 jit_solution(6959367701574539132)
XLA Ops:
  0.6 0.7 %constant_dynamic-update-slice_fusion.1 = bf16[2,3,4,256]{3,2,1,0:T(4,128)(2,1)S(1)} fusion(bf16[1,3,4,256]{3,2,1,0:T(4,128)(2,1)} %param.7), kind=kLoop, calls=%fused_computation.4 | loop fusion | bytes 12288
  1.4 0.7 %collective-permute-start = (f32[2,3,4,256]{3,2,1,0:T(4,128)S(1)}, f32[2,3,4,256]{3,2,1,0:T(4,128)S(1)}, u32[]{:S(2)}, u32[]{:S(2)}) collective-permute-start(f32[2,3,4,256]{3,2,1,0:T(4,128)S(1)} %convert_element_type.21), channel_id=1, source_target_pairs={{16,25},{32,41},{48,57},{80,89},{96,105},{112,121},{144,153},{160,... | collective-permute-start | bytes 73736 | tf_op jit(solution)/shard_map/ppermute | solution.py:368
  2.0 0.7 %collective-permute-start.1 = (f32[2,3,4,256]{3,2,1,0:T(4,128)S(1)}, f32[2,3,4,256]{3,2,1,0:T(4,128)S(1)}, u32[]{:S(2)}, u32[]{:S(2)}) collective-permute-start(f32[2,3,4,256]{3,2,1,0:T(4,128)S(1)} %convert_element_type.21), channel_id=1, source_target_pairs={{15,25},{31,41},{47,57},{79,89},{95,105},{111,121},{143,153},{159,... | collective-permute-start | bytes 73736 | tf_op jit(solution)/shard_map/ppermute | solution.py:369
  2.7 4.9 %collective-permute-start.2 = (bf16[2,3,4,256]{3,2,1,0:T(4,128)(2,1)S(1)}, bf16[2,3,4,256]{3,2,1,0:T(4,128)(2,1)S(1)}, u32[]{:S(2)}, u32[]{:S(2)}) collective-permute-start(bf16[2,3,4,256]{3,2,1,0:T(4,128)(2,1)S(1)} %constant_dynamic-update-slice_fusion.image_ref), channel_id=1, source_target_pairs={{0,1},{1,2},{2,3},{3,4},{4,5},{5,6},{6,7},{7,8},{8,9},{9,10},{10,1... | collective-permute-start | bytes 36872 | tf_op jit(solution)/shard_map/ppermute | solution.py:372
  7.7 0.0 copy-start
  7.7 0.0 copy-start.3
  7.7 0.7 %copy-done = bf16[64,3,4,4]{0,3,2,1:T(4,128)(2,1)S(1)} copy-done((bf16[64,3,4,4]{0,3,2,1:T(4,128)(2,1)S(1)}, bf16[64,3,4,4]{0,3,2,1:T(4,128)(2,1)}, u32[]{:S(2)}) %copy-start) | copy-done | bytes 6168
  8.4 0.3 critic_weights.1
  8.7 2.9 %collective-permute-done.2.previous_ref = bf16[2,3,4,256]{3,2,1,0:T(4,128)(2,1)S(1)} collective-permute-done((bf16[2,3,4,256]{3,2,1,0:T(4,128)(2,1)S(1)}, bf16[2,3,4,256]{3,2,1,0:T(4,128)(2,1)S(1)}, u32[]{:S(2)}, u32[]{:S(2)}) %collective-permute-start.2) | collective-permute-done | bytes 12320 | tf_op jit(solution)/shard_map/ppermute | solution.py:372
  11.5 1.0 %critic.1 = f32[2,1664]{1,0:T(2,128)S(1)} custom-call(s32[1]{0:T(128)} %bitcast.row_ref, f32[2,3,4,256]{3,2,1,0:T(4,128)S(1)} %collective-permute-done.under_ref, f32[2,3,4,256]{3,2,1,0:T(4,128)S(1)} %collective-permute-done.1.upper_ref, bf16[2,3,4,256]{3,2,1,0:T(4,128)(2,1)S(1)} %collective-permute-done.2.previous_ref, ...), custom_call_target="tpu_custom_call" | custom-call | tf_op jit(solution)/shard_map/critic/pallas_call | solution.py:187
  12.5 0.8 %broadcast_in_dim.28 = f16[32,2,1664]{2,1,0:T(2,128)(2,1)} broadcast(f16[2,1664]{1,0:T(2,128)(2,1)S(1)} %convert_element_type.22), dimensions={1,2} | broadcast | bytes 219648 | tf_op jit(solution)/shard_map/broadcast_in_dim | solution.py:357
  13.3 10.7 %all-to-all-start = ((f16[32,2,1664]{2,1,0:T(2,128)(2,1)}), f16[32,2,1664]{2,1,0:T(2,128)(2,1)S(1)}, u32[]{:S(2)}, u32[]{:S(2)}) async-start(f16[32,2,1664]{2,1,0:T(2,128)(2,1)} %broadcast_in_dim.28), calls=%async_computation | async-start | bytes 425984 | tf_op jit(solution)/shard_map/all_to_all | solution.py:359
  24.0 0.7 %collective-permute-start.4 = (f32[2,3,4,256]{3,2,1,0:T(4,128)S(1)}, f32[2,3,4,256]{3,2,1,0:T(4,128)S(1)}, u32[]{:S(2)}, u32[]{:S(2)}) collective-permute-start(f32[2,3,4,256]{3,2,1,0:T(4,128)S(1)} %convert_element_type.21), channel_id=1, source_target_pairs={{15,16},{31,32},{47,48},{16,15},{32,31},{48,47},{79,80},{95,96},{1... | collective-permute-start | bytes 73736 | tf_op jit(solution)/shard_map/ppermute | solution.py:374
  24.7 2.3 %collective-permute-start.3 = (bf16[2,3,4,256]{3,2,1,0:T(4,128)(2,1)S(1)}, bf16[2,3,4,256]{3,2,1,0:T(4,128)(2,1)S(1)}, u32[]{:S(2)}, u32[]{:S(2)}) collective-permute-start(bf16[2,3,4,256]{3,2,1,0:T(4,128)(2,1)S(1)} %constant_dynamic-update-slice_fusion.image_ref), channel_id=1, source_target_pairs={{1,0},{2,1},{3,2},{4,3},{5,4},{6,5},{7,6},{8,7},{9,8},{10,9},{11,1... | collective-permute-start | bytes 36872 | tf_op jit(solution)/shard_map/ppermute | solution.py:373
  27.0 0.1 copy.15.lpips_ref
  27.1 0.4 feature_weights.1
  27.5 2.3 %all-to-all-done = f16[32,2,1664]{2,1,0:T(2,128)(2,1)S(1)} async-done(((f16[32,2,1664]{2,1,0:T(2,128)(2,1)}), f16[32,2,1664]{2,1,0:T(2,128)(2,1)S(1)}, u32[]{:S(2)}, u32[]{:S(2)}) %all-to-all-start) | async-done | bytes 213024 | tf_op jit(solution)/shard_map/all_to_all | solution.py:359
  29.8 0.1 convert_reduce_fusion
  29.9 0.7 %broadcast_in_dim.29 = f16[16,2,1664]{2,1,0:T(2,128)(2,1)} broadcast(f16[2,1664]{1,0:T(2,128)(2,1)S(1)} %multiply_convert_fusion), dimensions={1,2} | broadcast | bytes 113152 | tf_op jit(solution)/shard_map/broadcast_in_dim | solution.py:357
  30.6 15.7 %all-to-all-start.1 = ((f16[16,2,1664]{2,1,0:T(2,128)(2,1)}), f16[16,2,1664]{2,1,0:T(2,128)(2,1)S(1)}, u32[]{:S(2)}, u32[]{:S(2)}) async-start(f16[16,2,1664]{2,1,0:T(2,128)(2,1)} %broadcast_in_dim.29), calls=%async_computation.1 | async-start | bytes 212992 | tf_op jit(solution)/shard_map/all_to_all | solution.py:359
  46.3 3.3 %features.1 = f32[3,4,256]{2,1,0:T(4,128)} custom-call(s32[1]{0:T(128)} %bitcast.row_ref, bf16[64,256]{1,0:T(8,128)(2,1)S(1)} %get-tuple-element.23.critic_bwd_ref, bf16[640,144]{1,0:T(8,128)(2,1)S(1)} %get-tuple-element.24.first_fwd_ref, bf16[48,384]{1,0:T(8,128)(2,1)S(1)} %get-tuple-element.25.first_bwd_ref, ...), custom_call_target="tpu_custom_call" | custom-call | flops 20000000000 | bytes 1000000 | tf_op jit(solution)/shard_map/features/pallas_call | solution.py:310
  49.7 2.8 %all-to-all-done.1 = f16[16,2,1664]{2,1,0:T(2,128)(2,1)S(1)} async-done(((f16[16,2,1664]{2,1,0:T(2,128)(2,1)}), f16[16,2,1664]{2,1,0:T(2,128)(2,1)S(1)}, u32[]{:S(2)}, u32[]{:S(2)}) %all-to-all-start.1) | async-done | bytes 106528 | tf_op jit(solution)/shard_map/all_to_all | solution.py:359
  52.5 0.1 convert_reduce_fusion.1.total_ref
  52.6 0.7 %finish.1 = (f32[3,4,4,64]{3,2,1,0:T(4,128)}, f32[1,64]{1,0:T(1,128)}) custom-call(f32[2,1664]{1,0:T(2,128)S(1)} %convert_reduce_fusion.1.total_ref), custom_call_target="tpu_custom_call" | custom-call | tf_op jit(solution)/shard_map/finish/pallas_call | solution.py:339
  (18 shorter events, 0.1 us)
Async XLA Ops:
  0.6 0.7 %copy-start.4 = (bf16[1,3,4,256]{3,2,1,0:T(4,128)(2,1)S(1)}, bf16[1,3,4,256]{3,2,1,0:T(4,128)(2,1)}, u32[]{:S(2)}) copy-start(bf16[1,3,4,256]{3,2,1,0:T(4,128)(2,1)} %param.8) | copy-start | bytes 18436
  1.4 10.2 %collective-permute-start = (f32[2,3,4,256]{3,2,1,0:T(4,128)S(1)}, f32[2,3,4,256]{3,2,1,0:T(4,128)S(1)}, u32[]{:S(2)}, u32[]{:S(2)}) collective-permute-start(f32[2,3,4,256]{3,2,1,0:T(4,128)S(1)} %convert_element_type.21), channel_id=1, source_target_pairs={{16,25},{32,41},{48,57},{80,89},{96,105},{112,121},{144,153},{160,... | collective-permute-start | bytes 73736 | tf_op jit(solution)/shard_map/ppermute | solution.py:368
  2.0 9.5 %collective-permute-start.1 = (f32[2,3,4,256]{3,2,1,0:T(4,128)S(1)}, f32[2,3,4,256]{3,2,1,0:T(4,128)S(1)}, u32[]{:S(2)}, u32[]{:S(2)}) collective-permute-start(f32[2,3,4,256]{3,2,1,0:T(4,128)S(1)} %convert_element_type.21), channel_id=1, source_target_pairs={{15,25},{31,41},{47,57},{79,89},{95,105},{111,121},{143,153},{159,... | collective-permute-start | bytes 73736 | tf_op jit(solution)/shard_map/ppermute | solution.py:369
  2.7 8.8 %collective-permute-start.2 = (bf16[2,3,4,256]{3,2,1,0:T(4,128)(2,1)S(1)}, bf16[2,3,4,256]{3,2,1,0:T(4,128)(2,1)S(1)}, u32[]{:S(2)}, u32[]{:S(2)}) collective-permute-start(bf16[2,3,4,256]{3,2,1,0:T(4,128)(2,1)S(1)} %constant_dynamic-update-slice_fusion.image_ref), channel_id=1, source_target_pairs={{0,1},{1,2},{2,3},{3,4},{4,5},{5,6},{6,7},{7,8},{8,9},{9,10},{10,1... | collective-permute-start | bytes 36872 | tf_op jit(solution)/shard_map/ppermute | solution.py:372
  7.7 0.7 %copy-start = (bf16[64,3,4,4]{0,3,2,1:T(4,128)(2,1)S(1)}, bf16[64,3,4,4]{0,3,2,1:T(4,128)(2,1)}, u32[]{:S(2)}) copy-start(bf16[64,3,4,4]{0,3,2,1:T(4,128)(2,1)} %param.12) | copy-start | bytes 18436
  7.7 0.7 %copy-start.1 = (f32[64]{0:T(128)S(1)}, f32[64]{0:T(128)}, u32[]{:S(2)}) copy-start(f32[64]{0:T(128)} %param.13) | copy-start | bytes 772
  7.7 1.0 %copy-start.3 = (bf16[64,3,3,3]{0,3,2,1:T(4,128)(2,1)S(1)}, bf16[64,3,3,3]{0,3,2,1:T(4,128)(2,1)}, u32[]{:S(2)}) copy-start(bf16[64,3,3,3]{0,3,2,1:T(4,128)(2,1)} %param.9) | copy-start | bytes 10372
  13.3 13.7 %copy-start.2 = (bf16[64,64,3,3]{1,0,3,2:T(8,128)(2,1)S(1)}, bf16[64,64,3,3]{1,0,3,2:T(8,128)(2,1)}, u32[]{:S(2)}) copy-start(bf16[64,64,3,3]{1,0,3,2:T(8,128)(2,1)} %param.10) | copy-start | bytes 221188
  13.3 16.5 %all-to-all-start = ((f16[32,2,1664]{2,1,0:T(2,128)(2,1)}), f16[32,2,1664]{2,1,0:T(2,128)(2,1)S(1)}, u32[]{:S(2)}, u32[]{:S(2)}) async-start(f16[32,2,1664]{2,1,0:T(2,128)(2,1)} %broadcast_in_dim.28), calls=%async_computation | async-start | bytes 425984 | tf_op jit(solution)/shard_map/all_to_all | solution.py:359
  24.0 3.0 %copy-start.5 = (f32[64]{0:T(128)S(1)}, f32[64]{0:T(128)}, u32[]{:S(2)}) copy-start(f32[64]{0:T(128)} %param.11) | copy-start | bytes 772
  24.0 22.3 %collective-permute-start.4 = (f32[2,3,4,256]{3,2,1,0:T(4,128)S(1)}, f32[2,3,4,256]{3,2,1,0:T(4,128)S(1)}, u32[]{:S(2)}, u32[]{:S(2)}) collective-permute-start(f32[2,3,4,256]{3,2,1,0:T(4,128)S(1)} %convert_element_type.21), channel_id=1, source_target_pairs={{15,16},{31,32},{47,48},{16,15},{32,31},{48,47},{79,80},{95,96},{1... | collective-permute-start | bytes 73736 | tf_op jit(solution)/shard_map/ppermute | solution.py:374
  24.7 21.6 %collective-permute-start.3 = (bf16[2,3,4,256]{3,2,1,0:T(4,128)(2,1)S(1)}, bf16[2,3,4,256]{3,2,1,0:T(4,128)(2,1)S(1)}, u32[]{:S(2)}, u32[]{:S(2)}) collective-permute-start(bf16[2,3,4,256]{3,2,1,0:T(4,128)(2,1)S(1)} %constant_dynamic-update-slice_fusion.image_ref), channel_id=1, source_target_pairs={{1,0},{2,1},{3,2},{4,3},{5,4},{6,5},{7,6},{8,7},{9,8},{10,9},{11,1... | collective-permute-start | bytes 36872 | tf_op jit(solution)/shard_map/ppermute | solution.py:373
  30.6 21.9 %all-to-all-start.1 = ((f16[16,2,1664]{2,1,0:T(2,128)(2,1)}), f16[16,2,1664]{2,1,0:T(2,128)(2,1)S(1)}, u32[]{:S(2)}, u32[]{:S(2)}) async-start(f16[16,2,1664]{2,1,0:T(2,128)(2,1)} %broadcast_in_dim.29), calls=%async_computation.1 | async-start | bytes 212992 | tf_op jit(solution)/shard_map/all_to_all | solution.py:359

commit v5 on v4

--- a/solution.py
+++ b/solution.py
@@ -15,8 +15,8 @@
 PLANE = ("y", "x", "c")
 COLUMN = ("zh", "zl")
 MIDDLE = 9
-PLANE_ORDER = [5] + [peer for peer in range(32) if peer != 5]
-COLUMN_ORDER = list(range(8, 16)) + list(range(8))
+PLANE_ORDER = [21] + [peer for peer in range(32) if peer != 21]
+COLUMN_ORDER = [(10 + peer) % 16 for peer in range(16)]
 F32 = jnp.float32
 BF16 = jnp.bfloat16
 VMEM = pl.BlockSpec(memory_space=pltpu.VMEM)
@@ -84,8 +84,11 @@
     )(critic, head)
 
 
-def feature_weights_kernel(first_ref, second_ref, critic_ref, critic_bwd_ref, first_fwd_ref, first_bwd_ref,
-                           second_fwd_ref, second_bwd_ref):
+def feature_weights_kernel(row_ref, first_ref, second_ref, critic_ref, next_ref, early_ref, under_ref, image_ref,
+                           critic_bwd_ref, first_fwd_ref, first_bwd_ref,
+                           second_fwd_ref, second_bwd_ref, copy_ref):
+    between = (row_ref[0] // 4 & 15) == MIDDLE
+    copy_ref[...] = jnp.where(between, under_ref[...], image_ref[...].astype(F32)).astype(BF16)
     critic = critic_ref[...]
     first = first_ref[...]
     for row in range(10):
@@ -109,17 +112,17 @@
         )
 
 
-def feature_weights(first, second, critic):
-    shapes = [(64, 256), (640, 144), (48, 384), (192, 192), (192, 192)]
+def feature_weights(*operands):
+    shapes = [(64, 256), (640, 144), (48, 384), (192, 192), (192, 192), (2, 3, 4, 256)]
     return pl.pallas_call(
         feature_weights_kernel,
         out_shape=[jax.ShapeDtypeStruct(shape, BF16) for shape in shapes],
-        in_specs=[VMEM] * 3,
+        in_specs=[SMEM] + [VMEM] * 7,
         out_specs=[VMEM] * len(shapes),
         compiler_params=SMALL,
-        cost_estimate=pl.CostEstimate(flops=100_000_000, bytes_accessed=1_000_000, transcendentals=0),
+        cost_estimate=pl.CostEstimate(flops=20_000_000_000, bytes_accessed=1_000_000, transcendentals=0),
         name="feature_weights",
-    )(first, second, critic)
+    )(*operands)
 
 
 def stack_taps(taps, image):
@@ -209,7 +212,7 @@
 
 
 def feature_kernel(row_ref, critic_bwd_ref, first_fwd_ref, first_bwd_ref, second_fwd_ref, second_bwd_ref,
-                   previous_ref, image_ref, next_ref, far_ref, lpips_ref, spread_ref, critic_fwd_ref, head_ref,
+                   previous_ref, image_ref, next_ref, early_ref, late_ref, lpips_ref, spread_ref, critic_fwd_ref, head_ref,
                    out_ref, slope_ref, pre_ref, act_ref):
     first_row = row_ref[0]
     place = first_row // 4 & 15
@@ -224,9 +227,9 @@
     for image in range(2):
         parts = []
         for channel in range(3):
-            far = far_ref[image, channel]
-            above = jnp.where(place == 0, far, previous_ref[image, channel].astype(F32))
-            below = jnp.where(place == 15, far, next_ref[image, channel].astype(F32))
+            far = late_ref[image, channel].astype(F32)
+            above = jnp.where(place == 0, early_ref[image, channel] + far, previous_ref[image, channel].astype(F32))
+            below = jnp.where(place == 15, far, next_ref[image, channel])
             here = jnp.concatenate(
                 [above, image_ref[image, channel].astype(F32), below, jnp.zeros_like(far)], axis=0
             )
@@ -310,7 +313,7 @@
     return pl.pallas_call(
         feature_kernel,
         out_shape=jax.ShapeDtypeStruct((3, 4, 256), F32),
-        in_specs=[SMEM] + [VMEM] * 13,
+        in_specs=[SMEM] + [VMEM] * 14,
         out_specs=VMEM,
         scratch_shapes=[
             pltpu.VMEM((384, 256), F32),
@@ -318,7 +321,7 @@
             pltpu.VMEM((512, 512), F32),
         ],
         compiler_params=pltpu.CompilerParams(vmem_limit_bytes=16 * 1024 * 1024),
-        cost_estimate=pl.CostEstimate(flops=20_000_000_000, bytes_accessed=1_000_000, transcendentals=1_000_000),
+        cost_estimate=pl.CostEstimate(flops=1_000_000_000, bytes_accessed=1_000_000, transcendentals=1_000_000),
         name="features",
     )(*operands)
 
@@ -370,17 +373,21 @@
     critic_rows = weight_rows(critic_conv)
     spread, critic_fwd, head = critic_weights(critic_rows, critic_head[None])
     previous = lax.ppermute(images, ROWS, [(k, k + 1) for k in range(count - 1) if k % 16 < 15])
-    following = lax.ppermute(images, ROWS, [(k + 1, k) for k in range(count - 1) if k % 16 < 15])
-    far = lax.ppermute(whole, ROWS, far_pairs + [(b, a) for a, b in far_pairs])
+    following = lax.ppermute(whole, ROWS, [(k + 1, k) for k in range(count - 1) if k % 16 < 15])
+    early = lax.ppermute(upper, ("zh",) + ROWS, [(b + MIDDLE, b) for a, b in far_pairs])
+    rest = [(count + a, count + b) for a, b in far_pairs]
+    for base in (0, count):
+        rest += [(base + b + MIDDLE, base + a) for a, b in far_pairs]
     sums = critic(first_row, under, upper, previous, images, spread, critic_fwd, head)
-    sums, first, second, again = lax.optimization_barrier(
-        (sums, weight_rows(vgg_first), jnp.transpose(vgg_second, (2, 3, 0, 1)), critic_rows)
-    )
-    weights = feature_weights(first, second, again)
     plane = exchange_sum(sums.astype(jnp.float16), PLANE, PLANE_ORDER)
+    plane, first, second, again = lax.optimization_barrier(
+        (plane, weight_rows(vgg_first), jnp.transpose(vgg_second, (2, 3, 0, 1)), critic_rows)
+    )
+    *weights, copied = feature_weights(first_row, first, second, again, following, early, under, images)
+    late = lax.ppermute(copied, ("zh",) + ROWS, rest)
     total = exchange_sum((plane * (1.0 / 32.0)).astype(jnp.float16), COLUMN, COLUMN_ORDER)
     grad_image = features(
-        first_row, *weights, previous, images, following, far, lpips_weights[:, None], spread, critic_fwd, head
+        first_row, *weights, previous, images, following, early, late, lpips_weights[:, None], spread, critic_fwd, head
     )
     conv_grad, head_grad = finish(total)
     return grad_image[None], jnp.transpose(conv_grad, (3, 0, 1, 2)), head_grad[0]

time: 53.8 us -> 50.9 us (0.946)
  waiting for transfers between devices: 8.03 us -> 5.81 us
  starting transfers between devices: 35.6 us -> 34.6 us
    all_to_all x2, waiting for transfers between devices: 5.16 us -> 2.91 us  [exchange_sum(): lax.all_to_all(copies, axes, 0, 0, axis_index_groups=groups).astype(F32)]
    all_to_all x2, starting transfers between devices: 26.4 us -> 24.7 us  [exchange_sum(): lax.all_to_all(copies, axes, 0, 0, axis_index_groups=groups).astype(F32)]
    ppermute x2 -> x3, starting transfers between devices: 2.93 us -> 3.59 us  [the longest x1 2.27 us: shards(): lax.ppermute(whole, ROWS, [(k + 1, k) for k in range(count - 1) if k % 16...]
  transfers between devices with their start and end apart: 7 -> 8, of which waited for: 3 -> 3; matrix products, arithmetic and copies ran while one was open for 2% -> 2% of each run, Pallas kernels for 8% -> 8%
where the time goes in v5:
time: 50.9 us; the launch traced here: 50.1 us
  starting transfers between devices  34.6 us (68%)
  waiting for transfers between devices  5.81 us (11%)
  Pallas kernels  5.67 us (11%)
  local copies, waits for them, and re-layouts  3.03 us (6%)
  between operations  0.82 us (2%)
    all_to_all x2, starting transfers between devices, exchange_sum(): lax.all_to_all(copies, axes, 0, 0, axis_index_groups=groups).astype(F32)  24.7 us
    ppermute x1, starting transfers between devices, shards(): lax.ppermute(images, ROWS, [(k, k + 1) for k in range(count - 1) if k % 1...  4.94 us
    pallas_call x1, Pallas kernels, features(): pl.pallas_call(feature_kernel, out_shape=jax.ShapeDtypeStruct((3, 4, 256)...  3.28 us
    all_to_all x2, waiting for transfers between devices, exchange_sum(): lax.all_to_all(copies, axes, 0, 0, axis_index_groups=groups).astype(F32)  2.91 us
    ppermute x1, waiting for transfers between devices, shards(): lax.ppermute(images, ROWS, [(k, k + 1) for k in range(count - 1) if k % 1...  2.89 us
    ppermute x1, starting transfers between devices, shards(): lax.ppermute(whole, ROWS, [(k + 1, k) for k in range(count - 1) if k % 16...  2.27 us
    broadcast_in_dim x2, local copies, waits for them, and re-layouts, exchange_sum(): copies = jnp.broadcast_to(value[None], (peers,) + value.shape)  1.5 us
    unnamed x13, local copies, waits for them, and re-layouts  1.41 us
  transfers between devices with their start and end apart: 8, of which 3 were waited for; matrix products, arithmetic and copies ran while one was open for 2% of the time, Pallas kernels for 8%

profile of v5, /device:TPU:1, one launch (start us, length us, event | category | flops | bytes accessed | tf_op | source)
XLA Modules:
  0.0 50.1 jit_solution(6592216162527016089)
XLA Ops:
  0.6 0.7 %constant_dynamic-update-slice_fusion.1 = bf16[2,3,4,256]{3,2,1,0:T(4,128)(2,1)S(1)} fusion(bf16[1,3,4,256]{3,2,1,0:T(4,128)(2,1)} %param.7), kind=kLoop, calls=%fused_computation.4 | loop fusion | bytes 12288
  1.4 0.7 %collective-permute-start = (f32[2,3,4,256]{3,2,1,0:T(4,128)S(1)}, f32[2,3,4,256]{3,2,1,0:T(4,128)S(1)}, u32[]{:S(2)}, u32[]{:S(2)}) collective-permute-start(f32[2,3,4,256]{3,2,1,0:T(4,128)S(1)} %convert_element_type.17), channel_id=1, source_target_pairs={{16,25},{32,41},{48,57},{80,89},{96,105},{112,121},{144,153},{160,... | collective-permute-start | bytes 73736 | tf_op jit(solution)/shard_map/ppermute | solution.py:371
  2.0 0.7 %collective-permute-start.1 = (f32[2,3,4,256]{3,2,1,0:T(4,128)S(1)}, f32[2,3,4,256]{3,2,1,0:T(4,128)S(1)}, u32[]{:S(2)}, u32[]{:S(2)}) collective-permute-start(f32[2,3,4,256]{3,2,1,0:T(4,128)S(1)} %convert_element_type.17), channel_id=1, source_target_pairs={{15,25},{31,41},{47,57},{79,89},{95,105},{111,121},{143,153},{159,... | collective-permute-start | bytes 73736 | tf_op jit(solution)/shard_map/ppermute | solution.py:372
  2.7 4.9 %collective-permute-start.2 = (bf16[2,3,4,256]{3,2,1,0:T(4,128)(2,1)S(1)}, bf16[2,3,4,256]{3,2,1,0:T(4,128)(2,1)S(1)}, u32[]{:S(2)}, u32[]{:S(2)}) collective-permute-start(bf16[2,3,4,256]{3,2,1,0:T(4,128)(2,1)S(1)} %constant_dynamic-update-slice_fusion.image_ref), channel_id=1, source_target_pairs={{0,1},{1,2},{2,3},{3,4},{4,5},{5,6},{6,7},{7,8},{8,9},{9,10},{10,1... | collective-permute-start | bytes 36872 | tf_op jit(solution)/shard_map/ppermute | solution.py:375
  7.7 0.0 copy-start
  7.7 0.7 %copy-done = bf16[64,3,4,4]{0,3,2,1:T(4,128)(2,1)S(1)} copy-done((bf16[64,3,4,4]{0,3,2,1:T(4,128)(2,1)S(1)}, bf16[64,3,4,4]{0,3,2,1:T(4,128)(2,1)}, u32[]{:S(2)}) %copy-start) | copy-done | bytes 6168
  8.4 0.3 critic_weights.1
  8.6 2.9 %collective-permute-done.2.previous_ref = bf16[2,3,4,256]{3,2,1,0:T(4,128)(2,1)S(1)} collective-permute-done((bf16[2,3,4,256]{3,2,1,0:T(4,128)(2,1)S(1)}, bf16[2,3,4,256]{3,2,1,0:T(4,128)(2,1)S(1)}, u32[]{:S(2)}, u32[]{:S(2)}) %collective-permute-start.2) | collective-permute-done | bytes 12320 | tf_op jit(solution)/shard_map/ppermute | solution.py:375
  11.5 1.0 %critic.1 = f32[2,1664]{1,0:T(2,128)S(1)} custom-call(s32[1]{0:T(128)} %bitcast.row_ref, f32[2,3,4,256]{3,2,1,0:T(4,128)S(1)} %collective-permute-done.under_ref, f32[2,3,4,256]{3,2,1,0:T(4,128)S(1)} %collective-permute-done.1.upper_ref, bf16[2,3,4,256]{3,2,1,0:T(4,128)(2,1)S(1)} %collective-permute-done.2.previous_ref, ...), custom_call_target="tpu_custom_call" | custom-call | tf_op jit(solution)/shard_map/critic/pallas_call | solution.py:190
  12.5 0.8 %broadcast_in_dim.26 = f16[32,2,1664]{2,1,0:T(2,128)(2,1)} broadcast(f16[2,1664]{1,0:T(2,128)(2,1)S(1)} %convert_element_type.18), dimensions={1,2} | broadcast | bytes 219648 | tf_op jit(solution)/shard_map/broadcast_in_dim | solution.py:360
  13.4 11.6 %all-to-all-start = ((f16[32,2,1664]{2,1,0:T(2,128)(2,1)}), f16[32,2,1664]{2,1,0:T(2,128)(2,1)S(1)}, u32[]{:S(2)}, u32[]{:S(2)}) async-start(f16[32,2,1664]{2,1,0:T(2,128)(2,1)} %broadcast_in_dim.26), calls=%async_computation | async-start | bytes 425984 | tf_op jit(solution)/shard_map/all_to_all | solution.py:362
  24.9 2.3 %collective-permute-start.3 = (f32[2,3,4,256]{3,2,1,0:T(4,128)S(1)}, f32[2,3,4,256]{3,2,1,0:T(4,128)S(1)}, u32[]{:S(2)}, u32[]{:S(2)}) collective-permute-start(f32[2,3,4,256]{3,2,1,0:T(4,128)S(1)} %convert_element_type.17), channel_id=1, source_target_pairs={{1,0},{2,1},{3,2},{4,3},{5,4},{6,5},{7,6},{8,7},{9,8},{10,9},{11,1... | collective-permute-start | bytes 73736 | tf_op jit(solution)/shard_map/ppermute | solution.py:376
  27.2 0.7 %collective-permute-start.4 = (f32[2,3,4,256]{3,2,1,0:T(4,128)S(1)}, f32[2,3,4,256]{3,2,1,0:T(4,128)S(1)}, u32[]{:S(2)}, u32[]{:S(2)}) collective-permute-start(f32[2,3,4,256]{3,2,1,0:T(4,128)S(1)} %collective-permute-done.1.upper_ref), channel_id=1, source_target_pairs={{25,16},{41,32},{57,48},{89,80},{105,96},{121,112},{153,144},{169,... | collective-permute-start | bytes 73736 | tf_op jit(solution)/shard_map/ppermute | solution.py:377
  27.9 0.7 %all-to-all-done = f16[32,2,1664]{2,1,0:T(2,128)(2,1)S(1)} async-done(((f16[32,2,1664]{2,1,0:T(2,128)(2,1)}), f16[32,2,1664]{2,1,0:T(2,128)(2,1)S(1)}, u32[]{:S(2)}, u32[]{:S(2)}) %all-to-all-start) | async-done | bytes 213024 | tf_op jit(solution)/shard_map/all_to_all | solution.py:362
  28.6 0.1 convert_reduce_fusion
  28.7 0.7 %broadcast_in_dim.29 = f16[16,2,1664]{2,1,0:T(2,128)(2,1)} broadcast(f16[2,1664]{1,0:T(2,128)(2,1)S(1)} %multiply_convert_fusion), dimensions={1,2} | broadcast | bytes 113152 | tf_op jit(solution)/shard_map/broadcast_in_dim | solution.py:360
  29.4 13.2 %all-to-all-start.1 = ((f16[16,2,1664]{2,1,0:T(2,128)(2,1)}), f16[16,2,1664]{2,1,0:T(2,128)(2,1)S(1)}, u32[]{:S(2)}, u32[]{:S(2)}) async-start(f16[16,2,1664]{2,1,0:T(2,128)(2,1)} %broadcast_in_dim.29), calls=%async_computation.1 | async-start | bytes 212992 | tf_op jit(solution)/shard_map/all_to_all | solution.py:362
  42.7 0.4 feature_weights.1
  43.1 0.7 %collective-permute-start.5 = (bf16[2,3,4,256]{3,2,1,0:T(4,128)(2,1)S(1)}, bf16[2,3,4,256]{3,2,1,0:T(4,128)(2,1)S(1)}, u32[]{:S(2)}, u32[]{:S(2)}) collective-permute-start(bf16[2,3,4,256]{3,2,1,0:T(4,128)(2,1)S(1)} %get-tuple-element.29), channel_id=1, source_target_pairs={{271,272},{287,288},{303,304},{25,15},{41,31},{57,47},{281,271},{2... | collective-permute-start | bytes 36872 | tf_op jit(solution)/shard_map/ppermute | solution.py:387
  43.8 0.1 copy.16.lpips_ref
  43.9 3.3 %features.1 = f32[3,4,256]{2,1,0:T(4,128)} custom-call(s32[1]{0:T(128)} %bitcast.row_ref, bf16[64,256]{1,0:T(8,128)(2,1)S(1)} %get-tuple-element.24.critic_bwd_ref, bf16[640,144]{1,0:T(8,128)(2,1)S(1)} %get-tuple-element.25.first_fwd_ref, bf16[48,384]{1,0:T(8,128)(2,1)S(1)} %get-tuple-element.26.first_bwd_ref, ...), custom_call_target="tpu_custom_call" | custom-call | flops 1000000000 | bytes 1000000 | tf_op jit(solution)/shard_map/features/pallas_call | solution.py:313
  47.2 2.2 %all-to-all-done.1 = f16[16,2,1664]{2,1,0:T(2,128)(2,1)S(1)} async-done(((f16[16,2,1664]{2,1,0:T(2,128)(2,1)}), f16[16,2,1664]{2,1,0:T(2,128)(2,1)S(1)}, u32[]{:S(2)}, u32[]{:S(2)}) %all-to-all-start.1) | async-done | bytes 106528 | tf_op jit(solution)/shard_map/all_to_all | solution.py:362
  49.3 0.1 convert_reduce_fusion.1.total_ref
  49.4 0.7 %finish.1 = (f32[3,4,4,64]{3,2,1,0:T(4,128)}, f32[1,64]{1,0:T(1,128)}) custom-call(f32[2,1664]{1,0:T(2,128)S(1)} %convert_reduce_fusion.1.total_ref), custom_call_target="tpu_custom_call" | custom-call | tf_op jit(solution)/shard_map/finish/pallas_call | solution.py:342
  (20 shorter events, 0.1 us)
Async XLA Ops:
  0.6 0.7 %copy-start.4 = (bf16[1,3,4,256]{3,2,1,0:T(4,128)(2,1)S(1)}, bf16[1,3,4,256]{3,2,1,0:T(4,128)(2,1)}, u32[]{:S(2)}) copy-start(bf16[1,3,4,256]{3,2,1,0:T(4,128)(2,1)} %param.8) | copy-start | bytes 18436
  1.4 10.2 %collective-permute-start = (f32[2,3,4,256]{3,2,1,0:T(4,128)S(1)}, f32[2,3,4,256]{3,2,1,0:T(4,128)S(1)}, u32[]{:S(2)}, u32[]{:S(2)}) collective-permute-start(f32[2,3,4,256]{3,2,1,0:T(4,128)S(1)} %convert_element_type.17), channel_id=1, source_target_pairs={{16,25},{32,41},{48,57},{80,89},{96,105},{112,121},{144,153},{160,... | collective-permute-start | bytes 73736 | tf_op jit(solution)/shard_map/ppermute | solution.py:371
  2.0 9.5 %collective-permute-start.1 = (f32[2,3,4,256]{3,2,1,0:T(4,128)S(1)}, f32[2,3,4,256]{3,2,1,0:T(4,128)S(1)}, u32[]{:S(2)}, u32[]{:S(2)}) collective-permute-start(f32[2,3,4,256]{3,2,1,0:T(4,128)S(1)} %convert_element_type.17), channel_id=1, source_target_pairs={{15,25},{31,41},{47,57},{79,89},{95,105},{111,121},{143,153},{159,... | collective-permute-start | bytes 73736 | tf_op jit(solution)/shard_map/ppermute | solution.py:372
  2.7 8.8 %collective-permute-start.2 = (bf16[2,3,4,256]{3,2,1,0:T(4,128)(2,1)S(1)}, bf16[2,3,4,256]{3,2,1,0:T(4,128)(2,1)S(1)}, u32[]{:S(2)}, u32[]{:S(2)}) collective-permute-start(bf16[2,3,4,256]{3,2,1,0:T(4,128)(2,1)S(1)} %constant_dynamic-update-slice_fusion.image_ref), channel_id=1, source_target_pairs={{0,1},{1,2},{2,3},{3,4},{4,5},{5,6},{6,7},{7,8},{8,9},{9,10},{10,1... | collective-permute-start | bytes 36872 | tf_op jit(solution)/shard_map/ppermute | solution.py:375
  7.7 0.7 %copy-start = (bf16[64,3,4,4]{0,3,2,1:T(4,128)(2,1)S(1)}, bf16[64,3,4,4]{0,3,2,1:T(4,128)(2,1)}, u32[]{:S(2)}) copy-start(bf16[64,3,4,4]{0,3,2,1:T(4,128)(2,1)} %param.12) | copy-start | bytes 18436
  7.7 0.7 %copy-start.1 = (f32[64]{0:T(128)S(1)}, f32[64]{0:T(128)}, u32[]{:S(2)}) copy-start(f32[64]{0:T(128)} %param.13) | copy-start | bytes 772
  13.4 13.8 %copy-start.3 = (bf16[64,3,3,3]{0,3,2,1:T(4,128)(2,1)S(1)}, bf16[64,3,3,3]{0,3,2,1:T(4,128)(2,1)}, u32[]{:S(2)}) copy-start(bf16[64,3,3,3]{0,3,2,1:T(4,128)(2,1)} %param.9) | copy-start | bytes 10372
  13.4 15.3 %all-to-all-start = ((f16[32,2,1664]{2,1,0:T(2,128)(2,1)}), f16[32,2,1664]{2,1,0:T(2,128)(2,1)S(1)}, u32[]{:S(2)}, u32[]{:S(2)}) async-start(f16[32,2,1664]{2,1,0:T(2,128)(2,1)} %broadcast_in_dim.26), calls=%async_computation | async-start | bytes 425984 | tf_op jit(solution)/shard_map/all_to_all | solution.py:362
  24.9 17.7 %collective-permute-start.3 = (f32[2,3,4,256]{3,2,1,0:T(4,128)S(1)}, f32[2,3,4,256]{3,2,1,0:T(4,128)S(1)}, u32[]{:S(2)}, u32[]{:S(2)}) collective-permute-start(f32[2,3,4,256]{3,2,1,0:T(4,128)S(1)} %convert_element_type.17), channel_id=1, source_target_pairs={{1,0},{2,1},{3,2},{4,3},{5,4},{6,5},{7,6},{8,7},{9,8},{10,9},{11,1... | collective-permute-start | bytes 73736 | tf_op jit(solution)/shard_map/ppermute | solution.py:376
  27.2 15.4 %collective-permute-start.4 = (f32[2,3,4,256]{3,2,1,0:T(4,128)S(1)}, f32[2,3,4,256]{3,2,1,0:T(4,128)S(1)}, u32[]{:S(2)}, u32[]{:S(2)}) collective-permute-start(f32[2,3,4,256]{3,2,1,0:T(4,128)S(1)} %collective-permute-done.1.upper_ref), channel_id=1, source_target_pairs={{25,16},{41,32},{57,48},{89,80},{105,96},{121,112},{153,144},{169,... | collective-permute-start | bytes 73736 | tf_op jit(solution)/shard_map/ppermute | solution.py:377
  28.7 13.9 %copy-start.2 = (bf16[64,64,3,3]{1,0,3,2:T(8,128)(2,1)S(1)}, bf16[64,64,3,3]{1,0,3,2:T(8,128)(2,1)}, u32[]{:S(2)}) copy-start(bf16[64,64,3,3]{1,0,3,2:T(8,128)(2,1)} %param.10) | copy-start | bytes 221188
  29.4 19.9 %all-to-all-start.1 = ((f16[16,2,1664]{2,1,0:T(2,128)(2,1)}), f16[16,2,1664]{2,1,0:T(2,128)(2,1)S(1)}, u32[]{:S(2)}, u32[]{:S(2)}) async-start(f16[16,2,1664]{2,1,0:T(2,128)(2,1)} %broadcast_in_dim.29), calls=%async_computation.1 | async-start | bytes 212992 | tf_op jit(solution)/shard_map/all_to_all | solution.py:362
  43.1 0.7 %copy-start.5 = (f32[64]{0:T(128)S(1)}, f32[64]{0:T(128)}, u32[]{:S(2)}) copy-start(f32[64]{0:T(128)} %param.11) | copy-start | bytes 772
  43.1 0.8 %collective-permute-start.5 = (bf16[2,3,4,256]{3,2,1,0:T(4,128)(2,1)S(1)}, bf16[2,3,4,256]{3,2,1,0:T(4,128)(2,1)S(1)}, u32[]{:S(2)}, u32[]{:S(2)}) collective-permute-start(bf16[2,3,4,256]{3,2,1,0:T(4,128)(2,1)S(1)} %get-tuple-element.29), channel_id=1, source_target_pairs={{271,272},{287,288},{303,304},{25,15},{41,31},{57,47},{281,271},{2... | collective-permute-start | bytes 36872 | tf_op jit(solution)/shard_map/ppermute | solution.py:387

commit v6 on v5

--- a/solution.py
+++ b/solution.py
@@ -15,8 +15,8 @@
 PLANE = ("y", "x", "c")
 COLUMN = ("zh", "zl")
 MIDDLE = 9
-PLANE_ORDER = [21] + [peer for peer in range(32) if peer != 21]
-COLUMN_ORDER = [(10 + peer) % 16 for peer in range(16)]
+PLANE_ORDER = [21, 0, 1, 2, 3, 6, 7, 8, 9, 24, 25, 4, 5, 10, 11, 14, 15, 16, 17, 26, 27, 30, 31, 12, 13, 18, 19, 22, 23, 28, 29, 20]
+COLUMN_ORDER = [10, 0, 1, 2, 3, 15, 4, 14, 5, 13, 6, 12, 7, 11, 8, 9]
 F32 = jnp.float32
 BF16 = jnp.bfloat16
 VMEM = pl.BlockSpec(memory_space=pltpu.VMEM)
@@ -177,7 +177,7 @@
     for block in range(12):
         here = grads[16 * block : 16 * block + 16]
         rows.append(here[1:5, :64] + here[3:7, 64:128])
-    packed = 128.0 * jnp.concatenate(
+    packed = 64.0 * jnp.concatenate(
         [jnp.concatenate(rows[:6], axis=0), jnp.concatenate(rows[6:], axis=0)], axis=1
     )
     for row in range(24):
@@ -330,7 +330,7 @@
     patches = 8 * 128 * 128
     for row in range(24):
         here = total_ref[row // 12 : row // 12 + 1, 128 * (row % 12) : 128 * (row % 12) + 128]
-        here = here * (32.0 / 128.0 / patches)
+        here = here * (32.0 / 64.0 / patches)
         channel, row_tap = row % 12 // 4, row % 4
         for half in range(2):
             col_tap = 2 * half + row // 12

time: 50.9 us -> 50.7 us (level)
  no operation moved by 1% of the time
where the time goes in v6:
time: 50.7 us; the launch traced here: 49.9 us
  starting transfers between devices  34.6 us (68%)
  Pallas kernels  5.67 us (11%)
  waiting for transfers between devices  5.64 us (11%)
  local copies, waits for them, and re-layouts  3.03 us (6%)
  between operations  0.82 us (2%)
    all_to_all x2, starting transfers between devices, exchange_sum(): lax.all_to_all(copies, axes, 0, 0, axis_index_groups=groups).astype(F32)  24.7 us
    ppermute x1, starting transfers between devices, shards(): lax.ppermute(images, ROWS, [(k, k + 1) for k in range(count - 1) if k % 1...  4.94 us
    pallas_call x1, Pallas kernels, features(): pl.pallas_call(feature_kernel, out_shape=jax.ShapeDtypeStruct((3, 4, 256)...  3.28 us
    ppermute x1, waiting for transfers between devices, shards(): lax.ppermute(images, ROWS, [(k, k + 1) for k in range(count - 1) if k % 1...  2.89 us
    all_to_all x2, waiting for transfers between devices, exchange_sum(): lax.all_to_all(copies, axes, 0, 0, axis_index_groups=groups).astype(F32)  2.74 us
    ppermute x1, starting transfers between devices, shards(): lax.ppermute(whole, ROWS, [(k + 1, k) for k in range(count - 1) if k % 16...  2.27 us
    broadcast_in_dim x2, local copies, waits for them, and re-layouts, exchange_sum(): copies = jnp.broadcast_to(value[None], (peers,) + value.shape)  1.5 us
    unnamed x13, local copies, waits for them, and re-layouts  1.41 us
  transfers between devices with their start and end apart: 8, of which 3 were waited for; matrix products, arithmetic and copies ran while one was open for 2% of the time, Pallas kernels for 8%

profile of v6, /device:TPU:1, one launch (start us, length us, event | category | flops | bytes accessed | tf_op | source)
XLA Modules:
  0.0 49.9 jit_solution(5411824599865565211)
XLA Ops:
  0.6 0.7 %constant_dynamic-update-slice_fusion.1 = bf16[2,3,4,256]{3,2,1,0:T(4,128)(2,1)S(1)} fusion(bf16[1,3,4,256]{3,2,1,0:T(4,128)(2,1)} %param.7), kind=kLoop, calls=%fused_computation.4 | loop fusion | bytes 12288
  1.4 0.7 %collective-permute-start = (f32[2,3,4,256]{3,2,1,0:T(4,128)S(1)}, f32[2,3,4,256]{3,2,1,0:T(4,128)S(1)}, u32[]{:S(2)}, u32[]{:S(2)}) collective-permute-start(f32[2,3,4,256]{3,2,1,0:T(4,128)S(1)} %convert_element_type.17), channel_id=1, source_target_pairs={{16,25},{32,41},{48,57},{80,89},{96,105},{112,121},{144,153},{160,... | collective-permute-start | bytes 73736 | tf_op jit(solution)/shard_map/ppermute | solution.py:371
  2.0 0.7 %collective-permute-start.1 = (f32[2,3,4,256]{3,2,1,0:T(4,128)S(1)}, f32[2,3,4,256]{3,2,1,0:T(4,128)S(1)}, u32[]{:S(2)}, u32[]{:S(2)}) collective-permute-start(f32[2,3,4,256]{3,2,1,0:T(4,128)S(1)} %convert_element_type.17), channel_id=1, source_target_pairs={{15,25},{31,41},{47,57},{79,89},{95,105},{111,121},{143,153},{159,... | collective-permute-start | bytes 73736 | tf_op jit(solution)/shard_map/ppermute | solution.py:372
  2.7 4.9 %collective-permute-start.2 = (bf16[2,3,4,256]{3,2,1,0:T(4,128)(2,1)S(1)}, bf16[2,3,4,256]{3,2,1,0:T(4,128)(2,1)S(1)}, u32[]{:S(2)}, u32[]{:S(2)}) collective-permute-start(bf16[2,3,4,256]{3,2,1,0:T(4,128)(2,1)S(1)} %constant_dynamic-update-slice_fusion.image_ref), channel_id=1, source_target_pairs={{0,1},{1,2},{2,3},{3,4},{4,5},{5,6},{6,7},{7,8},{8,9},{9,10},{10,1... | collective-permute-start | bytes 36872 | tf_op jit(solution)/shard_map/ppermute | solution.py:375
  7.7 0.0 copy-start
  7.7 0.7 %copy-done = bf16[64,3,4,4]{0,3,2,1:T(4,128)(2,1)S(1)} copy-done((bf16[64,3,4,4]{0,3,2,1:T(4,128)(2,1)S(1)}, bf16[64,3,4,4]{0,3,2,1:T(4,128)(2,1)}, u32[]{:S(2)}) %copy-start) | copy-done | bytes 6168
  8.4 0.3 critic_weights.1
  8.6 2.9 %collective-permute-done.2.previous_ref = bf16[2,3,4,256]{3,2,1,0:T(4,128)(2,1)S(1)} collective-permute-done((bf16[2,3,4,256]{3,2,1,0:T(4,128)(2,1)S(1)}, bf16[2,3,4,256]{3,2,1,0:T(4,128)(2,1)S(1)}, u32[]{:S(2)}, u32[]{:S(2)}) %collective-permute-start.2) | collective-permute-done | bytes 12320 | tf_op jit(solution)/shard_map/ppermute | solution.py:375
  11.5 1.0 %critic.1 = f32[2,1664]{1,0:T(2,128)S(1)} custom-call(s32[1]{0:T(128)} %bitcast.row_ref, f32[2,3,4,256]{3,2,1,0:T(4,128)S(1)} %collective-permute-done.under_ref, f32[2,3,4,256]{3,2,1,0:T(4,128)S(1)} %collective-permute-done.1.upper_ref, bf16[2,3,4,256]{3,2,1,0:T(4,128)(2,1)S(1)} %collective-permute-done.2.previous_ref, ...), custom_call_target="tpu_custom_call" | custom-call | tf_op jit(solution)/shard_map/critic/pallas_call | solution.py:190
  12.5 0.8 %broadcast_in_dim.26 = f16[32,2,1664]{2,1,0:T(2,128)(2,1)} broadcast(f16[2,1664]{1,0:T(2,128)(2,1)S(1)} %convert_element_type.18), dimensions={1,2} | broadcast | bytes 219648 | tf_op jit(solution)/shard_map/broadcast_in_dim | solution.py:360
  13.4 11.6 %all-to-all-start = ((f16[32,2,1664]{2,1,0:T(2,128)(2,1)}), f16[32,2,1664]{2,1,0:T(2,128)(2,1)S(1)}, u32[]{:S(2)}, u32[]{:S(2)}) async-start(f16[32,2,1664]{2,1,0:T(2,128)(2,1)} %broadcast_in_dim.26), calls=%async_computation | async-start | bytes 425984 | tf_op jit(solution)/shard_map/all_to_all | solution.py:362
  24.9 2.3 %collective-permute-start.3 = (f32[2,3,4,256]{3,2,1,0:T(4,128)S(1)}, f32[2,3,4,256]{3,2,1,0:T(4,128)S(1)}, u32[]{:S(2)}, u32[]{:S(2)}) collective-permute-start(f32[2,3,4,256]{3,2,1,0:T(4,128)S(1)} %convert_element_type.17), channel_id=1, source_target_pairs={{1,0},{2,1},{3,2},{4,3},{5,4},{6,5},{7,6},{8,7},{9,8},{10,9},{11,1... | collective-permute-start | bytes 73736 | tf_op jit(solution)/shard_map/ppermute | solution.py:376
  27.2 0.7 %collective-permute-start.4 = (f32[2,3,4,256]{3,2,1,0:T(4,128)S(1)}, f32[2,3,4,256]{3,2,1,0:T(4,128)S(1)}, u32[]{:S(2)}, u32[]{:S(2)}) collective-permute-start(f32[2,3,4,256]{3,2,1,0:T(4,128)S(1)} %collective-permute-done.1.upper_ref), channel_id=1, source_target_pairs={{25,16},{41,32},{57,48},{89,80},{105,96},{121,112},{153,144},{169,... | collective-permute-start | bytes 73736 | tf_op jit(solution)/shard_map/ppermute | solution.py:377
  27.9 0.6 %all-to-all-done = f16[32,2,1664]{2,1,0:T(2,128)(2,1)S(1)} async-done(((f16[32,2,1664]{2,1,0:T(2,128)(2,1)}), f16[32,2,1664]{2,1,0:T(2,128)(2,1)S(1)}, u32[]{:S(2)}, u32[]{:S(2)}) %all-to-all-start) | async-done | bytes 213024 | tf_op jit(solution)/shard_map/all_to_all | solution.py:362
  28.5 0.1 convert_reduce_fusion
  28.7 0.7 %broadcast_in_dim.29 = f16[16,2,1664]{2,1,0:T(2,128)(2,1)} broadcast(f16[2,1664]{1,0:T(2,128)(2,1)S(1)} %multiply_convert_fusion), dimensions={1,2} | broadcast | bytes 113152 | tf_op jit(solution)/shard_map/broadcast_in_dim | solution.py:360
  29.3 13.2 %all-to-all-start.1 = ((f16[16,2,1664]{2,1,0:T(2,128)(2,1)}), f16[16,2,1664]{2,1,0:T(2,128)(2,1)S(1)}, u32[]{:S(2)}, u32[]{:S(2)}) async-start(f16[16,2,1664]{2,1,0:T(2,128)(2,1)} %broadcast_in_dim.29), calls=%async_computation.1 | async-start | bytes 212992 | tf_op jit(solution)/shard_map/all_to_all | solution.py:362
  42.6 0.4 feature_weights.1
  43.0 0.7 %collective-permute-start.5 = (bf16[2,3,4,256]{3,2,1,0:T(4,128)(2,1)S(1)}, bf16[2,3,4,256]{3,2,1,0:T(4,128)(2,1)S(1)}, u32[]{:S(2)}, u32[]{:S(2)}) collective-permute-start(bf16[2,3,4,256]{3,2,1,0:T(4,128)(2,1)S(1)} %get-tuple-element.29), channel_id=1, source_target_pairs={{271,272},{287,288},{303,304},{25,15},{41,31},{57,47},{281,271},{2... | collective-permute-start | bytes 36872 | tf_op jit(solution)/shard_map/ppermute | solution.py:387
  43.7 0.1 copy.16.lpips_ref
  43.8 3.3 %features.1 = f32[3,4,256]{2,1,0:T(4,128)} custom-call(s32[1]{0:T(128)} %bitcast.row_ref, bf16[64,256]{1,0:T(8,128)(2,1)S(1)} %get-tuple-element.24.critic_bwd_ref, bf16[640,144]{1,0:T(8,128)(2,1)S(1)} %get-tuple-element.25.first_fwd_ref, bf16[48,384]{1,0:T(8,128)(2,1)S(1)} %get-tuple-element.26.first_bwd_ref, ...), custom_call_target="tpu_custom_call" | custom-call | flops 1000000000 | bytes 1000000 | tf_op jit(solution)/shard_map/features/pallas_call | solution.py:313
  47.1 2.1 %all-to-all-done.1 = f16[16,2,1664]{2,1,0:T(2,128)(2,1)S(1)} async-done(((f16[16,2,1664]{2,1,0:T(2,128)(2,1)}), f16[16,2,1664]{2,1,0:T(2,128)(2,1)S(1)}, u32[]{:S(2)}, u32[]{:S(2)}) %all-to-all-start.1) | async-done | bytes 106528 | tf_op jit(solution)/shard_map/all_to_all | solution.py:362
  49.2 0.1 convert_reduce_fusion.1.total_ref
  49.2 0.7 %finish.1 = (f32[3,4,4,64]{3,2,1,0:T(4,128)}, f32[1,64]{1,0:T(1,128)}) custom-call(f32[2,1664]{1,0:T(2,128)S(1)} %convert_reduce_fusion.1.total_ref), custom_call_target="tpu_custom_call" | custom-call | tf_op jit(solution)/shard_map/finish/pallas_call | solution.py:342
  (20 shorter events, 0.1 us)
Async XLA Ops:
  0.6 0.7 %copy-start.4 = (bf16[1,3,4,256]{3,2,1,0:T(4,128)(2,1)S(1)}, bf16[1,3,4,256]{3,2,1,0:T(4,128)(2,1)}, u32[]{:S(2)}) copy-start(bf16[1,3,4,256]{3,2,1,0:T(4,128)(2,1)} %param.8) | copy-start | bytes 18436
  1.4 10.2 %collective-permute-start = (f32[2,3,4,256]{3,2,1,0:T(4,128)S(1)}, f32[2,3,4,256]{3,2,1,0:T(4,128)S(1)}, u32[]{:S(2)}, u32[]{:S(2)}) collective-permute-start(f32[2,3,4,256]{3,2,1,0:T(4,128)S(1)} %convert_element_type.17), channel_id=1, source_target_pairs={{16,25},{32,41},{48,57},{80,89},{96,105},{112,121},{144,153},{160,... | collective-permute-start | bytes 73736 | tf_op jit(solution)/shard_map/ppermute | solution.py:371
  2.0 9.5 %collective-permute-start.1 = (f32[2,3,4,256]{3,2,1,0:T(4,128)S(1)}, f32[2,3,4,256]{3,2,1,0:T(4,128)S(1)}, u32[]{:S(2)}, u32[]{:S(2)}) collective-permute-start(f32[2,3,4,256]{3,2,1,0:T(4,128)S(1)} %convert_element_type.17), channel_id=1, source_target_pairs={{15,25},{31,41},{47,57},{79,89},{95,105},{111,121},{143,153},{159,... | collective-permute-start | bytes 73736 | tf_op jit(solution)/shard_map/ppermute | solution.py:372
  2.7 8.8 %collective-permute-start.2 = (bf16[2,3,4,256]{3,2,1,0:T(4,128)(2,1)S(1)}, bf16[2,3,4,256]{3,2,1,0:T(4,128)(2,1)S(1)}, u32[]{:S(2)}, u32[]{:S(2)}) collective-permute-start(bf16[2,3,4,256]{3,2,1,0:T(4,128)(2,1)S(1)} %constant_dynamic-update-slice_fusion.image_ref), channel_id=1, source_target_pairs={{0,1},{1,2},{2,3},{3,4},{4,5},{5,6},{6,7},{7,8},{8,9},{9,10},{10,1... | collective-permute-start | bytes 36872 | tf_op jit(solution)/shard_map/ppermute | solution.py:375
  7.7 0.7 %copy-start = (bf16[64,3,4,4]{0,3,2,1:T(4,128)(2,1)S(1)}, bf16[64,3,4,4]{0,3,2,1:T(4,128)(2,1)}, u32[]{:S(2)}) copy-start(bf16[64,3,4,4]{0,3,2,1:T(4,128)(2,1)} %param.12) | copy-start | bytes 18436
  7.7 0.7 %copy-start.1 = (f32[64]{0:T(128)S(1)}, f32[64]{0:T(128)}, u32[]{:S(2)}) copy-start(f32[64]{0:T(128)} %param.13) | copy-start | bytes 772
  13.4 13.8 %copy-start.3 = (bf16[64,3,3,3]{0,3,2,1:T(4,128)(2,1)S(1)}, bf16[64,3,3,3]{0,3,2,1:T(4,128)(2,1)}, u32[]{:S(2)}) copy-start(bf16[64,3,3,3]{0,3,2,1:T(4,128)(2,1)} %param.9) | copy-start | bytes 10372
  13.4 15.2 %all-to-all-start = ((f16[32,2,1664]{2,1,0:T(2,128)(2,1)}), f16[32,2,1664]{2,1,0:T(2,128)(2,1)S(1)}, u32[]{:S(2)}, u32[]{:S(2)}) async-start(f16[32,2,1664]{2,1,0:T(2,128)(2,1)} %broadcast_in_dim.26), calls=%async_computation | async-start | bytes 425984 | tf_op jit(solution)/shard_map/all_to_all | solution.py:362
  24.9 17.6 %collective-permute-start.3 = (f32[2,3,4,256]{3,2,1,0:T(4,128)S(1)}, f32[2,3,4,256]{3,2,1,0:T(4,128)S(1)}, u32[]{:S(2)}, u32[]{:S(2)}) collective-permute-start(f32[2,3,4,256]{3,2,1,0:T(4,128)S(1)} %convert_element_type.17), channel_id=1, source_target_pairs={{1,0},{2,1},{3,2},{4,3},{5,4},{6,5},{7,6},{8,7},{9,8},{10,9},{11,1... | collective-permute-start | bytes 73736 | tf_op jit(solution)/shard_map/ppermute | solution.py:376
  27.2 15.3 %collective-permute-start.4 = (f32[2,3,4,256]{3,2,1,0:T(4,128)S(1)}, f32[2,3,4,256]{3,2,1,0:T(4,128)S(1)}, u32[]{:S(2)}, u32[]{:S(2)}) collective-permute-start(f32[2,3,4,256]{3,2,1,0:T(4,128)S(1)} %collective-permute-done.1.upper_ref), channel_id=1, source_target_pairs={{25,16},{41,32},{57,48},{89,80},{105,96},{121,112},{153,144},{169,... | collective-permute-start | bytes 73736 | tf_op jit(solution)/shard_map/ppermute | solution.py:377
  28.6 13.9 %copy-start.2 = (bf16[64,64,3,3]{1,0,3,2:T(8,128)(2,1)S(1)}, bf16[64,64,3,3]{1,0,3,2:T(8,128)(2,1)}, u32[]{:S(2)}) copy-start(bf16[64,64,3,3]{1,0,3,2:T(8,128)(2,1)} %param.10) | copy-start | bytes 221188
  29.3 19.8 %all-to-all-start.1 = ((f16[16,2,1664]{2,1,0:T(2,128)(2,1)}), f16[16,2,1664]{2,1,0:T(2,128)(2,1)S(1)}, u32[]{:S(2)}, u32[]{:S(2)}) async-start(f16[16,2,1664]{2,1,0:T(2,128)(2,1)} %broadcast_in_dim.29), calls=%async_computation.1 | async-start | bytes 212992 | tf_op jit(solution)/shard_map/all_to_all | solution.py:362
  43.0 0.7 %copy-start.5 = (f32[64]{0:T(128)S(1)}, f32[64]{0:T(128)}, u32[]{:S(2)}) copy-start(f32[64]{0:T(128)} %param.11) | copy-start | bytes 772
  43.0 0.8 %collective-permute-start.5 = (bf16[2,3,4,256]{3,2,1,0:T(4,128)(2,1)S(1)}, bf16[2,3,4,256]{3,2,1,0:T(4,128)(2,1)S(1)}, u32[]{:S(2)}, u32[]{:S(2)}) collective-permute-start(bf16[2,3,4,256]{3,2,1,0:T(4,128)(2,1)S(1)} %get-tuple-element.29), channel_id=1, source_target_pairs={{271,272},{287,288},{303,304},{25,15},{41,31},{57,47},{281,271},{2... | collective-permute-start | bytes 36872 | tf_op jit(solution)/shard_map/ppermute | solution.py:387

commit v7 on v6

--- a/solution.py
+++ b/solution.py
@@ -16,7 +16,7 @@
 COLUMN = ("zh", "zl")
 MIDDLE = 9
 PLANE_ORDER = [21, 0, 1, 2, 3, 6, 7, 8, 9, 24, 25, 4, 5, 10, 11, 14, 15, 16, 17, 26, 27, 30, 31, 12, 13, 18, 19, 22, 23, 28, 29, 20]
-COLUMN_ORDER = [10, 0, 1, 2, 3, 15, 4, 14, 5, 13, 6, 12, 7, 11, 8, 9]
+COLUMN_ORDER = [10, 8, 7, 6, 9, 5, 4, 3, 2, 11, 12, 13, 14, 1, 15, 0]
 F32 = jnp.float32
 BF16 = jnp.bfloat16
 VMEM = pl.BlockSpec(memory_space=pltpu.VMEM)

time: 50.7 us -> 50.8 us (level)
  no operation moved by 1% of the time
where the time goes in v7:
time: 50.8 us; the launch traced here: 50.3 us
  starting transfers between devices  34.6 us (68%)
  waiting for transfers between devices  6 us (12%)
  Pallas kernels  5.66 us (11%)
  local copies, waits for them, and re-layouts  3.03 us (6%)
  between operations  0.82 us (2%)
    all_to_all x2, starting transfers between devices, exchange_sum(): lax.all_to_all(copies, axes, 0, 0, axis_index_groups=groups).astype(F32)  24.8 us
    ppermute x1, starting transfers between devices, shards(): lax.ppermute(images, ROWS, [(k, k + 1) for k in range(count - 1) if k % 1...  4.94 us
    pallas_call x1, Pallas kernels, features(): pl.pallas_call(feature_kernel, out_shape=jax.ShapeDtypeStruct((3, 4, 256)...  3.28 us
    all_to_all x2, waiting for transfers between devices, exchange_sum(): lax.all_to_all(copies, axes, 0, 0, axis_index_groups=groups).astype(F32)  3.1 us
    ppermute x1, waiting for transfers between devices, shards(): lax.ppermute(images, ROWS, [(k, k + 1) for k in range(count - 1) if k % 1...  2.89 us
    ppermute x1, starting transfers between devices, shards(): lax.ppermute(whole, ROWS, [(k + 1, k) for k in range(count - 1) if k % 16...  2.27 us
    broadcast_in_dim x2, local copies, waits for them, and re-layouts, exchange_sum(): copies = jnp.broadcast_to(value[None], (peers,) + value.shape)  1.5 us
    unnamed x13, local copies, waits for them, and re-layouts  1.41 us
  transfers between devices with their start and end apart: 8, of which 3 were waited for; matrix products, arithmetic and copies ran while one was open for 2% of the time, Pallas kernels for 8%

profile of v7, /device:TPU:1, one launch (start us, length us, event | category | flops | bytes accessed | tf_op | source)
XLA Modules:
  0.0 50.3 jit_solution(13049483084497423393)
XLA Ops:
  0.6 0.7 %constant_dynamic-update-slice_fusion.1 = bf16[2,3,4,256]{3,2,1,0:T(4,128)(2,1)S(1)} fusion(bf16[1,3,4,256]{3,2,1,0:T(4,128)(2,1)} %param.7), kind=kLoop, calls=%fused_computation.4 | loop fusion | bytes 12288
  1.4 0.7 %collective-permute-start = (f32[2,3,4,256]{3,2,1,0:T(4,128)S(1)}, f32[2,3,4,256]{3,2,1,0:T(4,128)S(1)}, u32[]{:S(2)}, u32[]{:S(2)}) collective-permute-start(f32[2,3,4,256]{3,2,1,0:T(4,128)S(1)} %convert_element_type.17), channel_id=1, source_target_pairs={{16,25},{32,41},{48,57},{80,89},{96,105},{112,121},{144,153},{160,... | collective-permute-start | bytes 73736 | tf_op jit(solution)/shard_map/ppermute | solution.py:371
  2.0 0.7 %collective-permute-start.1 = (f32[2,3,4,256]{3,2,1,0:T(4,128)S(1)}, f32[2,3,4,256]{3,2,1,0:T(4,128)S(1)}, u32[]{:S(2)}, u32[]{:S(2)}) collective-permute-start(f32[2,3,4,256]{3,2,1,0:T(4,128)S(1)} %convert_element_type.17), channel_id=1, source_target_pairs={{15,25},{31,41},{47,57},{79,89},{95,105},{111,121},{143,153},{159,... | collective-permute-start | bytes 73736 | tf_op jit(solution)/shard_map/ppermute | solution.py:372
  2.7 4.9 %collective-permute-start.2 = (bf16[2,3,4,256]{3,2,1,0:T(4,128)(2,1)S(1)}, bf16[2,3,4,256]{3,2,1,0:T(4,128)(2,1)S(1)}, u32[]{:S(2)}, u32[]{:S(2)}) collective-permute-start(bf16[2,3,4,256]{3,2,1,0:T(4,128)(2,1)S(1)} %constant_dynamic-update-slice_fusion.image_ref), channel_id=1, source_target_pairs={{0,1},{1,2},{2,3},{3,4},{4,5},{5,6},{6,7},{7,8},{8,9},{9,10},{10,1... | collective-permute-start | bytes 36872 | tf_op jit(solution)/shard_map/ppermute | solution.py:375
  7.7 0.0 copy-start
  7.7 0.7 %copy-done = bf16[64,3,4,4]{0,3,2,1:T(4,128)(2,1)S(1)} copy-done((bf16[64,3,4,4]{0,3,2,1:T(4,128)(2,1)S(1)}, bf16[64,3,4,4]{0,3,2,1:T(4,128)(2,1)}, u32[]{:S(2)}) %copy-start) | copy-done | bytes 6168
  8.4 0.3 critic_weights.1
  8.6 2.9 %collective-permute-done.2.previous_ref = bf16[2,3,4,256]{3,2,1,0:T(4,128)(2,1)S(1)} collective-permute-done((bf16[2,3,4,256]{3,2,1,0:T(4,128)(2,1)S(1)}, bf16[2,3,4,256]{3,2,1,0:T(4,128)(2,1)S(1)}, u32[]{:S(2)}, u32[]{:S(2)}) %collective-permute-start.2) | collective-permute-done | bytes 12320 | tf_op jit(solution)/shard_map/ppermute | solution.py:375
  11.5 1.0 %critic.1 = f32[2,1664]{1,0:T(2,128)S(1)} custom-call(s32[1]{0:T(128)} %bitcast.row_ref, f32[2,3,4,256]{3,2,1,0:T(4,128)S(1)} %collective-permute-done.under_ref, f32[2,3,4,256]{3,2,1,0:T(4,128)S(1)} %collective-permute-done.1.upper_ref, bf16[2,3,4,256]{3,2,1,0:T(4,128)(2,1)S(1)} %collective-permute-done.2.previous_ref, ...), custom_call_target="tpu_custom_call" | custom-call | tf_op jit(solution)/shard_map/critic/pallas_call | solution.py:190
  12.5 0.8 %broadcast_in_dim.26 = f16[32,2,1664]{2,1,0:T(2,128)(2,1)} broadcast(f16[2,1664]{1,0:T(2,128)(2,1)S(1)} %convert_element_type.18), dimensions={1,2} | broadcast | bytes 219648 | tf_op jit(solution)/shard_map/broadcast_in_dim | solution.py:360
  13.4 11.6 %all-to-all-start = ((f16[32,2,1664]{2,1,0:T(2,128)(2,1)}), f16[32,2,1664]{2,1,0:T(2,128)(2,1)S(1)}, u32[]{:S(2)}, u32[]{:S(2)}) async-start(f16[32,2,1664]{2,1,0:T(2,128)(2,1)} %broadcast_in_dim.26), calls=%async_computation | async-start | bytes 425984 | tf_op jit(solution)/shard_map/all_to_all | solution.py:362
  24.9 2.3 %collective-permute-start.3 = (f32[2,3,4,256]{3,2,1,0:T(4,128)S(1)}, f32[2,3,4,256]{3,2,1,0:T(4,128)S(1)}, u32[]{:S(2)}, u32[]{:S(2)}) collective-permute-start(f32[2,3,4,256]{3,2,1,0:T(4,128)S(1)} %convert_element_type.17), channel_id=1, source_target_pairs={{1,0},{2,1},{3,2},{4,3},{5,4},{6,5},{7,6},{8,7},{9,8},{10,9},{11,1... | collective-permute-start | bytes 73736 | tf_op jit(solution)/shard_map/ppermute | solution.py:376
  27.2 0.7 %collective-permute-start.4 = (f32[2,3,4,256]{3,2,1,0:T(4,128)S(1)}, f32[2,3,4,256]{3,2,1,0:T(4,128)S(1)}, u32[]{:S(2)}, u32[]{:S(2)}) collective-permute-start(f32[2,3,4,256]{3,2,1,0:T(4,128)S(1)} %collective-permute-done.1.upper_ref), channel_id=1, source_target_pairs={{25,16},{41,32},{57,48},{89,80},{105,96},{121,112},{153,144},{169,... | collective-permute-start | bytes 73736 | tf_op jit(solution)/shard_map/ppermute | solution.py:377
  27.9 0.6 %all-to-all-done = f16[32,2,1664]{2,1,0:T(2,128)(2,1)S(1)} async-done(((f16[32,2,1664]{2,1,0:T(2,128)(2,1)}), f16[32,2,1664]{2,1,0:T(2,128)(2,1)S(1)}, u32[]{:S(2)}, u32[]{:S(2)}) %all-to-all-start) | async-done | bytes 213024 | tf_op jit(solution)/shard_map/all_to_all | solution.py:362
  28.5 0.1 convert_reduce_fusion
  28.7 0.7 %broadcast_in_dim.29 = f16[16,2,1664]{2,1,0:T(2,128)(2,1)} broadcast(f16[2,1664]{1,0:T(2,128)(2,1)S(1)} %multiply_convert_fusion), dimensions={1,2} | broadcast | bytes 113152 | tf_op jit(solution)/shard_map/broadcast_in_dim | solution.py:360
  29.3 13.2 %all-to-all-start.1 = ((f16[16,2,1664]{2,1,0:T(2,128)(2,1)}), f16[16,2,1664]{2,1,0:T(2,128)(2,1)S(1)}, u32[]{:S(2)}, u32[]{:S(2)}) async-start(f16[16,2,1664]{2,1,0:T(2,128)(2,1)} %broadcast_in_dim.29), calls=%async_computation.1 | async-start | bytes 212992 | tf_op jit(solution)/shard_map/all_to_all | solution.py:362
  42.6 0.4 feature_weights.1
  43.0 0.7 %collective-permute-start.5 = (bf16[2,3,4,256]{3,2,1,0:T(4,128)(2,1)S(1)}, bf16[2,3,4,256]{3,2,1,0:T(4,128)(2,1)S(1)}, u32[]{:S(2)}, u32[]{:S(2)}) collective-permute-start(bf16[2,3,4,256]{3,2,1,0:T(4,128)(2,1)S(1)} %get-tuple-element.29), channel_id=1, source_target_pairs={{271,272},{287,288},{303,304},{25,15},{41,31},{57,47},{281,271},{2... | collective-permute-start | bytes 36872 | tf_op jit(solution)/shard_map/ppermute | solution.py:387
  43.7 0.1 copy.16.lpips_ref
  43.8 3.3 %features.1 = f32[3,4,256]{2,1,0:T(4,128)} custom-call(s32[1]{0:T(128)} %bitcast.row_ref, bf16[64,256]{1,0:T(8,128)(2,1)S(1)} %get-tuple-element.24.critic_bwd_ref, bf16[640,144]{1,0:T(8,128)(2,1)S(1)} %get-tuple-element.25.first_fwd_ref, bf16[48,384]{1,0:T(8,128)(2,1)S(1)} %get-tuple-element.26.first_bwd_ref, ...), custom_call_target="tpu_custom_call" | custom-call | flops 1000000000 | bytes 1000000 | tf_op jit(solution)/shard_map/features/pallas_call | solution.py:313
  47.1 2.5 %all-to-all-done.1 = f16[16,2,1664]{2,1,0:T(2,128)(2,1)S(1)} async-done(((f16[16,2,1664]{2,1,0:T(2,128)(2,1)}), f16[16,2,1664]{2,1,0:T(2,128)(2,1)S(1)}, u32[]{:S(2)}, u32[]{:S(2)}) %all-to-all-start.1) | async-done | bytes 106528 | tf_op jit(solution)/shard_map/all_to_all | solution.py:362
  49.5 0.1 convert_reduce_fusion.1.total_ref
  49.6 0.7 %finish.1 = (f32[3,4,4,64]{3,2,1,0:T(4,128)}, f32[1,64]{1,0:T(1,128)}) custom-call(f32[2,1664]{1,0:T(2,128)S(1)} %convert_reduce_fusion.1.total_ref), custom_call_target="tpu_custom_call" | custom-call | tf_op jit(solution)/shard_map/finish/pallas_call | solution.py:342
  (20 shorter events, 0.1 us)
Async XLA Ops:
  0.6 0.7 %copy-start.4 = (bf16[1,3,4,256]{3,2,1,0:T(4,128)(2,1)S(1)}, bf16[1,3,4,256]{3,2,1,0:T(4,128)(2,1)}, u32[]{:S(2)}) copy-start(bf16[1,3,4,256]{3,2,1,0:T(4,128)(2,1)} %param.8) | copy-start | bytes 18436
  1.4 10.2 %collective-permute-start = (f32[2,3,4,256]{3,2,1,0:T(4,128)S(1)}, f32[2,3,4,256]{3,2,1,0:T(4,128)S(1)}, u32[]{:S(2)}, u32[]{:S(2)}) collective-permute-start(f32[2,3,4,256]{3,2,1,0:T(4,128)S(1)} %convert_element_type.17), channel_id=1, source_target_pairs={{16,25},{32,41},{48,57},{80,89},{96,105},{112,121},{144,153},{160,... | collective-permute-start | bytes 73736 | tf_op jit(solution)/shard_map/ppermute | solution.py:371
  2.0 9.5 %collective-permute-start.1 = (f32[2,3,4,256]{3,2,1,0:T(4,128)S(1)}, f32[2,3,4,256]{3,2,1,0:T(4,128)S(1)}, u32[]{:S(2)}, u32[]{:S(2)}) collective-permute-start(f32[2,3,4,256]{3,2,1,0:T(4,128)S(1)} %convert_element_type.17), channel_id=1, source_target_pairs={{15,25},{31,41},{47,57},{79,89},{95,105},{111,121},{143,153},{159,... | collective-permute-start | bytes 73736 | tf_op jit(solution)/shard_map/ppermute | solution.py:372
  2.7 8.8 %collective-permute-start.2 = (bf16[2,3,4,256]{3,2,1,0:T(4,128)(2,1)S(1)}, bf16[2,3,4,256]{3,2,1,0:T(4,128)(2,1)S(1)}, u32[]{:S(2)}, u32[]{:S(2)}) collective-permute-start(bf16[2,3,4,256]{3,2,1,0:T(4,128)(2,1)S(1)} %constant_dynamic-update-slice_fusion.image_ref), channel_id=1, source_target_pairs={{0,1},{1,2},{2,3},{3,4},{4,5},{5,6},{6,7},{7,8},{8,9},{9,10},{10,1... | collective-permute-start | bytes 36872 | tf_op jit(solution)/shard_map/ppermute | solution.py:375
  7.7 0.7 %copy-start = (bf16[64,3,4,4]{0,3,2,1:T(4,128)(2,1)S(1)}, bf16[64,3,4,4]{0,3,2,1:T(4,128)(2,1)}, u32[]{:S(2)}) copy-start(bf16[64,3,4,4]{0,3,2,1:T(4,128)(2,1)} %param.12) | copy-start | bytes 18436
  7.7 0.7 %copy-start.1 = (f32[64]{0:T(128)S(1)}, f32[64]{0:T(128)}, u32[]{:S(2)}) copy-start(f32[64]{0:T(128)} %param.13) | copy-start | bytes 772
  13.4 13.8 %copy-start.3 = (bf16[64,3,3,3]{0,3,2,1:T(4,128)(2,1)S(1)}, bf16[64,3,3,3]{0,3,2,1:T(4,128)(2,1)}, u32[]{:S(2)}) copy-start(bf16[64,3,3,3]{0,3,2,1:T(4,128)(2,1)} %param.9) | copy-start | bytes 10372
  13.4 15.2 %all-to-all-start = ((f16[32,2,1664]{2,1,0:T(2,128)(2,1)}), f16[32,2,1664]{2,1,0:T(2,128)(2,1)S(1)}, u32[]{:S(2)}, u32[]{:S(2)}) async-start(f16[32,2,1664]{2,1,0:T(2,128)(2,1)} %broadcast_in_dim.26), calls=%async_computation | async-start | bytes 425984 | tf_op jit(solution)/shard_map/all_to_all | solution.py:362
  24.9 17.6 %collective-permute-start.3 = (f32[2,3,4,256]{3,2,1,0:T(4,128)S(1)}, f32[2,3,4,256]{3,2,1,0:T(4,128)S(1)}, u32[]{:S(2)}, u32[]{:S(2)}) collective-permute-start(f32[2,3,4,256]{3,2,1,0:T(4,128)S(1)} %convert_element_type.17), channel_id=1, source_target_pairs={{1,0},{2,1},{3,2},{4,3},{5,4},{6,5},{7,6},{8,7},{9,8},{10,9},{11,1... | collective-permute-start | bytes 73736 | tf_op jit(solution)/shard_map/ppermute | solution.py:376
  27.2 15.3 %collective-permute-start.4 = (f32[2,3,4,256]{3,2,1,0:T(4,128)S(1)}, f32[2,3,4,256]{3,2,1,0:T(4,128)S(1)}, u32[]{:S(2)}, u32[]{:S(2)}) collective-permute-start(f32[2,3,4,256]{3,2,1,0:T(4,128)S(1)} %collective-permute-done.1.upper_ref), channel_id=1, source_target_pairs={{25,16},{41,32},{57,48},{89,80},{105,96},{121,112},{153,144},{169,... | collective-permute-start | bytes 73736 | tf_op jit(solution)/shard_map/ppermute | solution.py:377
  28.6 13.9 %copy-start.2 = (bf16[64,64,3,3]{1,0,3,2:T(8,128)(2,1)S(1)}, bf16[64,64,3,3]{1,0,3,2:T(8,128)(2,1)}, u32[]{:S(2)}) copy-start(bf16[64,64,3,3]{1,0,3,2:T(8,128)(2,1)} %param.10) | copy-start | bytes 221188
  29.3 20.2 %all-to-all-start.1 = ((f16[16,2,1664]{2,1,0:T(2,128)(2,1)}), f16[16,2,1664]{2,1,0:T(2,128)(2,1)S(1)}, u32[]{:S(2)}, u32[]{:S(2)}) async-start(f16[16,2,1664]{2,1,0:T(2,128)(2,1)} %broadcast_in_dim.29), calls=%async_computation.1 | async-start | bytes 212992 | tf_op jit(solution)/shard_map/all_to_all | solution.py:362
  43.0 0.7 %copy-start.5 = (f32[64]{0:T(128)S(1)}, f32[64]{0:T(128)}, u32[]{:S(2)}) copy-start(f32[64]{0:T(128)} %param.11) | copy-start | bytes 772
  43.0 0.8 %collective-permute-start.5 = (bf16[2,3,4,256]{3,2,1,0:T(4,128)(2,1)S(1)}, bf16[2,3,4,256]{3,2,1,0:T(4,128)(2,1)S(1)}, u32[]{:S(2)}, u32[]{:S(2)}) collective-permute-start(bf16[2,3,4,256]{3,2,1,0:T(4,128)(2,1)S(1)} %get-tuple-element.29), channel_id=1, source_target_pairs={{271,272},{287,288},{303,304},{25,15},{41,31},{57,47},{281,271},{2... | collective-permute-start | bytes 36872 | tf_op jit(solution)/shard_map/ppermute | solution.py:387

commit v8 on v7

--- a/solution.py
+++ b/solution.py
@@ -16,7 +16,7 @@
 COLUMN = ("zh", "zl")
 MIDDLE = 9
 PLANE_ORDER = [21, 0, 1, 2, 3, 6, 7, 8, 9, 24, 25, 4, 5, 10, 11, 14, 15, 16, 17, 26, 27, 30, 31, 12, 13, 18, 19, 22, 23, 28, 29, 20]
-COLUMN_ORDER = [10, 8, 7, 6, 9, 5, 4, 3, 2, 11, 12, 13, 14, 1, 15, 0]
+COLUMN_ORDER = [11, 0, 1, 2, 3, 15, 4, 14, 5, 13, 6, 12, 7, 10, 8, 9]
 F32 = jnp.float32
 BF16 = jnp.bfloat16
 VMEM = pl.BlockSpec(memory_space=pltpu.VMEM)

time: 50.8 us -> 50.5 us (level)
  starting transfers between devices: 34.6 us -> 33.7 us
    all_to_all x2, starting transfers between devices: 24.8 us -> 23.8 us  [exchange_sum(): lax.all_to_all(copies, axes, 0, 0, axis_index_groups=groups).astype(F32)]
where the time goes in v8:
time: 50.5 us; the launch traced here: 49.8 us
  starting transfers between devices  33.7 us (67%)
  waiting for transfers between devices  6.44 us (13%)
  Pallas kernels  5.67 us (11%)
  local copies, waits for them, and re-layouts  3.03 us (6%)
  between operations  0.82 us (2%)
    all_to_all x2, starting transfers between devices, exchange_sum(): lax.all_to_all(copies, axes, 0, 0, axis_index_groups=groups).astype(F32)  23.8 us
    ppermute x1, starting transfers between devices, shards(): lax.ppermute(images, ROWS, [(k, k + 1) for k in range(count - 1) if k % 1...  4.94 us
    all_to_all x2, waiting for transfers between devices, exchange_sum(): lax.all_to_all(copies, axes, 0, 0, axis_index_groups=groups).astype(F32)  3.54 us
    pallas_call x1, Pallas kernels, features(): pl.pallas_call(feature_kernel, out_shape=jax.ShapeDtypeStruct((3, 4, 256)...  3.28 us
    ppermute x1, waiting for transfers between devices, shards(): lax.ppermute(images, ROWS, [(k, k + 1) for k in range(count - 1) if k % 1...  2.89 us
    ppermute x1, starting transfers between devices, shards(): lax.ppermute(whole, ROWS, [(k + 1, k) for k in range(count - 1) if k % 16...  2.27 us
    broadcast_in_dim x2, local copies, waits for them, and re-layouts, exchange_sum(): copies = jnp.broadcast_to(value[None], (peers,) + value.shape)  1.5 us
    unnamed x13, local copies, waits for them, and re-layouts  1.41 us
  transfers between devices with their start and end apart: 8, of which 3 were waited for; matrix products, arithmetic and copies ran while one was open for 2% of the time, Pallas kernels for 8%

profile of v8, /device:TPU:1, one launch (start us, length us, event | category | flops | bytes accessed | tf_op | source)
XLA Modules:
  0.0 49.8 jit_solution(2456306442406643700)
XLA Ops:
  0.6 0.7 %constant_dynamic-update-slice_fusion.1 = bf16[2,3,4,256]{3,2,1,0:T(4,128)(2,1)S(1)} fusion(bf16[1,3,4,256]{3,2,1,0:T(4,128)(2,1)} %param.7), kind=kLoop, calls=%fused_computation.4 | loop fusion | bytes 12288
  1.4 0.7 %collective-permute-start = (f32[2,3,4,256]{3,2,1,0:T(4,128)S(1)}, f32[2,3,4,256]{3,2,1,0:T(4,128)S(1)}, u32[]{:S(2)}, u32[]{:S(2)}) collective-permute-start(f32[2,3,4,256]{3,2,1,0:T(4,128)S(1)} %convert_element_type.17), channel_id=1, source_target_pairs={{16,25},{32,41},{48,57},{80,89},{96,105},{112,121},{144,153},{160,... | collective-permute-start | bytes 73736 | tf_op jit(solution)/shard_map/ppermute | solution.py:371
  2.0 0.7 %collective-permute-start.1 = (f32[2,3,4,256]{3,2,1,0:T(4,128)S(1)}, f32[2,3,4,256]{3,2,1,0:T(4,128)S(1)}, u32[]{:S(2)}, u32[]{:S(2)}) collective-permute-start(f32[2,3,4,256]{3,2,1,0:T(4,128)S(1)} %convert_element_type.17), channel_id=1, source_target_pairs={{15,25},{31,41},{47,57},{79,89},{95,105},{111,121},{143,153},{159,... | collective-permute-start | bytes 73736 | tf_op jit(solution)/shard_map/ppermute | solution.py:372
  2.7 4.9 %collective-permute-start.2 = (bf16[2,3,4,256]{3,2,1,0:T(4,128)(2,1)S(1)}, bf16[2,3,4,256]{3,2,1,0:T(4,128)(2,1)S(1)}, u32[]{:S(2)}, u32[]{:S(2)}) collective-permute-start(bf16[2,3,4,256]{3,2,1,0:T(4,128)(2,1)S(1)} %constant_dynamic-update-slice_fusion.image_ref), channel_id=1, source_target_pairs={{0,1},{1,2},{2,3},{3,4},{4,5},{5,6},{6,7},{7,8},{8,9},{9,10},{10,1... | collective-permute-start | bytes 36872 | tf_op jit(solution)/shard_map/ppermute | solution.py:375
  7.7 0.0 copy-start
  7.7 0.7 %copy-done = bf16[64,3,4,4]{0,3,2,1:T(4,128)(2,1)S(1)} copy-done((bf16[64,3,4,4]{0,3,2,1:T(4,128)(2,1)S(1)}, bf16[64,3,4,4]{0,3,2,1:T(4,128)(2,1)}, u32[]{:S(2)}) %copy-start) | copy-done | bytes 6168
  8.4 0.3 critic_weights.1
  8.6 2.9 %collective-permute-done.2.previous_ref = bf16[2,3,4,256]{3,2,1,0:T(4,128)(2,1)S(1)} collective-permute-done((bf16[2,3,4,256]{3,2,1,0:T(4,128)(2,1)S(1)}, bf16[2,3,4,256]{3,2,1,0:T(4,128)(2,1)S(1)}, u32[]{:S(2)}, u32[]{:S(2)}) %collective-permute-start.2) | collective-permute-done | bytes 12320 | tf_op jit(solution)/shard_map/ppermute | solution.py:375
  11.5 1.0 %critic.1 = f32[2,1664]{1,0:T(2,128)S(1)} custom-call(s32[1]{0:T(128)} %bitcast.row_ref, f32[2,3,4,256]{3,2,1,0:T(4,128)S(1)} %collective-permute-done.under_ref, f32[2,3,4,256]{3,2,1,0:T(4,128)S(1)} %collective-permute-done.1.upper_ref, bf16[2,3,4,256]{3,2,1,0:T(4,128)(2,1)S(1)} %collective-permute-done.2.previous_ref, ...), custom_call_target="tpu_custom_call" | custom-call | tf_op jit(solution)/shard_map/critic/pallas_call | solution.py:190
  12.5 0.8 %broadcast_in_dim.26 = f16[32,2,1664]{2,1,0:T(2,128)(2,1)} broadcast(f16[2,1664]{1,0:T(2,128)(2,1)S(1)} %convert_element_type.18), dimensions={1,2} | broadcast | bytes 219648 | tf_op jit(solution)/shard_map/broadcast_in_dim | solution.py:360
  13.4 11.6 %all-to-all-start = ((f16[32,2,1664]{2,1,0:T(2,128)(2,1)}), f16[32,2,1664]{2,1,0:T(2,128)(2,1)S(1)}, u32[]{:S(2)}, u32[]{:S(2)}) async-start(f16[32,2,1664]{2,1,0:T(2,128)(2,1)} %broadcast_in_dim.26), calls=%async_computation | async-start | bytes 425984 | tf_op jit(solution)/shard_map/all_to_all | solution.py:362
  24.9 2.3 %collective-permute-start.3 = (f32[2,3,4,256]{3,2,1,0:T(4,128)S(1)}, f32[2,3,4,256]{3,2,1,0:T(4,128)S(1)}, u32[]{:S(2)}, u32[]{:S(2)}) collective-permute-start(f32[2,3,4,256]{3,2,1,0:T(4,128)S(1)} %convert_element_type.17), channel_id=1, source_target_pairs={{1,0},{2,1},{3,2},{4,3},{5,4},{6,5},{7,6},{8,7},{9,8},{10,9},{11,1... | collective-permute-start | bytes 73736 | tf_op jit(solution)/shard_map/ppermute | solution.py:376
  27.2 0.7 %collective-permute-start.4 = (f32[2,3,4,256]{3,2,1,0:T(4,128)S(1)}, f32[2,3,4,256]{3,2,1,0:T(4,128)S(1)}, u32[]{:S(2)}, u32[]{:S(2)}) collective-permute-start(f32[2,3,4,256]{3,2,1,0:T(4,128)S(1)} %collective-permute-done.1.upper_ref), channel_id=1, source_target_pairs={{25,16},{41,32},{57,48},{89,80},{105,96},{121,112},{153,144},{169,... | collective-permute-start | bytes 73736 | tf_op jit(solution)/shard_map/ppermute | solution.py:377
  27.9 0.6 %all-to-all-done = f16[32,2,1664]{2,1,0:T(2,128)(2,1)S(1)} async-done(((f16[32,2,1664]{2,1,0:T(2,128)(2,1)}), f16[32,2,1664]{2,1,0:T(2,128)(2,1)S(1)}, u32[]{:S(2)}, u32[]{:S(2)}) %all-to-all-start) | async-done | bytes 213024 | tf_op jit(solution)/shard_map/all_to_all | solution.py:362
  28.5 0.1 convert_reduce_fusion
  28.7 0.7 %broadcast_in_dim.29 = f16[16,2,1664]{2,1,0:T(2,128)(2,1)} broadcast(f16[2,1664]{1,0:T(2,128)(2,1)S(1)} %multiply_convert_fusion), dimensions={1,2} | broadcast | bytes 113152 | tf_op jit(solution)/shard_map/broadcast_in_dim | solution.py:360
  29.3 12.3 %all-to-all-start.1 = ((f16[16,2,1664]{2,1,0:T(2,128)(2,1)}), f16[16,2,1664]{2,1,0:T(2,128)(2,1)S(1)}, u32[]{:S(2)}, u32[]{:S(2)}) async-start(f16[16,2,1664]{2,1,0:T(2,128)(2,1)} %broadcast_in_dim.29), calls=%async_computation.1 | async-start | bytes 212992 | tf_op jit(solution)/shard_map/all_to_all | solution.py:362
  41.7 0.4 feature_weights.1
  42.1 0.7 %collective-permute-start.5 = (bf16[2,3,4,256]{3,2,1,0:T(4,128)(2,1)S(1)}, bf16[2,3,4,256]{3,2,1,0:T(4,128)(2,1)S(1)}, u32[]{:S(2)}, u32[]{:S(2)}) collective-permute-start(bf16[2,3,4,256]{3,2,1,0:T(4,128)(2,1)S(1)} %get-tuple-element.29), channel_id=1, source_target_pairs={{271,272},{287,288},{303,304},{25,15},{41,31},{57,47},{281,271},{2... | collective-permute-start | bytes 36872 | tf_op jit(solution)/shard_map/ppermute | solution.py:387
  42.8 0.1 copy.16.lpips_ref
  42.9 3.3 %features.1 = f32[3,4,256]{2,1,0:T(4,128)} custom-call(s32[1]{0:T(128)} %bitcast.row_ref, bf16[64,256]{1,0:T(8,128)(2,1)S(1)} %get-tuple-element.24.critic_bwd_ref, bf16[640,144]{1,0:T(8,128)(2,1)S(1)} %get-tuple-element.25.first_fwd_ref, bf16[48,384]{1,0:T(8,128)(2,1)S(1)} %get-tuple-element.26.first_bwd_ref, ...), custom_call_target="tpu_custom_call" | custom-call | flops 1000000000 | bytes 1000000 | tf_op jit(solution)/shard_map/features/pallas_call | solution.py:313
  46.2 2.9 %all-to-all-done.1 = f16[16,2,1664]{2,1,0:T(2,128)(2,1)S(1)} async-done(((f16[16,2,1664]{2,1,0:T(2,128)(2,1)}), f16[16,2,1664]{2,1,0:T(2,128)(2,1)S(1)}, u32[]{:S(2)}, u32[]{:S(2)}) %all-to-all-start.1) | async-done | bytes 106528 | tf_op jit(solution)/shard_map/all_to_all | solution.py:362
  49.1 0.1 convert_reduce_fusion.1.total_ref
  49.1 0.7 %finish.1 = (f32[3,4,4,64]{3,2,1,0:T(4,128)}, f32[1,64]{1,0:T(1,128)}) custom-call(f32[2,1664]{1,0:T(2,128)S(1)} %convert_reduce_fusion.1.total_ref), custom_call_target="tpu_custom_call" | custom-call | tf_op jit(solution)/shard_map/finish/pallas_call | solution.py:342
  (20 shorter events, 0.1 us)
Async XLA Ops:
  0.6 0.7 %copy-start.4 = (bf16[1,3,4,256]{3,2,1,0:T(4,128)(2,1)S(1)}, bf16[1,3,4,256]{3,2,1,0:T(4,128)(2,1)}, u32[]{:S(2)}) copy-start(bf16[1,3,4,256]{3,2,1,0:T(4,128)(2,1)} %param.8) | copy-start | bytes 18436
  1.4 10.2 %collective-permute-start = (f32[2,3,4,256]{3,2,1,0:T(4,128)S(1)}, f32[2,3,4,256]{3,2,1,0:T(4,128)S(1)}, u32[]{:S(2)}, u32[]{:S(2)}) collective-permute-start(f32[2,3,4,256]{3,2,1,0:T(4,128)S(1)} %convert_element_type.17), channel_id=1, source_target_pairs={{16,25},{32,41},{48,57},{80,89},{96,105},{112,121},{144,153},{160,... | collective-permute-start | bytes 73736 | tf_op jit(solution)/shard_map/ppermute | solution.py:371
  2.0 9.5 %collective-permute-start.1 = (f32[2,3,4,256]{3,2,1,0:T(4,128)S(1)}, f32[2,3,4,256]{3,2,1,0:T(4,128)S(1)}, u32[]{:S(2)}, u32[]{:S(2)}) collective-permute-start(f32[2,3,4,256]{3,2,1,0:T(4,128)S(1)} %convert_element_type.17), channel_id=1, source_target_pairs={{15,25},{31,41},{47,57},{79,89},{95,105},{111,121},{143,153},{159,... | collective-permute-start | bytes 73736 | tf_op jit(solution)/shard_map/ppermute | solution.py:372
  2.7 8.8 %collective-permute-start.2 = (bf16[2,3,4,256]{3,2,1,0:T(4,128)(2,1)S(1)}, bf16[2,3,4,256]{3,2,1,0:T(4,128)(2,1)S(1)}, u32[]{:S(2)}, u32[]{:S(2)}) collective-permute-start(bf16[2,3,4,256]{3,2,1,0:T(4,128)(2,1)S(1)} %constant_dynamic-update-slice_fusion.image_ref), channel_id=1, source_target_pairs={{0,1},{1,2},{2,3},{3,4},{4,5},{5,6},{6,7},{7,8},{8,9},{9,10},{10,1... | collective-permute-start | bytes 36872 | tf_op jit(solution)/shard_map/ppermute | solution.py:375
  7.7 0.7 %copy-start = (bf16[64,3,4,4]{0,3,2,1:T(4,128)(2,1)S(1)}, bf16[64,3,4,4]{0,3,2,1:T(4,128)(2,1)}, u32[]{:S(2)}) copy-start(bf16[64,3,4,4]{0,3,2,1:T(4,128)(2,1)} %param.12) | copy-start | bytes 18436
  7.7 0.7 %copy-start.1 = (f32[64]{0:T(128)S(1)}, f32[64]{0:T(128)}, u32[]{:S(2)}) copy-start(f32[64]{0:T(128)} %param.13) | copy-start | bytes 772
  13.4 13.8 %copy-start.3 = (bf16[64,3,3,3]{0,3,2,1:T(4,128)(2,1)S(1)}, bf16[64,3,3,3]{0,3,2,1:T(4,128)(2,1)}, u32[]{:S(2)}) copy-start(bf16[64,3,3,3]{0,3,2,1:T(4,128)(2,1)} %param.9) | copy-start | bytes 10372
  13.4 15.2 %all-to-all-start = ((f16[32,2,1664]{2,1,0:T(2,128)(2,1)}), f16[32,2,1664]{2,1,0:T(2,128)(2,1)S(1)}, u32[]{:S(2)}, u32[]{:S(2)}) async-start(f16[32,2,1664]{2,1,0:T(2,128)(2,1)} %broadcast_in_dim.26), calls=%async_computation | async-start | bytes 425984 | tf_op jit(solution)/shard_map/all_to_all | solution.py:362
  24.9 16.7 %collective-permute-start.3 = (f32[2,3,4,256]{3,2,1,0:T(4,128)S(1)}, f32[2,3,4,256]{3,2,1,0:T(4,128)S(1)}, u32[]{:S(2)}, u32[]{:S(2)}) collective-permute-start(f32[2,3,4,256]{3,2,1,0:T(4,128)S(1)} %convert_element_type.17), channel_id=1, source_target_pairs={{1,0},{2,1},{3,2},{4,3},{5,4},{6,5},{7,6},{8,7},{9,8},{10,9},{11,1... | collective-permute-start | bytes 73736 | tf_op jit(solution)/shard_map/ppermute | solution.py:376
  27.2 14.4 %collective-permute-start.4 = (f32[2,3,4,256]{3,2,1,0:T(4,128)S(1)}, f32[2,3,4,256]{3,2,1,0:T(4,128)S(1)}, u32[]{:S(2)}, u32[]{:S(2)}) collective-permute-start(f32[2,3,4,256]{3,2,1,0:T(4,128)S(1)} %collective-permute-done.1.upper_ref), channel_id=1, source_target_pairs={{25,16},{41,32},{57,48},{89,80},{105,96},{121,112},{153,144},{169,... | collective-permute-start | bytes 73736 | tf_op jit(solution)/shard_map/ppermute | solution.py:377
  28.6 13.0 %copy-start.2 = (bf16[64,64,3,3]{1,0,3,2:T(8,128)(2,1)S(1)}, bf16[64,64,3,3]{1,0,3,2:T(8,128)(2,1)}, u32[]{:S(2)}) copy-start(bf16[64,64,3,3]{1,0,3,2:T(8,128)(2,1)} %param.10) | copy-start | bytes 221188
  29.3 19.7 %all-to-all-start.1 = ((f16[16,2,1664]{2,1,0:T(2,128)(2,1)}), f16[16,2,1664]{2,1,0:T(2,128)(2,1)S(1)}, u32[]{:S(2)}, u32[]{:S(2)}) async-start(f16[16,2,1664]{2,1,0:T(2,128)(2,1)} %broadcast_in_dim.29), calls=%async_computation.1 | async-start | bytes 212992 | tf_op jit(solution)/shard_map/all_to_all | solution.py:362
  42.1 0.7 %copy-start.5 = (f32[64]{0:T(128)S(1)}, f32[64]{0:T(128)}, u32[]{:S(2)}) copy-start(f32[64]{0:T(128)} %param.11) | copy-start | bytes 772
  42.1 0.8 %collective-permute-start.5 = (bf16[2,3,4,256]{3,2,1,0:T(4,128)(2,1)S(1)}, bf16[2,3,4,256]{3,2,1,0:T(4,128)(2,1)S(1)}, u32[]{:S(2)}, u32[]{:S(2)}) collective-permute-start(bf16[2,3,4,256]{3,2,1,0:T(4,128)(2,1)S(1)} %get-tuple-element.29), channel_id=1, source_target_pairs={{271,272},{287,288},{303,304},{25,15},{41,31},{57,47},{281,271},{2... | collective-permute-start | bytes 36872 | tf_op jit(solution)/shard_map/ppermute | solution.py:387
